TPU v7x, 32 devices: a whole 2x2x4 slice. The times are simulated.
32 devices in a mesh: fsdp: 4 (over y, core), cand: 8 (over z, x).
Axes of the slice: x: 2, y: 2, z: 4, core: 2. Of those that a mesh axis runs over, the one named last changes fastest.
Arguments:
- positions_init: float32 [256, 8192], P(('fsdp', 'cand')), may hold values from -6 to 6
- momenta_init: float32 [256, 8192], P(('fsdp', 'cand')), may hold values from -6 to 6
- kernel: bfloat16 [4096, 8192], P('fsdp'), may hold values from -0.0625 to 0.0625
- bias: bfloat16 [4096], P('fsdp'), may hold values from -4 to 4
- amplitude: bfloat16 [4096], P('fsdp'), may hold values from 0.3984375 to 2.5
- shift: float32 [8192], replicated, may hold values from -4 to 4
- omega: bfloat16 [8192, 8192], P('fsdp', 'cand'), may hold values from -0.0625 to 0.0625
- phase: float32 [8192], P('fsdp'), may hold values from -3.140625 to 3.140625
- samples: bfloat16 [8192, 128], P('fsdp'), may hold values from -6 to 6
Outputs:
- tracked: bfloat16 [256, 8192], P(('fsdp', 'cand'))
- final_positions: float32 [256, 8192], P(('fsdp', 'cand'))
- acquisition: float32 [256, 128], P(('fsdp', 'cand'))
All inputs are finite; a program needn't handle non-finite values.
Results may differ from a plain program's by a relative error of at most 0.0062.
Values may be sent and summed in bfloat16 or wider, within the bound.
No kernel may reach another device: no remote copies, remote signals or barrier semaphores. Data moves between devices by JAX's collectives and lax.ppermute only.
A program may use at most 192 MiB of HBM per device.

v0:
```python
import jax
import jax.numpy as jnp
from jax import lax
from jax.sharding import PartitionSpec as P

F = 8192


def local(positions_init, momenta_init, kernel, bias, amplitude, shift, omega, phase, samples):
    positions = positions_init
    momenta = momenta_init
    rounded = momenta.astype(jnp.bfloat16)
    rows_piece = lax.all_gather(kernel, "fsdp", axis=0, tiled=True)
    bias_piece = lax.all_gather(bias, "fsdp", axis=0, tiled=True)
    amp_piece = lax.all_gather(amplitude, "fsdp", axis=0, tiled=True)
    scores = lax.dot_general(
        rounded, rows_piece, (((1,), (1,)), ((), ())), preferred_element_type=jnp.float32
    )
    scores = scores + bias_piece.astype(jnp.float32)[None, :]
    activated = (amp_piece.astype(jnp.float32)[None, :] * jnp.tanh(scores)).astype(jnp.bfloat16)
    force = jnp.dot(activated, rows_piece, preferred_element_type=jnp.float32)
    positions, momenta = (momenta + shift[None, :], force - positions)
    tracked = momenta.astype(jnp.bfloat16)
    group_tracked = lax.all_gather(tracked, "fsdp", axis=0, tiled=True)
    angles = lax.dot_general(
        group_tracked,
        lax.all_gather(omega, "cand", axis=1, tiled=True),
        (((1,), (1,)), ((), ())),
        preferred_element_type=jnp.float32,
    )
    features = (jnp.sqrt(2.0 / F) * jnp.cos(angles + phase[None, :])).astype(jnp.bfloat16)
    acquisition = lax.psum_scatter(
        jnp.dot(features, samples, preferred_element_type=jnp.float32),
        "fsdp",
        scatter_dimension=0,
        tiled=True,
    )
    return (tracked, positions, acquisition)


def solution(mesh):
    return jax.shard_map(
        local,
        mesh=mesh,
        in_specs=(
            P(("fsdp", "cand"), None),
            P(("fsdp", "cand"), None),
            P("fsdp", None),
            P("fsdp"),
            P("fsdp"),
            P(),
            P("fsdp", "cand"),
            P("fsdp"),
            P("fsdp", None),
        ),
        out_specs=(P(("fsdp", "cand"), None), P(("fsdp", "cand"), None), P(("fsdp", "cand"), None)),
        check_vma=False,
    )
```

profile of v0, /device:TPU:0, one launch (start us, length us, event | category | flops | bytes accessed | tf_op | source)
XLA Modules:
  0.0 1078.7 jit_solution(12456488148666935146)
XLA Ops:
  7.2 0.0 copy-start
  7.2 0.0 copy-start.2
  7.2 0.0 all-gather.3.cloned.1.call-start
  7.2 0.7 all-gather.3.cloned.1.call-update
  7.9 0.0 all-gather.5.cloned.1.call-start
  8.0 0.7 all-gather.5.cloned.1.call-update
  8.7 6.3 all_gather.15
  15.0 5.5 all_gather.17
  20.5 1.3 dynamic-slice
  22.4 1.8 broadcast_add_fusion
  24.2 0.0 copy-start.3
  24.2 380.9 %all-gather.3.cloned.1.call-done = bf16[4096,8192]{1,0:T(8,128)(2,1)} async-done(((bf16[1024,8192]{1,0:T(8,128)(2,1)}), bf16[4096,8192]{1,0:T(8,128)(2,1)}) %all-gather.3.cloned.1.call-update) | async-done | bytes 67108880 | tf_op jit(solution)/shard_map/all_gather | solution.py:13
  405.1 26.5 %fusion.3.clone.4 = bf16[8,4096]{1,0:T(8,128)(2,1)S(1)} fusion(bf16[4096,8192]{1,0:T(8,128)(2,1)} %all-gather.3.cloned.1.call-done, f32[8,8192]{1,0:T(8,128)} %param.10, f32[4096]{0:T(1024)S(1)} %convert_element_type.20, f32[4096]{0:T(1024)S(1)} %convert_element_type.18), kind=kOutput, calls=%fused_computation.5.clone.clone.clone.1 | convolution fusion | flops 537034752 | bytes 67469312 | tf_op jit(solution)/shard_map/dot_general | solution.py:16
  431.6 0.0 copy-done.2
  431.6 22.8 %fusion = bf16[8,8192]{1,0:T(8,128)(2,1)S(1)} fusion(f32[8,8192]{1,0:T(8,128)S(1)} %copy-done.2, bf16[4096,8192]{1,0:T(8,128)(2,1)} %all-gather.3.cloned.1.call-done, bf16[8,4096]{1,0:T(8,128)(2,1)S(1)} %fusion.3.clone.4), kind=kOutput, calls=%fused_computation.1 | convolution fusion | flops 537001984 | bytes 67567616 | tf_op jit(solution)/shard_map/dot_general | solution.py:21
  454.3 0.0 copy-start.1
  454.3 7.2 all_gather.18
  461.5 582.8 %all-gather.5.cloned.1.call-done = bf16[2048,8192]{1,0:T(8,128)(2,1)} async-done(((bf16[2048,1024]{1,0:T(8,128)(2,1)}), bf16[2048,8192]{1,0:T(8,128)(2,1)}) %all-gather.5.cloned.1.call-update) | async-done | bytes 33554448 | tf_op jit(solution)/shard_map/all_gather | solution.py:27
  1044.4 0.0 copy-done
  1044.4 0.0 copy-done.3
  1044.4 15.7 %fusion.7 = f32[32,128]{1,0:T(8,128)S(1)} fusion(bf16[2048,128]{1,0:T(8,128)(2,1)S(1)} %copy-done, bf16[32,8192]{1,0:T(8,128)(2,1)S(1)} %all_gather.18, bf16[2048,8192]{1,0:T(8,128)(2,1)} %all-gather.5.cloned.1.call-done, f32[2048]{0:T(1024)S(1)} %copy-done.3), kind=kOutput, calls=%fused_computation.10 | convolution fusion | flops 1090715648 | bytes 34627584 | tf_op jit(solution)/shard_map/dot_general | solution.py:33
  1060.1 11.2 %all-reduce = f32[32,128]{1,0:T(8,128)S(1)} all-reduce(f32[32,128]{1,0:T(8,128)S(1)} %fusion.7), channel_id=2, replica_groups=mesh['fsdp'=4,'cand'=8] {'fsdp'}, use_global_device_ids=true, to_apply=%region_0.0.clone | all-reduce | flops 4096 | bytes 32768
  1071.3 0.6 constant_dynamic-slice_fusion
  1071.9 0.0 copy-done.1
  (2 shorter events, 0.0 us)
Async XLA Ops:
  7.2 1037.2 %copy-start = (bf16[2048,128]{1,0:T(8,128)(2,1)S(1)}, bf16[2048,128]{1,0:T(8,128)(2,1)}, u32[]{:S(2)}) copy-start(bf16[2048,128]{1,0:T(8,128)(2,1)} %param.17) | copy-start | bytes 1572868
  7.2 424.4 %copy-start.2 = (f32[8,8192]{1,0:T(8,128)S(1)}, f32[8,8192]{1,0:T(8,128)}, u32[]{:S(2)}) copy-start(f32[8,8192]{1,0:T(8,128)} %param.9) | copy-start | bytes 786436
  7.2 397.9 %all-gather.3.cloned.1.call-start = ((), (), s32[]{:S(2)}) async-start(), calls=%async_computation | async-start | bytes 83886080 | tf_op jit(solution)/shard_map/all_gather | solution.py:13
  7.9 1036.4 %all-gather.5.cloned.1.call-start = ((), (), s32[]{:S(2)}) async-start(), calls=%async_computation.1 | async-start | bytes 37748736 | tf_op jit(solution)/shard_map/all_gather | solution.py:27
  24.2 1020.2 %copy-start.3 = (f32[2048]{0:T(1024)S(1)}, f32[2048]{0:T(1024)}, u32[]{:S(2)}) copy-start(f32[2048]{0:T(1024)} %param.16) | copy-start | bytes 24580
  454.3 617.5 %copy-start.1 = (bf16[8,8192]{1,0:T(8,128)(2,1)}, bf16[8,8192]{1,0:T(8,128)(2,1)S(1)}, u32[]{:S(2)}) copy-start(bf16[8,8192]{1,0:T(8,128)(2,1)S(1)} %fusion) | copy-start | bytes 393220
Sparse Core Ops, SparseCore 0:
  9.6 395.4 all-gather.2
  406.6 637.7 all-gather.4
where the time goes:
time: 1080 us
  waiting for transfers between devices  965 us (89%)
  matrix products  65 us (6%)
  blocking collectives  30.2 us (3%)
  between operations  14.8 us (1%)
    all_gather x1, waiting for transfers between devices, local(): lax.all_gather(omega, 'cand', axis=1, tiled=True)  583 us
    all_gather x1, waiting for transfers between devices, local(): rows_piece = lax.all_gather(kernel, 'fsdp', axis=0, tiled=True)  381 us
    dot_general x1, matrix products, local(): lax.dot_general(rounded, rows_piece, (((1,), (1,)), ((), ())), preferred_...  26.5 us
    dot_general x1, matrix products, local(): force = jnp.dot(activated, rows_piece, preferred_element_type=jnp.float32)  22.8 us
  transfers between devices with their start and end apart: 2, of which 2 were waited for; matrix products, arithmetic and copies ran while one was open for 5% of the time, Pallas kernels for 0%

commit v1 on v0

v1 whole, which is shorter than its diff:
```python
import jax
import jax.numpy as jnp
from jax import lax
from jax.sharding import PartitionSpec as P


def local(positions_init, momenta_init, kernel, bias, amplitude, shift, omega, phase, samples):
    f32 = jnp.float32
    features_all = samples.shape[0] * lax.axis_size("fsdp")
    n_fsdp, n_cand = lax.axis_size("fsdp"), lax.axis_size("cand")
    own = positions_init.shape[0]
    rounded = lax.all_gather(momenta_init.astype(jnp.bfloat16), "fsdp", axis=0, tiled=True)
    scores = lax.dot_general(rounded, kernel, (((1,), (1,)), ((), ())), preferred_element_type=f32)
    scores = scores + bias.astype(f32)[None, :]
    activated = (amplitude.astype(f32)[None, :] * jnp.tanh(scores)).astype(jnp.bfloat16)
    partial = jnp.dot(activated, kernel, preferred_element_type=f32)
    force = lax.psum_scatter(partial, "fsdp", scatter_dimension=0, tiled=True)
    positions = momenta_init + shift[None, :]
    tracked = (force - positions_init).astype(jnp.bfloat16)
    columns = lax.all_to_all(tracked, "cand", split_axis=1, concat_axis=0, tiled=True)
    every = lax.all_gather(columns, "fsdp", axis=0, tiled=False)
    every = every.reshape(n_fsdp, n_cand, own, -1).transpose(1, 0, 2, 3).reshape(n_fsdp * n_cand * own, -1)
    part_angles = lax.dot_general(every, omega, (((1,), (1,)), ((), ())), preferred_element_type=f32)
    angles = lax.psum_scatter(part_angles, "cand", scatter_dimension=0, tiled=True)
    features = (jnp.sqrt(2.0 / features_all) * jnp.cos(angles + phase[None, :])).astype(jnp.bfloat16)
    acquisition = lax.psum_scatter(
        jnp.dot(features, samples, preferred_element_type=f32), "fsdp", scatter_dimension=0, tiled=True
    )
    return (tracked, positions, acquisition)


def solution(mesh):
    both = P(("fsdp", "cand"), None)
    return jax.shard_map(
        local,
        mesh=mesh,
        in_specs=(both, both, P("fsdp", None), P("fsdp"), P("fsdp"), P(), P("fsdp", "cand"), P("fsdp"), P("fsdp", None)),
        out_specs=(both, both, both),
        check_vma=False,
    )
```

time: 1080 us -> 175 us (0.16)
  waiting for transfers between devices: 965 us -> 90.1 us
  matrix products: 65 us -> 26.1 us
    all_gather x2 -> x0, waiting for transfers between devices: 964 us -> none  [the longest x1 583 us: local(): lax.all_gather(omega, 'cand', axis=1, tiled=True)]
    reduce_scatter x0 -> x2, waiting for transfers between devices: none -> 90.1 us  [the longest x1 64.2 us: local(): lax.psum_scatter(part_angles, 'cand', scatter_dimension=0, tiled=True)]
    dot_general x3, matrix products: 65 us -> 26.1 us  [the longest x1 19.3 us: local(): partial = jnp.dot(activated, kernel, preferred_element_type=f32)]
    all_to_all x0 -> x1, blocking collectives: none -> 12.6 us  [local(): lax.all_to_all(tracked, 'cand', split_axis=1, concat_axis=0, tiled=True)]
  transfers between devices with their start and end apart: 2 -> 2, of which waited for: 2 -> 2; matrix products, arithmetic and copies ran while one was open for 5% -> 0% of each run, Pallas kernels for 0% -> 0%
where the time goes in v1:
time: 175 us; the launch traced here: 174 us
  waiting for transfers between devices  90.1 us (51%)
  blocking collectives  37.9 us (22%)
  matrix products  26.1 us (15%)
  between operations  14.7 us (8%)
  other arithmetic  4.19 us (2%)
    reduce_scatter x1, waiting for transfers between devices, local(): lax.psum_scatter(part_angles, 'cand', scatter_dimension=0, tiled=True)  64.2 us
    reduce_scatter x1, waiting for transfers between devices, local(): force = lax.psum_scatter(partial, 'fsdp', scatter_dimension=0, tiled=True)  25.9 us
    dot_general x1, matrix products, local(): partial = jnp.dot(activated, kernel, preferred_element_type=f32)  19.3 us
    all_to_all x1, blocking collectives, local(): lax.all_to_all(tracked, 'cand', split_axis=1, concat_axis=0, tiled=True)  12.6 us
    unnamed x1, blocking collectives  10.1 us
    all_gather x1, blocking collectives, local(): lax.all_gather(momenta_init.astype(jnp.bfloat16), 'fsdp', axis=0, tiled=T...  8.63 us
    all_gather x1, blocking collectives, local(): every = lax.all_gather(columns, 'fsdp', axis=0, tiled=False)  6.5 us
    dot_general x1, matrix products, local(): lax.dot_general(every, omega, (((1,), (1,)), ((), ())), preferred_element...  4.86 us
  transfers between devices with their start and end apart: 2, of which 2 were waited for; matrix products, arithmetic and copies ran while one was open for 0% of the time, Pallas kernels for 0%

profile of v1, /device:TPU:0, one launch (start us, length us, event | category | flops | bytes accessed | tf_op | source)
XLA Modules:
  0.0 174.4 jit_solution(1006251369425878409)
XLA Ops:
  7.2 0.0 copy-start
  7.2 0.0 reduce-scatter.3.cloned.1.call-start
  7.2 1.8 %broadcast_add_fusion = (f32[8,8192]{1,0:T(8,128)}, bf16[8,8192]{1,0:T(8,128)(2,1)S(1)}) fusion(f32[8,8192]{1,0:T(8,128)} %param.10, f32[8192]{0:T(1024)} %param.14), kind=kLoop, calls=%fused_computation.10 | loop fusion | flops 131072 | bytes 688128 | tf_op jit(solution)/shard_map/add | solution.py:18
  9.0 8.6 %all_gather.9 = bf16[32,8192]{1,0:T(8,128)(2,1)S(1)} all-gather(bf16[8,8192]{1,0:T(8,128)(2,1)S(1)} %get-tuple-element.4), channel_id=1, replica_groups=mesh['fsdp'=4,'cand'=8] {'fsdp'}, dimensions={0}, use_global_device_ids=true | all-gather | bytes 655360 | tf_op jit(solution)/shard_map/all_gather | solution.py:12
  17.7 0.7 convert_element_type.20
  18.4 0.7 convert_element_type.18
  19.0 0.0 copy-start.2
  19.1 0.0 copy-start.4
  19.1 0.0 copy-start.3
  19.1 19.3 %fusion.3 = f32[32,8192]{1,0:T(8,128)} fusion(bf16[1024,8192]{1,0:T(8,128)(2,1)} %param.11, bf16[32,8192]{1,0:T(8,128)(2,1)S(1)} %all_gather.9, f32[1024]{0:T(1024)S(1)} %convert_element_type.20, f32[1024]{0:T(1024)S(1)} %convert_element_type.18), kind=kOutput, calls=%fused_computation.4 | convolution fusion | flops 1073840128 | bytes 18358272 | tf_op jit(solution)/shard_map/dot_general | solution.py:16
  38.4 0.0 reduce-scatter.3.cloned.1.call-update
  38.4 0.0 reduce-scatter.5.cloned.1.call-start
  38.5 25.9 %reduce-scatter.3.cloned.1.call-done = f32[8,8192]{1,0:T(8,128)} async-done(((f32[32,8192]{1,0:T(8,128)}), f32[8,8192]{1,0:T(8,128)}) %reduce-scatter.3.cloned.1.call-update) | async-done | bytes 262160 | tf_op jit(solution)/shard_map/reduce_scatter | solution.py:17
  64.3 0.0 copy-done.2
  64.3 1.0 subtract_convert_fusion
  65.3 0.0 copy-start.1
  65.3 12.6 %all_to_all.16 = bf16[8,8,1024]{2,0,1:T(8,128)(2,1)S(1)} all-to-all(bf16[8,8,1024]{2,0,1:T(8,128)(2,1)S(1)} %bitcast.16), channel_id=1, replica_groups=mesh['fsdp'=4,'cand'=8] {'cand'}, dimensions={1} | all-to-all | bytes 262144 | tf_op jit(solution)/shard_map/all_to_all | solution.py:20
  78.0 6.5 %all_gather.11 = bf16[4,64,1024]{2,1,0:T(8,128)(2,1)S(1)} all-gather(bf16[1,64,1024]{2,1,0:T(8,128)(2,1)S(1)} %bitcast.17), channel_id=1, replica_groups=mesh['fsdp'=4,'cand'=8] {'fsdp'}, dimensions={0}, use_global_device_ids=true | all-gather | bytes 655360 | tf_op jit(solution)/shard_map/all_gather | solution.py:21
  84.5 4.9 %fusion.10 = f32[256,2048]{1,0:T(8,128)} fusion(bf16[256,1024]{1,0:T(8,128)(2,1)S(1)} %bitcast.18, bf16[2048,1024]{1,0:T(8,128)(2,1)} %param.15), kind=kOutput, calls=%fused_computation.15 | convolution fusion | flops 1073741824 | bytes 6815744 | tf_op jit(solution)/shard_map/dot_general | solution.py:23
  89.4 0.0 reduce-scatter.5.cloned.1.call-update
  89.4 0.0 copy-done.4
  89.4 0.6 dynamic-slice
  90.7 64.2 %reduce-scatter.5.cloned.1.call-done = f32[32,2048]{1,0:T(8,128)} async-done(((f32[256,2048]{1,0:T(8,128)}), f32[32,2048]{1,0:T(8,128)}) %reduce-scatter.5.cloned.1.call-update) | async-done | bytes 262160 | tf_op jit(solution)/shard_map/reduce_scatter | solution.py:24
  154.9 0.0 copy-done
  154.9 0.0 copy-done.3
  154.9 1.9 %fusion.4 = f32[32,128]{1,0:T(8,128)S(1)} fusion(bf16[2048,128]{1,0:T(8,128)(2,1)S(1)} %copy-done, f32[32,2048]{1,0:T(8,128)} %reduce-scatter.5.cloned.1.call-done, f32[2048]{0:T(1024)S(1)} %copy-done.3), kind=kOutput, calls=%fused_computation.7 | convolution fusion | flops 16973824 | bytes 811008 | tf_op jit(solution)/shard_map/dot_general | solution.py:27
  156.8 10.1 %all-reduce = f32[32,128]{1,0:T(8,128)S(1)} all-reduce(f32[32,128]{1,0:T(8,128)S(1)} %fusion.4), channel_id=4, replica_groups=mesh['fsdp'=4,'cand'=8] {'fsdp'}, use_global_device_ids=true, to_apply=%region_2.0.clone | all-reduce | flops 4096 | bytes 32768
  166.9 0.6 constant_dynamic-slice_fusion
  167.5 0.0 copy-done.1
  (1 shorter events, 0.0 us)
Async XLA Ops:
  7.2 147.7 %copy-start = (bf16[2048,128]{1,0:T(8,128)(2,1)S(1)}, bf16[2048,128]{1,0:T(8,128)(2,1)}, u32[]{:S(2)}) copy-start(bf16[2048,128]{1,0:T(8,128)(2,1)} %param.17) | copy-start | bytes 1572868
  7.2 57.2 %reduce-scatter.3.cloned.1.call-start = ((), (), s32[]{:S(2)}) async-start(), calls=%async_computation.3 | async-start | bytes 1310720 | tf_op jit(solution)/shard_map/reduce_scatter | solution.py:17
  19.0 45.3 %copy-start.2 = (f32[8,8192]{1,0:T(8,128)S(1)}, f32[8,8192]{1,0:T(8,128)}, u32[]{:S(2)}) copy-start(f32[8,8192]{1,0:T(8,128)} %param.9) | copy-start | bytes 786436
  19.1 70.4 %copy-start.4 = (u32[32]{0:T(128)S(1)}, u32[32]{0:T(128)}, u32[]{:S(2)}) copy-start(u32[32]{0:T(128)} %constant.6) | copy-start | bytes 388
  19.1 135.8 %copy-start.3 = (f32[2048]{0:T(1024)S(1)}, f32[2048]{0:T(1024)}, u32[]{:S(2)}) copy-start(f32[2048]{0:T(1024)} %param.16) | copy-start | bytes 24580
  38.4 116.5 %reduce-scatter.5.cloned.1.call-start = ((), (), s32[]{:S(2)}) async-start(), calls=%async_computation.4 | async-start | bytes 2359296 | tf_op jit(solution)/shard_map/reduce_scatter | solution.py:24
  65.3 102.2 %copy-start.1 = (bf16[8,8192]{1,0:T(8,128)(2,1)}, bf16[8,8192]{1,0:T(8,128)(2,1)S(1)}, u32[]{:S(2)}) copy-start(bf16[8,8192]{1,0:T(8,128)(2,1)S(1)} %subtract_convert_fusion) | copy-start | bytes 393220
Sparse Core Ops, SparseCore 0:
  38.5 25.7 reduce-scatter.2
  89.5 65.3 reduce-scatter.4

commit v2 on v1

v2 whole, which is shorter than its diff:
```python
import functools
import math

import jax
import jax.numpy as jnp
from jax import lax
from jax.experimental import pallas as pl
from jax.experimental.pallas import tpu as pltpu
from jax.sharding import PartitionSpec as P

F32, BF16 = jnp.float32, jnp.bfloat16
NT = (((1,), (1,)), ((), ()))
VM = pl.BlockSpec(memory_space=pltpu.VMEM)


def swap(x, axis, bit):
    n = lax.axis_size(axis)
    return lax.ppermute(x, axis, [(i, i ^ bit) for i in range(n)])


def force_kernel(m_ref, k_ref, b_ref, a_ref, keep_ref, send_ref, act_ref, *, rows, cols):
    hidden, width = k_ref.shape
    half = keep_ref.shape[0]

    @pl.loop(0, hidden // rows)
    def _(j):
        r = pl.ds(pl.multiple_of(j * rows, rows), rows)
        s = lax.dot_general(m_ref[...], k_ref[r, :], NT, preferred_element_type=F32)
        s = s + b_ref[:, r].astype(F32)
        act_ref[:, r] = (a_ref[:, r].astype(F32) * jnp.tanh(s)).astype(BF16)

    @pl.loop(0, width // cols)
    def _(j):
        c = pl.ds(pl.multiple_of(j * cols, cols), cols)
        f = jnp.dot(act_ref[...], k_ref[:, c], preferred_element_type=F32)
        keep_ref[:, c] = f[:half]
        send_ref[:, c] = f[half:]


def force_parts(m, kernel, bias, amplitude):
    hidden, width = kernel.shape
    n = m.shape[0]
    out = jax.ShapeDtypeStruct((n // 2, width), F32)
    return pl.pallas_call(
        functools.partial(force_kernel, rows=math.gcd(hidden, 512), cols=math.gcd(width, 2048)),
        out_shape=(out, out),
        in_specs=[VM, VM, VM, VM],
        out_specs=(VM, VM),
        scratch_shapes=[pltpu.VMEM((n, hidden), BF16)],
        compiler_params=pltpu.CompilerParams(vmem_limit_bytes=34 * 2**20),
        name="force_parts",
    )(m, pltpu.with_memory_space_constraint(kernel, pltpu.VMEM), bias[None, :], amplitude[None, :])


def angle_kernel(t_ref, w_ref, keep_ref, send_ref, *, block):
    a = lax.dot_general(t_ref[...], w_ref[...], NT, preferred_element_type=F32)
    for i in range(t_ref.shape[0] // (2 * block)):
        keep_ref[i * block : (i + 1) * block, :] = a[2 * i * block : (2 * i + 1) * block]
        send_ref[i * block : (i + 1) * block, :] = a[(2 * i + 1) * block : (2 * i + 2) * block].astype(BF16)


def angle_parts(t, omega, block):
    n, feats = t.shape[0] // 2, omega.shape[0]
    cols = math.gcd(feats, 512)
    return pl.pallas_call(
        functools.partial(angle_kernel, block=block),
        grid=(feats // cols,),
        out_shape=(jax.ShapeDtypeStruct((n, feats), F32), jax.ShapeDtypeStruct((n, feats), BF16)),
        in_specs=[
            pl.BlockSpec(t.shape, lambda i: (0, 0)),
            pl.BlockSpec((cols, omega.shape[1]), lambda i: (i, 0)),
        ],
        out_specs=(pl.BlockSpec((n, cols), lambda i: (0, i)), pl.BlockSpec((n, cols), lambda i: (0, i))),
        compiler_params=pltpu.CompilerParams(vmem_limit_bytes=24 * 2**20),
        name="angle_parts",
    )(t, omega)


def local(positions_init, momenta_init, kernel, bias, amplitude, shift, omega, phase, samples):
    n_fsdp, n_cand = lax.axis_size("fsdp"), lax.axis_size("cand")
    own, width = positions_init.shape
    feats = omega.shape[0]
    bits = [1 << b for b in range(n_fsdp.bit_length() - 1)]
    cand = lax.axis_index("cand")
    outer, inner = cand // 2, cand % 2
    n_outer = n_cand // 2

    m = momenta_init.astype(BF16)
    for bit in reversed(bits):
        m = jnp.concatenate([m, swap(m, "fsdp", bit)], axis=0)
    keep, send = force_parts(m, kernel, bias, amplitude)
    keep = keep + swap(send, "fsdp", 1)
    for bit in bits[1:]:
        half = keep.shape[0] // 2
        keep = keep[:half] + swap(keep[half:].astype(BF16), "fsdp", bit).astype(F32)
    tracked = (keep - positions_init).astype(BF16)
    positions = momenta_init + shift[None, :]

    by_outer = tracked.reshape(own, n_outer, width // n_outer)
    piece = lambda j: lax.dynamic_index_in_dim(by_outer, outer ^ j, axis=1, keepdims=False)
    t = jnp.concatenate([piece(0)] + [swap(piece(j), "cand", 2 * j) for j in range(1, n_outer)], axis=0)
    lo, hi = t[:, : t.shape[1] // 2], t[:, t.shape[1] // 2 :]
    t = jnp.concatenate([jnp.where(inner == 0, lo, hi), swap(jnp.where(inner == 0, hi, lo), "cand", 1)], axis=0)
    for bit in reversed(bits):
        t = jnp.concatenate([t, swap(t, "fsdp", bit)], axis=0)

    keep, send = angle_parts(t, omega, n_outer * own)
    keep = keep + swap(send, "cand", 1).astype(F32)
    keep = keep.reshape(n_fsdp, n_outer, own, feats)
    angles = keep[:, 0]
    for j in range(1, n_outer):
        angles = angles + swap(keep[:, j].astype(BF16), "cand", 2 * j).astype(F32)
    angles = angles.reshape(n_fsdp * own, feats)
    features = (jnp.sqrt(2.0 / (feats * n_fsdp)) * jnp.cos(angles + phase[None, :])).astype(BF16)
    acquisition = jnp.dot(features, samples, preferred_element_type=F32)
    for bit in bits:
        half = acquisition.shape[0] // 2
        acquisition = acquisition[:half] + swap(acquisition[half:], "fsdp", bit)
    return (tracked, positions, acquisition)


def solution(mesh):
    both = P(("fsdp", "cand"), None)
    return jax.shard_map(
        local,
        mesh=mesh,
        in_specs=(both, both, P("fsdp", None), P("fsdp"), P("fsdp"), P(), P("fsdp", "cand"), P("fsdp"), P("fsdp", None)),
        out_specs=(both, both, both),
        check_vma=False,
    )
```

time: 175 us -> 92.4 us (0.53)
  waiting for transfers between devices: 90.1 us -> 48 us
  blocking collectives: 37.9 us -> 0 us
  matrix products: 26.1 us -> 1.03 us
  starting transfers between devices: 0.08 us -> 19.6 us
  between operations: 14.7 us -> 0.82 us
  Pallas kernels: 0 us -> 10.5 us
  local copies, waits for them, and re-layouts: 1.24 us -> 9.42 us
    reduce_scatter x2 -> x0, waiting for transfers between devices: 90.1 us -> none  [the longest x1 64.2 us: local(): lax.psum_scatter(part_angles, 'cand', scatter_dimension=0, tiled=True)]
    ppermute x0 -> x16, waiting for transfers between devices: none -> 48 us  [swap(): return lax.ppermute(x, axis, [(i, i ^ bit) for i in range(n)])]
    dot_general x3 -> x1, matrix products: 26.1 us -> 1.03 us  [local(): acquisition = jnp.dot(features, samples, preferred_element_type=F32)]
    ppermute x0 -> x16, starting transfers between devices: none -> 19.6 us  [swap(): return lax.ppermute(x, axis, [(i, i ^ bit) for i in range(n)])]
    all_gather x2 -> x0, blocking collectives: 15.1 us -> none  [the longest x1 8.63 us: local(): lax.all_gather(momenta_init.astype(jnp.bfloat16), 'fsdp', axis=0, tiled=T...]
    all_to_all x1 -> x0, blocking collectives: 12.6 us -> none  [local(): lax.all_to_all(tracked, 'cand', split_axis=1, concat_axis=0, tiled=True)]
    pallas_call x0 -> x2, Pallas kernels: none -> 10.5 us  [the longest x1 8.49 us: force_parts(): pl.pallas_call(functools.partial(force_kernel, rows=math.gcd(hidden, 512)...]
    unnamed x1 -> x0, blocking collectives: 10.1 us -> none
  transfers between devices with their start and end apart: 2 -> 16, of which waited for: 2 -> 15; matrix products, arithmetic and copies ran while one was open for 0% -> 1% of each run, Pallas kernels for 0% -> 0%
where the time goes in v2:
time: 92.4 us; the launch traced here: 92.1 us
  waiting for transfers between devices  48 us (52%)
  starting transfers between devices  19.6 us (21%)
  Pallas kernels  10.5 us (11%)
  local copies, waits for them, and re-layouts  9.42 us (10%)
  other arithmetic  2.84 us (3%)
  matrix products  1.03 us (1%)
    ppermute x16, waiting for transfers between devices, swap(): return lax.ppermute(x, axis, [(i, i ^ bit) for i in range(n)])  48 us
    ppermute x16, starting transfers between devices, swap(): return lax.ppermute(x, axis, [(i, i ^ bit) for i in range(n)])  19.6 us
    pallas_call x1, Pallas kernels, force_parts(): pl.pallas_call(functools.partial(force_kernel, rows=math.gcd(hidden, 512)...  8.49 us
    unnamed x12, local copies, waits for them, and re-layouts  7.97 us
    pallas_call x1, Pallas kernels, angle_parts(): pl.pallas_call(functools.partial(angle_kernel, block=block), grid=(feats...  1.98 us
  transfers between devices with their start and end apart: 16, of which 15 were waited for; matrix products, arithmetic and copies ran while one was open for 1% of the time, Pallas kernels for 0%

profile of v2, /device:TPU:0, one launch (start us, length us, event | category | flops | bytes accessed | tf_op | source)
XLA Modules:
  0.0 92.1 jit_solution(18402280950277126976)
XLA Ops:
  0.7 1.8 %broadcast_add_fusion = (f32[8,8192]{1,0:T(8,128)}, bf16[8,8192]{1,0:T(8,128)(2,1)S(1)}) fusion(f32[8,8192]{1,0:T(8,128)} %param.10, f32[8192]{0:T(1024)} %param.14), kind=kLoop, calls=%fused_computation.26 | loop fusion | flops 131072 | bytes 688128 | tf_op jit(solution)/shard_map/add | solution.py:97
  2.5 3.0 %collective-permute-start = (bf16[8,8192]{1,0:T(8,128)(2,1)S(1)}, bf16[8,8192]{1,0:T(8,128)(2,1)S(1)}, u32[]{:S(2)}, u32[]{:S(2)}) collective-permute-start(bf16[8,8192]{1,0:T(8,128)(2,1)S(1)} %get-tuple-element.15), channel_id=1, source_target_pairs={{0,16},{8,24},{16,0},{24,8},{1,17},{9,25},{17,1},{25,9},{2,18},{10... | collective-permute-start | bytes 393224 | tf_op jit(solution)/shard_map/ppermute | solution.py:18
  5.5 3.5 %collective-permute-done = bf16[8,8192]{1,0:T(8,128)(2,1)S(1)} collective-permute-done((bf16[8,8192]{1,0:T(8,128)(2,1)S(1)}, bf16[8,8192]{1,0:T(8,128)(2,1)S(1)}, u32[]{:S(2)}, u32[]{:S(2)}) %collective-permute-start) | collective-permute-done | bytes 131104 | tf_op jit(solution)/shard_map/ppermute | solution.py:18
  9.1 0.7 broadcast_in_dim.8.b_ref
  9.8 0.7 broadcast_in_dim.9.a_ref
  10.6 5.8 %copy-done.1 = bf16[1024,8192]{1,0:T(8,128)(2,1)S(1)} copy-done((bf16[1024,8192]{1,0:T(8,128)(2,1)S(1)}, bf16[1024,8192]{1,0:T(8,128)(2,1)}, u32[]{:S(2)}) %copy-start.1) | copy-done | bytes 16777240
  16.4 8.5 %force_parts.1 = (f32[16,8192]{1,0:T(8,128)S(1)}, f32[16,8192]{1,0:T(8,128)S(1)}) custom-call(bf16[32,8192]{1,0:T(8,128)(2,1)S(1)} %pad_maximum_fusion.m_ref, bf16[1024,8192]{1,0:T(8,128)(2,1)S(1)} %copy-done.1, bf16[1,1024]{1,0:T(2,128)(2,1)S(1)} %broadcast_in_dim.8.b_ref, bf16[1,1024]{1,0:T(2,128)(2,1)S(1)} %broadcast_in_dim.9.a_ref), custom_call_target="tpu_custom_call" | custom-call | tf_op jit(solution)/shard_map/force_parts/pallas_call | solution.py:44
  25.3 1.6 %collective-permute-done.2 = f32[16,8192]{1,0:T(8,128)S(1)} collective-permute-done((f32[16,8192]{1,0:T(8,128)S(1)}, f32[16,8192]{1,0:T(8,128)S(1)}, u32[]{:S(2)}, u32[]{:S(2)}) %collective-permute-start.2) | collective-permute-done | bytes 524320 | tf_op jit(solution)/shard_map/ppermute | solution.py:18
  26.9 1.8 %collective-permute-start.3 = (bf16[8,8192]{1,0:T(8,128)(2,1)S(1)}, bf16[8,8192]{1,0:T(8,128)(2,1)S(1)}, u32[]{:S(2)}, u32[]{:S(2)}) collective-permute-start(bf16[8,8192]{1,0:T(8,128)(2,1)S(1)} %slice.97), channel_id=1, source_target_pairs={{0,16},{8,24},{16,0},{24,8},{1,17},{9,25},{17,1},{25,9},{2,18},{10... | collective-permute-start | bytes 393224 | tf_op jit(solution)/shard_map/ppermute | solution.py:18
  28.7 4.0 %collective-permute-done.3 = bf16[8,8192]{1,0:T(8,128)(2,1)S(1)} collective-permute-done((bf16[8,8192]{1,0:T(8,128)(2,1)S(1)}, bf16[8,8192]{1,0:T(8,128)(2,1)S(1)}, u32[]{:S(2)}, u32[]{:S(2)}) %collective-permute-start.3) | collective-permute-done | bytes 131104 | tf_op jit(solution)/shard_map/ppermute | solution.py:18
  32.8 3.9 %collective-permute-start.6 = (bf16[8,2048]{1,0:T(8,128)(2,1)S(1)}, bf16[8,2048]{1,0:T(8,128)(2,1)S(1)}, u32[]{:S(2)}, u32[]{:S(2)}) collective-permute-start(bf16[8,2048]{1,0:T(8,128)(2,1)S(1)} %get-tuple-element.19), channel_id=1, source_target_pairs={{0,6},{1,7},{2,4},{3,5},{4,2},{5,3},{6,0},{7,1},{8,14},{9,15},{10,... | collective-permute-start | bytes 98312 | tf_op jit(solution)/shard_map/ppermute | solution.py:18
  36.7 0.6 collective-permute-start.4
  37.3 1.4 %collective-permute-done.6 = bf16[8,2048]{1,0:T(8,128)(2,1)S(1)} collective-permute-done((bf16[8,2048]{1,0:T(8,128)(2,1)S(1)}, bf16[8,2048]{1,0:T(8,128)(2,1)S(1)}, u32[]{:S(2)}, u32[]{:S(2)}) %collective-permute-start.6) | collective-permute-done | bytes 32800 | tf_op jit(solution)/shard_map/ppermute | solution.py:18
  38.7 2.8 %collective-permute-done.5 = bf16[8,2048]{1,0:T(8,128)(2,1)S(1)} collective-permute-done((bf16[8,2048]{1,0:T(8,128)(2,1)S(1)}, bf16[8,2048]{1,0:T(8,128)(2,1)S(1)}, u32[]{:S(2)}, u32[]{:S(2)}) %collective-permute-start.5) | collective-permute-done | bytes 32800 | tf_op jit(solution)/shard_map/ppermute | solution.py:18
  41.6 1.6 %collective-permute-start.7 = (bf16[32,1024]{1,0:T(8,128)(2,1)S(1)}, bf16[32,1024]{1,0:T(8,128)(2,1)S(1)}, u32[]{:S(2)}, u32[]{:S(2)}) collective-permute-start(bf16[32,1024]{1,0:T(8,128)(2,1)S(1)} %get-tuple-element.17), channel_id=1, source_target_pairs={{0,1},{1,0},{2,3},{3,2},{4,5},{5,4},{6,7},{7,6},{8,9},{9,8},{10,11... | collective-permute-start | bytes 196616 | tf_op jit(solution)/shard_map/ppermute | solution.py:18
  43.1 2.8 %collective-permute-done.7 = bf16[32,1024]{1,0:T(8,128)(2,1)S(1)} collective-permute-done((bf16[32,1024]{1,0:T(8,128)(2,1)S(1)}, bf16[32,1024]{1,0:T(8,128)(2,1)S(1)}, u32[]{:S(2)}, u32[]{:S(2)}) %collective-permute-start.7) | collective-permute-done | bytes 65568 | tf_op jit(solution)/shard_map/ppermute | solution.py:18
  45.9 1.6 %collective-permute-start.8 = (bf16[64,1024]{1,0:T(8,128)(2,1)S(1)}, bf16[64,1024]{1,0:T(8,128)(2,1)S(1)}, u32[]{:S(2)}, u32[]{:S(2)}) collective-permute-start(bf16[64,1024]{1,0:T(8,128)(2,1)S(1)} %pad_maximum_fusion.5), channel_id=1, source_target_pairs={{0,16},{8,24},{16,0},{24,8},{1,17},{9,25},{17,1},{25,9},{2,18},{10... | collective-permute-start | bytes 393224 | tf_op jit(solution)/shard_map/ppermute | solution.py:18
  47.5 3.4 %collective-permute-done.8 = bf16[64,1024]{1,0:T(8,128)(2,1)S(1)} collective-permute-done((bf16[64,1024]{1,0:T(8,128)(2,1)S(1)}, bf16[64,1024]{1,0:T(8,128)(2,1)S(1)}, u32[]{:S(2)}, u32[]{:S(2)}) %collective-permute-start.8) | collective-permute-done | bytes 131104 | tf_op jit(solution)/shard_map/ppermute | solution.py:18
  51.0 1.5 %collective-permute-done.9 = bf16[128,1024]{1,0:T(8,128)(2,1)S(1)} collective-permute-done((bf16[128,1024]{1,0:T(8,128)(2,1)S(1)}, bf16[128,1024]{1,0:T(8,128)(2,1)S(1)}, u32[]{:S(2)}, u32[]{:S(2)}) %collective-permute-start.9) | collective-permute-done | bytes 262176 | tf_op jit(solution)/shard_map/ppermute | solution.py:18
  52.6 2.2 %copy-done.2 = bf16[2048,1024]{1,0:T(8,128)(2,1)S(1)} copy-done((bf16[2048,1024]{1,0:T(8,128)(2,1)S(1)}, bf16[2048,1024]{1,0:T(8,128)(2,1)}, u32[]{:S(2)}) %copy-start.2) | copy-done | bytes 4194328
  54.8 2.0 %angle_parts.1 = (f32[128,2048]{1,0:T(8,128)S(1)}, bf16[128,2048]{1,0:T(8,128)(2,1)S(1)}) custom-call(bf16[256,1024]{1,0:T(8,128)(2,1)S(1)} %pad_maximum_fusion.1.t_ref, bf16[2048,1024]{1,0:T(8,128)(2,1)S(1)} %copy-done.2), custom_call_target="tpu_custom_call" | custom-call | tf_op jit(solution)/shard_map/angle_parts/pallas_call | solution.py:65
  56.8 1.6 %collective-permute-start.10 = (bf16[128,2048]{1,0:T(8,128)(2,1)S(1)}, bf16[128,2048]{1,0:T(8,128)(2,1)S(1)}, u32[]{:S(2)}, u32[]{:S(2)}) collective-permute-start(bf16[128,2048]{1,0:T(8,128)(2,1)S(1)} %get-tuple-element.10), channel_id=1, source_target_pairs={{0,1},{1,0},{2,3},{3,2},{4,5},{5,4},{6,7},{7,6},{8,9},{9,8},{10,11... | collective-permute-start | bytes 1572872 | tf_op jit(solution)/shard_map/ppermute | solution.py:18
  58.3 12.5 %collective-permute-done.10 = bf16[128,2048]{1,0:T(8,128)(2,1)S(1)} collective-permute-done((bf16[128,2048]{1,0:T(8,128)(2,1)S(1)}, bf16[128,2048]{1,0:T(8,128)(2,1)S(1)}, u32[]{:S(2)}, u32[]{:S(2)}) %collective-permute-start.10) | collective-permute-done | bytes 524320 | tf_op jit(solution)/shard_map/ppermute | solution.py:18
  71.1 3.5 %collective-permute-start.13 = (bf16[4,8,2048]{2,1,0:T(8,128)(2,1)S(1)}, bf16[4,8,2048]{2,1,0:T(8,128)(2,1)S(1)}, u32[]{:S(2)}, u32[]{:S(2)}) collective-permute-start(bf16[4,8,2048]{2,1,0:T(8,128)(2,1)S(1)} %get-tuple-element.12), channel_id=1, source_target_pairs={{0,6},{1,7},{2,4},{3,5},{4,2},{5,3},{6,0},{7,1},{8,14},{9,15},{10,... | collective-permute-start | bytes 393224 | tf_op jit(solution)/shard_map/ppermute | solution.py:18
  74.6 2.0 %collective-permute-done.11 = bf16[4,8,2048]{2,1,0:T(8,128)(2,1)S(1)} collective-permute-done((bf16[4,8,2048]{2,1,0:T(8,128)(2,1)S(1)}, bf16[4,8,2048]{2,1,0:T(8,128)(2,1)S(1)}, u32[]{:S(2)}, u32[]{:S(2)}) %collective-permute-start.11) | collective-permute-done | bytes 131104 | tf_op jit(solution)/shard_map/ppermute | solution.py:18
  76.6 4.9 %collective-permute-done.13 = bf16[4,8,2048]{2,1,0:T(8,128)(2,1)S(1)} collective-permute-done((bf16[4,8,2048]{2,1,0:T(8,128)(2,1)S(1)}, bf16[4,8,2048]{2,1,0:T(8,128)(2,1)S(1)}, u32[]{:S(2)}, u32[]{:S(2)}) %collective-permute-start.13) | collective-permute-done | bytes 131104 | tf_op jit(solution)/shard_map/ppermute | solution.py:18
  81.5 4.2 %collective-permute-done.12 = bf16[4,8,2048]{2,1,0:T(8,128)(2,1)S(1)} collective-permute-done((bf16[4,8,2048]{2,1,0:T(8,128)(2,1)S(1)}, bf16[4,8,2048]{2,1,0:T(8,128)(2,1)S(1)}, u32[]{:S(2)}, u32[]{:S(2)}) %collective-permute-start.12) | collective-permute-done | bytes 131104 | tf_op jit(solution)/shard_map/ppermute | solution.py:18
  85.7 1.0 %fusion.10 = f32[32,128]{1,0:T(8,128)S(1)} fusion(bf16[2048,128]{1,0:T(8,128)(2,1)S(1)} %copy-done, f32[4,4,8,2048]{3,2,1,0:T(8,128)S(1)} %bitcast.54, bf16[4,8,2048]{2,1,0:T(8,128)(2,1)S(1)} %collective-permute-done.13, bf16[4,8,2048]{2,1,0:T(8,128)(2,1)S(1)} %collective-permute-done.12, bf16[4,8,2048]{2,1,0:T(8,128)(2,1)S(1)} %collective-permute-done.11, ...), kind=kOutput, calls=%fused_computation.18 | convolution fusion | flops 17367040 | bytes 1204224 | tf_op jit(solution)/shard_map/dot_general | solution.py:115
  86.7 1.2 %collective-permute-done.14 = f32[16,128]{1,0:T(8,128)S(1)} collective-permute-done((f32[16,128]{1,0:T(8,128)S(1)}, f32[16,128]{1,0:T(8,128)S(1)}, u32[]{:S(2)}, u32[]{:S(2)}) %collective-permute-start.14) | collective-permute-done | bytes 8224 | tf_op jit(solution)/shard_map/ppermute | solution.py:18
  87.9 1.5 %collective-permute-start.15 = (f32[8,128]{1,0:T(8,128)S(1)}, f32[8,128]{1,0:T(8,128)S(1)}, u32[]{:S(2)}, u32[]{:S(2)}) collective-permute-start(f32[8,128]{1,0:T(8,128)S(1)} %slice.63), channel_id=1, source_target_pairs={{0,16},{8,24},{16,0},{24,8},{1,17},{9,25},{17,1},{25,9},{2,18},{10... | collective-permute-start | bytes 12296 | tf_op jit(solution)/shard_map/ppermute | solution.py:18
  89.4 2.1 %collective-permute-done.15 = f32[8,128]{1,0:T(8,128)S(1)} collective-permute-done((f32[8,128]{1,0:T(8,128)S(1)}, f32[8,128]{1,0:T(8,128)S(1)}, u32[]{:S(2)}, u32[]{:S(2)}) %collective-permute-start.15) | collective-permute-done | bytes 4128 | tf_op jit(solution)/shard_map/ppermute | solution.py:18
  91.5 0.6 slice_add_fusion.2
  (36 shorter events, 1.3 us)
Async XLA Ops:
  0.6 85.1 %copy-start = (bf16[2048,128]{1,0:T(8,128)(2,1)S(1)}, bf16[2048,128]{1,0:T(8,128)(2,1)}, u32[]{:S(2)}) copy-start(bf16[2048,128]{1,0:T(8,128)(2,1)} %param.17) | copy-start | bytes 1572868
  0.6 32.1 %copy-start.4 = (f32[8,8192]{1,0:T(8,128)S(1)}, f32[8,8192]{1,0:T(8,128)}, u32[]{:S(2)}) copy-start(f32[8,8192]{1,0:T(8,128)} %param.9) | copy-start | bytes 786436
  2.5 6.5 %collective-permute-start = (bf16[8,8192]{1,0:T(8,128)(2,1)S(1)}, bf16[8,8192]{1,0:T(8,128)(2,1)S(1)}, u32[]{:S(2)}, u32[]{:S(2)}) collective-permute-start(bf16[8,8192]{1,0:T(8,128)(2,1)S(1)} %get-tuple-element.15), channel_id=1, source_target_pairs={{0,16},{8,24},{16,0},{24,8},{1,17},{9,25},{17,1},{25,9},{2,18},{10... | collective-permute-start | bytes 393224 | tf_op jit(solution)/shard_map/ppermute | solution.py:18
  9.0 76.7 %copy-start.5 = (f32[2048]{0:T(1024)S(1)}, f32[2048]{0:T(1024)}, u32[]{:S(2)}) copy-start(f32[2048]{0:T(1024)} %param.16) | copy-start | bytes 24580
  9.0 1.6 %collective-permute-start.1 = (bf16[16,8192]{1,0:T(8,128)(2,1)S(1)}, bf16[16,8192]{1,0:T(8,128)(2,1)S(1)}, u32[]{:S(2)}, u32[]{:S(2)}) collective-permute-start(bf16[16,8192]{1,0:T(8,128)(2,1)S(1)} %pad_maximum_fusion.2), channel_id=1, source_target_pairs={{0,8},{8,0},{16,24},{24,16},{1,9},{9,1},{17,25},{25,17},{2,10},{10... | collective-permute-start | bytes 786440 | tf_op jit(solution)/shard_map/ppermute | solution.py:18
  10.6 5.8 %copy-start.1 = (bf16[1024,8192]{1,0:T(8,128)(2,1)S(1)}, bf16[1024,8192]{1,0:T(8,128)(2,1)}, u32[]{:S(2)}) copy-start(bf16[1024,8192]{1,0:T(8,128)(2,1)} %k_ref.1) | copy-start | bytes 50331652
  24.9 1.9 %collective-permute-start.2 = (f32[16,8192]{1,0:T(8,128)S(1)}, f32[16,8192]{1,0:T(8,128)S(1)}, u32[]{:S(2)}, u32[]{:S(2)}) collective-permute-start(f32[16,8192]{1,0:T(8,128)S(1)} %get-tuple-element.8), channel_id=1, source_target_pairs={{0,8},{8,0},{16,24},{24,16},{1,9},{9,1},{17,25},{25,17},{2,10},{10... | collective-permute-start | bytes 1572872 | tf_op jit(solution)/shard_map/ppermute | solution.py:18
  26.9 5.8 %collective-permute-start.3 = (bf16[8,8192]{1,0:T(8,128)(2,1)S(1)}, bf16[8,8192]{1,0:T(8,128)(2,1)S(1)}, u32[]{:S(2)}, u32[]{:S(2)}) collective-permute-start(bf16[8,8192]{1,0:T(8,128)(2,1)S(1)} %slice.97), channel_id=1, source_target_pairs={{0,16},{8,24},{16,0},{24,8},{1,17},{9,25},{17,1},{25,9},{2,18},{10... | collective-permute-start | bytes 393224 | tf_op jit(solution)/shard_map/ppermute | solution.py:18
  32.8 59.3 %copy-start.3 = (bf16[8,8192]{1,0:T(8,128)(2,1)}, bf16[8,8192]{1,0:T(8,128)(2,1)S(1)}, u32[]{:S(2)}) copy-start(bf16[8,8192]{1,0:T(8,128)(2,1)S(1)} %fusion.9) | copy-start | bytes 393220
  32.8 5.9 %collective-permute-start.6 = (bf16[8,2048]{1,0:T(8,128)(2,1)S(1)}, bf16[8,2048]{1,0:T(8,128)(2,1)S(1)}, u32[]{:S(2)}, u32[]{:S(2)}) collective-permute-start(bf16[8,2048]{1,0:T(8,128)(2,1)S(1)} %get-tuple-element.19), channel_id=1, source_target_pairs={{0,6},{1,7},{2,4},{3,5},{4,2},{5,3},{6,0},{7,1},{8,14},{9,15},{10,... | collective-permute-start | bytes 98312 | tf_op jit(solution)/shard_map/ppermute | solution.py:18
  36.7 4.8 %collective-permute-start.5 = (bf16[8,2048]{1,0:T(8,128)(2,1)S(1)}, bf16[8,2048]{1,0:T(8,128)(2,1)S(1)}, u32[]{:S(2)}, u32[]{:S(2)}) collective-permute-start(bf16[8,2048]{1,0:T(8,128)(2,1)S(1)} %get-tuple-element.20), channel_id=1, source_target_pairs={{0,4},{1,5},{2,6},{3,7},{4,0},{5,1},{6,2},{7,3},{8,12},{9,13},{10,... | collective-permute-start | bytes 98312 | tf_op jit(solution)/shard_map/ppermute | solution.py:18
  36.7 4.8 %collective-permute-start.4 = (bf16[8,2048]{1,0:T(8,128)(2,1)S(1)}, bf16[8,2048]{1,0:T(8,128)(2,1)S(1)}, u32[]{:S(2)}, u32[]{:S(2)}) collective-permute-start(bf16[8,2048]{1,0:T(8,128)(2,1)S(1)} %get-tuple-element.21), channel_id=1, source_target_pairs={{0,2},{1,3},{2,0},{3,1},{4,6},{5,7},{6,4},{7,5},{8,10},{9,11},{10,... | collective-permute-start | bytes 98312 | tf_op jit(solution)/shard_map/ppermute | solution.py:18
  41.6 4.3 %collective-permute-start.7 = (bf16[32,1024]{1,0:T(8,128)(2,1)S(1)}, bf16[32,1024]{1,0:T(8,128)(2,1)S(1)}, u32[]{:S(2)}, u32[]{:S(2)}) collective-permute-start(bf16[32,1024]{1,0:T(8,128)(2,1)S(1)} %get-tuple-element.17), channel_id=1, source_target_pairs={{0,1},{1,0},{2,3},{3,2},{4,5},{5,4},{6,7},{7,6},{8,9},{9,8},{10,11... | collective-permute-start | bytes 196616 | tf_op jit(solution)/shard_map/ppermute | solution.py:18
  45.9 5.0 %collective-permute-start.8 = (bf16[64,1024]{1,0:T(8,128)(2,1)S(1)}, bf16[64,1024]{1,0:T(8,128)(2,1)S(1)}, u32[]{:S(2)}, u32[]{:S(2)}) collective-permute-start(bf16[64,1024]{1,0:T(8,128)(2,1)S(1)} %pad_maximum_fusion.5), channel_id=1, source_target_pairs={{0,16},{8,24},{16,0},{24,8},{1,17},{9,25},{17,1},{25,9},{2,18},{10... | collective-permute-start | bytes 393224 | tf_op jit(solution)/shard_map/ppermute | solution.py:18
  51.0 1.6 %collective-permute-start.9 = (bf16[128,1024]{1,0:T(8,128)(2,1)S(1)}, bf16[128,1024]{1,0:T(8,128)(2,1)S(1)}, u32[]{:S(2)}, u32[]{:S(2)}) collective-permute-start(bf16[128,1024]{1,0:T(8,128)(2,1)S(1)} %pad_maximum_fusion.3), channel_id=1, source_target_pairs={{0,8},{8,0},{16,24},{24,16},{1,9},{9,1},{17,25},{25,17},{2,10},{10... | collective-permute-start | bytes 786440 | tf_op jit(solution)/shard_map/ppermute | solution.py:18
  52.6 2.2 %copy-start.2 = (bf16[2048,1024]{1,0:T(8,128)(2,1)S(1)}, bf16[2048,1024]{1,0:T(8,128)(2,1)}, u32[]{:S(2)}) copy-start(bf16[2048,1024]{1,0:T(8,128)(2,1)} %w_ref.1) | copy-start | bytes 12582916
  56.8 14.0 %collective-permute-start.10 = (bf16[128,2048]{1,0:T(8,128)(2,1)S(1)}, bf16[128,2048]{1,0:T(8,128)(2,1)S(1)}, u32[]{:S(2)}, u32[]{:S(2)}) collective-permute-start(bf16[128,2048]{1,0:T(8,128)(2,1)S(1)} %get-tuple-element.10), channel_id=1, source_target_pairs={{0,1},{1,0},{2,3},{3,2},{4,5},{5,4},{6,7},{7,6},{8,9},{9,8},{10,11... | collective-permute-start | bytes 1572872 | tf_op jit(solution)/shard_map/ppermute | solution.py:18
  71.0 5.6 %collective-permute-start.11 = (bf16[4,8,2048]{2,1,0:T(8,128)(2,1)S(1)}, bf16[4,8,2048]{2,1,0:T(8,128)(2,1)S(1)}, u32[]{:S(2)}, u32[]{:S(2)}) collective-permute-start(bf16[4,8,2048]{2,1,0:T(8,128)(2,1)S(1)} %get-tuple-element.11), channel_id=1, source_target_pairs={{0,2},{1,3},{2,0},{3,1},{4,6},{5,7},{6,4},{7,5},{8,10},{9,11},{10,... | collective-permute-start | bytes 393224 | tf_op jit(solution)/shard_map/ppermute | solution.py:18
  71.1 10.4 %collective-permute-start.13 = (bf16[4,8,2048]{2,1,0:T(8,128)(2,1)S(1)}, bf16[4,8,2048]{2,1,0:T(8,128)(2,1)S(1)}, u32[]{:S(2)}, u32[]{:S(2)}) collective-permute-start(bf16[4,8,2048]{2,1,0:T(8,128)(2,1)S(1)} %get-tuple-element.12), channel_id=1, source_target_pairs={{0,6},{1,7},{2,4},{3,5},{4,2},{5,3},{6,0},{7,1},{8,14},{9,15},{10,... | collective-permute-start | bytes 393224 | tf_op jit(solution)/shard_map/ppermute | solution.py:18
  74.6 11.1 %collective-permute-start.12 = (bf16[4,8,2048]{2,1,0:T(8,128)(2,1)S(1)}, bf16[4,8,2048]{2,1,0:T(8,128)(2,1)S(1)}, u32[]{:S(2)}, u32[]{:S(2)}) collective-permute-start(bf16[4,8,2048]{2,1,0:T(8,128)(2,1)S(1)} %get-tuple-element.13), channel_id=1, source_target_pairs={{0,4},{1,5},{2,6},{3,7},{4,0},{5,1},{6,2},{7,3},{8,12},{9,13},{10,... | collective-permute-start | bytes 393224 | tf_op jit(solution)/shard_map/ppermute | solution.py:18
  86.7 1.2 %collective-permute-start.14 = (f32[16,128]{1,0:T(8,128)S(1)}, f32[16,128]{1,0:T(8,128)S(1)}, u32[]{:S(2)}, u32[]{:S(2)}) collective-permute-start(f32[16,128]{1,0:T(8,128)S(1)} %slice.61), channel_id=1, source_target_pairs={{0,8},{8,0},{16,24},{24,16},{1,9},{9,1},{17,25},{25,17},{2,10},{10... | collective-permute-start | bytes 24584 | tf_op jit(solution)/shard_map/ppermute | solution.py:18
  87.9 3.6 %collective-permute-start.15 = (f32[8,128]{1,0:T(8,128)S(1)}, f32[8,128]{1,0:T(8,128)S(1)}, u32[]{:S(2)}, u32[]{:S(2)}) collective-permute-start(f32[8,128]{1,0:T(8,128)S(1)} %slice.63), channel_id=1, source_target_pairs={{0,16},{8,24},{16,0},{24,8},{1,17},{9,25},{17,1},{25,9},{2,18},{10... | collective-permute-start | bytes 12296 | tf_op jit(solution)/shard_map/ppermute | solution.py:18

commit v3 on v2

v3 whole, which is shorter than its diff:
```python
import functools
import math

import jax
import jax.numpy as jnp
from jax import lax
from jax.experimental import pallas as pl
from jax.experimental.pallas import tpu as pltpu
from jax.sharding import PartitionSpec as P

F32, BF16 = jnp.float32, jnp.bfloat16
NT = (((1,), (1,)), ((), ()))
VM = pl.BlockSpec(memory_space=pltpu.VMEM)


def swap(x, axis, bit):
    n = lax.axis_size(axis)
    return lax.ppermute(x, axis, [(i, i ^ bit) for i in range(n)])


def swap_both(x, fsdp_bit, cand_bit):
    m, n = lax.axis_size("fsdp"), lax.axis_size("cand")
    pairs = [(i * n + j, (i ^ fsdp_bit) * n + (j ^ cand_bit)) for i in range(m) for j in range(n)]
    return lax.ppermute(x, ("fsdp", "cand"), pairs)


def load_kernel(src_ref, *refs, start):
    *dst_refs, sems = refs
    copies = []
    for dst_ref in dst_refs:
        copies.append(pltpu.make_async_copy(src_ref.at[pl.ds(start, dst_ref.shape[0])], dst_ref, sems.at[len(copies)]))
        copies[-1].start()
        start += dst_ref.shape[0]
    for c in copies:
        c.wait()


def load(x, start, sizes, name):
    return pl.pallas_call(
        functools.partial(load_kernel, start=start),
        out_shape=tuple(pltpu.VMEM((rows, x.shape[1]), x.dtype) for rows in sizes),
        in_specs=[pl.BlockSpec(memory_space=pltpu.HBM)],
        out_specs=(VM,) * len(sizes),
        scratch_shapes=[pltpu.SemaphoreType.DMA((len(sizes),))],
        compiler_params=pltpu.CompilerParams(vmem_limit_bytes=2**20),
        cost_estimate=pl.CostEstimate(
            flops=0, bytes_accessed=2 * sum(sizes) * x.shape[1] * x.dtype.itemsize, transcendentals=0
        ),
        name=name,
    )(x)


def force_kernel(m_ref, first_ref, second_ref, b_ref, a_ref, keep_ref, send_ref, act_ref, *, cols):
    early, width = first_ref.shape
    half = keep_ref.shape[0]
    at = 0
    for ref in (first_ref, second_ref):
        s = lax.dot_general(m_ref[...], ref[...], NT, preferred_element_type=F32)
        c = slice(at, at + ref.shape[0])
        s = s + b_ref[:, c].astype(F32)
        act_ref[:, c] = (a_ref[:, c].astype(F32) * jnp.tanh(s)).astype(BF16)
        at += ref.shape[0]

    @pl.loop(0, width // cols)
    def _(j):
        c = pl.ds(pl.multiple_of(j * cols, cols), cols)
        f = jnp.dot(act_ref[:, :early], first_ref[:, c], preferred_element_type=F32)
        f = f + jnp.dot(act_ref[:, early:], second_ref[:, c], preferred_element_type=F32)
        keep_ref[:, c] = f[:half]
        send_ref[:, c] = f[half:]


def force_parts(m, first, second, bias, amplitude):
    n, width = m.shape
    hidden = bias.shape[0]
    out = pltpu.VMEM((n // 2, width), F32)
    return pl.pallas_call(
        functools.partial(force_kernel, cols=math.gcd(width, 2048)),
        out_shape=(out, out),
        in_specs=[VM] * 5,
        out_specs=(VM, VM),
        scratch_shapes=[pltpu.VMEM((n, hidden), BF16)],
        compiler_params=pltpu.CompilerParams(vmem_limit_bytes=8 * 2**20),
        cost_estimate=pl.CostEstimate(
            flops=4 * 256 * hidden * width, bytes_accessed=2 * hidden * width, transcendentals=n * hidden
        ),
        name="force_parts",
    )(m, first, second, bias[None, :], amplitude[None, :])


def angle_kernel(t_ref, w_ref, keep_ref, send_ref, *, block):
    a = lax.dot_general(t_ref[...], w_ref[...], NT, preferred_element_type=F32)
    for i in range(t_ref.shape[0] // (2 * block)):
        keep_ref[i * block : (i + 1) * block, :] = a[2 * i * block : (2 * i + 1) * block]
        send_ref[i * block : (i + 1) * block, :] = a[(2 * i + 1) * block : (2 * i + 2) * block].astype(BF16)


def angle_parts(t, omega, block):
    n, cols = t.shape[0] // 2, omega.shape[0]
    return pl.pallas_call(
        functools.partial(angle_kernel, block=block),
        out_shape=(pltpu.VMEM((n, cols), F32), pltpu.VMEM((n, cols), BF16)),
        in_specs=[VM, VM],
        out_specs=(VM, VM),
        compiler_params=pltpu.CompilerParams(vmem_limit_bytes=8 * 2**20),
        cost_estimate=pl.CostEstimate(
            flops=4 * n * cols * t.shape[1], bytes_accessed=2 * cols * t.shape[1], transcendentals=0
        ),
        name="angle_parts",
    )(t, omega)


def local(positions_init, momenta_init, kernel, bias, amplitude, shift, omega, phase, samples):
    n_fsdp, n_cand = lax.axis_size("fsdp"), lax.axis_size("cand")
    own, width = positions_init.shape
    feats = omega.shape[0]
    bits = [1 << b for b in range(n_fsdp.bit_length() - 1)]
    cand = lax.axis_index("cand")
    outer, inner = cand // 2, cand % 2
    n_outer = n_cand // 2
    kernel = pltpu.with_memory_space_constraint(kernel, pltpu.HBM)
    omega = pltpu.with_memory_space_constraint(omega, pltpu.HBM)

    early = kernel.shape[0] * 5 // 8
    first = load(kernel, 0, [early], "load_first")[0]
    second = load(kernel, early, [kernel.shape[0] - early], "load_second")[0]
    m = momenta_init.astype(BF16)
    for bit in reversed(bits):
        if bit == 1:
            m, first = lax.optimization_barrier((m, first))
        m = jnp.concatenate([m, swap(m, "fsdp", bit)], axis=0)
    keep, send = force_parts(m, first, second, bias, amplitude)
    keep = keep + swap(send, "fsdp", 1)
    for bit in bits[1:]:
        half = keep.shape[0] // 2
        keep = keep[:half] + swap(keep[half:].astype(BF16), "fsdp", bit).astype(F32)
    tracked = (keep - positions_init).astype(BF16)

    by_outer = tracked.reshape(own, n_outer, width // n_outer)
    piece = lambda j: lax.dynamic_index_in_dim(by_outer, outer ^ j, axis=1, keepdims=False)
    t = jnp.concatenate([piece(0)] + [swap(piece(j), "cand", 2 * j) for j in range(1, n_outer)], axis=0)
    lo, hi = t[:, : t.shape[1] // 2], t[:, t.shape[1] // 2 :]
    mine, other = jnp.where(inner == 0, lo, hi), jnp.where(inner == 0, hi, lo)
    mine, other, omega = lax.optimization_barrier((mine, other, omega))
    omega = load(omega, 0, [feats // 2, feats // 2], "load_omega")
    t = jnp.concatenate([mine, swap(other, "cand", 1), swap(mine, "fsdp", 2), swap_both(other, 2, 1)], axis=0)
    t, omega = lax.optimization_barrier((t, omega))
    for bit in reversed(bits):
        if bit == 2:
            continue
        t = jnp.concatenate([t, swap(t, "fsdp", bit)], axis=0)
    t, momenta_init = lax.optimization_barrier((t, momenta_init))
    positions = momenta_init + shift[None, :]

    sums = []
    for w in omega:
        keep, send = angle_parts(t, w, n_outer * own)
        sums.append(keep + swap(send, "cand", 1).astype(F32))
    acquisition = 0.0
    start = 0
    for keep in sums:
        cols = keep.shape[1]
        keep = keep.reshape(n_fsdp, n_outer, own, cols)
        angles = keep[:, 0]
        for j in range(1, n_outer):
            angles = angles + swap(keep[:, j].astype(BF16), "cand", 2 * j).astype(F32)
        c = slice(start, start + cols)
        start += cols
        angles = angles.reshape(n_fsdp * own, cols) + phase[None, c]
        features = (jnp.sqrt(2.0 / (feats * n_fsdp)) * jnp.cos(angles)).astype(BF16)
        acquisition = acquisition + jnp.dot(features, samples[c], preferred_element_type=F32)
    for bit in bits:
        half = acquisition.shape[0] // 2
        acquisition = acquisition[:half] + swap(acquisition[half:], "fsdp", bit)
    return (tracked, positions, acquisition)


def solution(mesh):
    both = P(("fsdp", "cand"), None)
    return jax.shard_map(
        local,
        mesh=mesh,
        in_specs=(both, both, P("fsdp", None), P("fsdp"), P("fsdp"), P(), P("fsdp", "cand"), P("fsdp"), P("fsdp", None)),
        out_specs=(both, both, both),
        check_vma=False,
    )
```

time: 92.4 us -> 75.4 us (0.82)
  waiting for transfers between devices: 48 us -> 26.1 us
  local copies, waits for them, and re-layouts: 9.42 us -> 0.14 us
  Pallas kernels: 10.5 us -> 18.9 us
  starting transfers between devices: 19.6 us -> 25.3 us
    ppermute x16 -> x20, waiting for transfers between devices: 48 us -> 26.1 us  [swap(): return lax.ppermute(x, axis, [(i, i ^ bit) for i in range(n)])]
    pallas_call x2 -> x6, Pallas kernels: 10.5 us -> 18.9 us  [the longest x3 9.02 us: load(): pl.pallas_call(functools.partial(load_kernel, start=start), out_shape=tup...]
    unnamed x12 -> x16, local copies, waits for them, and re-layouts: 7.97 us -> 0.05 us
    ppermute x16 -> x20, starting transfers between devices: 19.6 us -> 23.1 us  [swap(): return lax.ppermute(x, axis, [(i, i ^ bit) for i in range(n)])]
    ppermute x0 -> x1, starting transfers between devices: none -> 2.21 us  [swap_both(): return lax.ppermute(x, ('fsdp', 'cand'), pairs)]
    add x1, other arithmetic: 1.84 us -> 0.73 us  [local(): positions = momenta_init + shift[None, :]]
    convert_element_type x0 -> x1, other arithmetic: none -> 0.97 us  [local(): m = momenta_init.astype(BF16)]
  transfers between devices with their start and end apart: 16 -> 21, of which waited for: 15 -> 13; matrix products, arithmetic and copies ran while one was open for 1% -> 2% of each run, Pallas kernels for 0% -> 13%
where the time goes in v3:
time: 75.4 us; the launch traced here: 75.2 us
  waiting for transfers between devices  26.1 us (35%)
  starting transfers between devices  25.3 us (34%)
  Pallas kernels  18.9 us (25%)
  other arithmetic  2.71 us (4%)
  matrix products  1.18 us (2%)
  between operations  0.94 us (1%)
    ppermute x20, waiting for transfers between devices, swap(): return lax.ppermute(x, axis, [(i, i ^ bit) for i in range(n)])  26.1 us
    ppermute x20, starting transfers between devices, swap(): return lax.ppermute(x, axis, [(i, i ^ bit) for i in range(n)])  23.1 us
    pallas_call x3, Pallas kernels, load(): pl.pallas_call(functools.partial(load_kernel, start=start), out_shape=tup...  9.02 us
    pallas_call x1, Pallas kernels, force_parts(): pl.pallas_call(functools.partial(force_kernel, cols=math.gcd(width, 2048)...  8.37 us
    ppermute x1, starting transfers between devices, swap_both(): return lax.ppermute(x, ('fsdp', 'cand'), pairs)  2.21 us
  transfers between devices with their start and end apart: 21, of which 13 were waited for; matrix products, arithmetic and copies ran while one was open for 2% of the time, Pallas kernels for 13%

profile of v3, /device:TPU:0, one launch (start us, length us, event | category | flops | bytes accessed | tf_op | source)
XLA Modules:
  0.0 75.2 jit_solution(10055639260846232474)
XLA Ops:
  0.6 1.0 %convert_element_type.64 = bf16[8,8192]{1,0:T(8,128)(2,1)S(1)} convert(f32[8,8192]{1,0:T(8,128)} %param.10) | non-fusion elementwise | flops 65536 | bytes 393216 | tf_op jit(solution)/shard_map/convert_element_type | solution.py:127
  1.6 3.0 %collective-permute-start = (bf16[8,8192]{1,0:T(8,128)(2,1)S(1)}, bf16[8,8192]{1,0:T(8,128)(2,1)S(1)}, u32[]{:S(2)}, u32[]{:S(2)}) collective-permute-start(bf16[8,8192]{1,0:T(8,128)(2,1)S(1)} %convert_element_type.64), channel_id=1, source_target_pairs={{0,16},{8,24},{16,0},{24,8},{1,17},{9,25},{17,1},{25,9},{2,18},{10... | collective-permute-start | bytes 393224 | tf_op jit(solution)/shard_map/ppermute | solution.py:18
  4.6 4.0 %load_first.1.first_ref = bf16[640,8192]{1,0:T(8,128)(2,1)S(1)} custom-call(bf16[1024,8192]{1,0:T(8,128)(2,1)} %src_ref.3), custom_call_target="tpu_custom_call" | custom-call | bytes 20971520 | tf_op jit(solution)/shard_map/load_first/pallas_call | solution.py:39
  8.8 2.8 %load_second.1.second_ref = bf16[384,8192]{1,0:T(8,128)(2,1)S(1)} custom-call(bf16[1024,8192]{1,0:T(8,128)(2,1)} %src_ref.3), custom_call_target="tpu_custom_call" | custom-call | bytes 12582912 | tf_op jit(solution)/shard_map/load_second/pallas_call | solution.py:39
  11.7 8.4 %force_parts.1 = (f32[16,8192]{1,0:T(8,128)S(1)}, f32[16,8192]{1,0:T(8,128)S(1)}) custom-call(bf16[32,8192]{1,0:T(8,128)(2,1)S(1)} %pad_maximum_fusion.m_ref, bf16[640,8192]{1,0:T(8,128)(2,1)S(1)} %load_first.1.first_ref, bf16[384,8192]{1,0:T(8,128)(2,1)S(1)} %load_second.1.second_ref, bf16[1,1024]{1,0:T(2,128)(2,1)S(1)} %broadcast_in_dim.4.b_ref, ...), custom_call_target="tpu_custom_call" | custom-call | flops 8589934592 | bytes 16777216 | tf_op jit(solution)/shard_map/force_parts/pallas_call | solution.py:77
  20.6 1.5 %collective-permute-done.2 = f32[16,8192]{1,0:T(8,128)S(1)} collective-permute-done((f32[16,8192]{1,0:T(8,128)S(1)}, f32[16,8192]{1,0:T(8,128)S(1)}, u32[]{:S(2)}, u32[]{:S(2)}) %collective-permute-start.2) | collective-permute-done | bytes 524320 | tf_op jit(solution)/shard_map/ppermute | solution.py:18
  22.2 1.3 %collective-permute-start.3 = (bf16[8,8192]{1,0:T(8,128)(2,1)S(1)}, bf16[8,8192]{1,0:T(8,128)(2,1)S(1)}, u32[]{:S(2)}, u32[]{:S(2)}) collective-permute-start(bf16[8,8192]{1,0:T(8,128)(2,1)S(1)} %slice.161), channel_id=1, source_target_pairs={{0,16},{8,24},{16,0},{24,8},{1,17},{9,25},{17,1},{25,9},{2,18},{10... | collective-permute-start | bytes 393224 | tf_op jit(solution)/shard_map/ppermute | solution.py:18
  23.5 4.5 %collective-permute-done.3 = bf16[8,8192]{1,0:T(8,128)(2,1)S(1)} collective-permute-done((bf16[8,8192]{1,0:T(8,128)(2,1)S(1)}, bf16[8,8192]{1,0:T(8,128)(2,1)S(1)}, u32[]{:S(2)}, u32[]{:S(2)}) %collective-permute-start.3) | collective-permute-done | bytes 131104 | tf_op jit(solution)/shard_map/ppermute | solution.py:18
  28.1 3.7 %collective-permute-start.6 = (bf16[8,2048]{1,0:T(8,128)(2,1)S(1)}, bf16[8,2048]{1,0:T(8,128)(2,1)S(1)}, u32[]{:S(2)}, u32[]{:S(2)}) collective-permute-start(bf16[8,2048]{1,0:T(8,128)(2,1)S(1)} %get-tuple-element.48), channel_id=1, source_target_pairs={{0,6},{1,7},{2,4},{3,5},{4,2},{5,3},{6,0},{7,1},{8,14},{9,15},{10,... | collective-permute-start | bytes 98312 | tf_op jit(solution)/shard_map/ppermute | solution.py:18
  31.8 0.8 %collective-permute-start.4 = (bf16[8,2048]{1,0:T(8,128)(2,1)S(1)}, bf16[8,2048]{1,0:T(8,128)(2,1)S(1)}, u32[]{:S(2)}, u32[]{:S(2)}) collective-permute-start(bf16[8,2048]{1,0:T(8,128)(2,1)S(1)} %get-tuple-element.50), channel_id=1, source_target_pairs={{0,2},{1,3},{2,0},{3,1},{4,6},{5,7},{6,4},{7,5},{8,10},{9,11},{10,... | collective-permute-start | bytes 98312 | tf_op jit(solution)/shard_map/ppermute | solution.py:18
  32.6 1.7 %collective-permute-done.6 = bf16[8,2048]{1,0:T(8,128)(2,1)S(1)} collective-permute-done((bf16[8,2048]{1,0:T(8,128)(2,1)S(1)}, bf16[8,2048]{1,0:T(8,128)(2,1)S(1)}, u32[]{:S(2)}, u32[]{:S(2)}) %collective-permute-start.6) | collective-permute-done | bytes 32800 | tf_op jit(solution)/shard_map/ppermute | solution.py:18
  34.2 2.4 %collective-permute-done.5 = bf16[8,2048]{1,0:T(8,128)(2,1)S(1)} collective-permute-done((bf16[8,2048]{1,0:T(8,128)(2,1)S(1)}, bf16[8,2048]{1,0:T(8,128)(2,1)S(1)}, u32[]{:S(2)}, u32[]{:S(2)}) %collective-permute-start.5) | collective-permute-done | bytes 32800 | tf_op jit(solution)/shard_map/ppermute | solution.py:18
  36.6 2.2 %collective-permute-start.9 = (bf16[32,1024]{1,0:T(8,128)(2,1)S(1)}, bf16[32,1024]{1,0:T(8,128)(2,1)S(1)}, u32[]{:S(2)}, u32[]{:S(2)}) collective-permute-start(bf16[32,1024]{1,0:T(8,128)(2,1)S(1)} %get-tuple-element.26), channel_id=1, source_target_pairs={{0,17},{1,16},{2,19},{3,18},{4,21},{5,20},{6,23},{7,22},{8,25},{9,... | collective-permute-start | bytes 196616 | tf_op jit(solution)/shard_map/ppermute | solution.py:24
  38.9 0.8 %collective-permute-start.8 = (bf16[32,1024]{1,0:T(8,128)(2,1)S(1)}, bf16[32,1024]{1,0:T(8,128)(2,1)S(1)}, u32[]{:S(2)}, u32[]{:S(2)}) collective-permute-start(bf16[32,1024]{1,0:T(8,128)(2,1)S(1)} %get-tuple-element.25), channel_id=1, source_target_pairs={{0,16},{8,24},{16,0},{24,8},{1,17},{9,25},{17,1},{25,9},{2,18},{10... | collective-permute-start | bytes 196616 | tf_op jit(solution)/shard_map/ppermute | solution.py:18
  40.2 2.2 %load_omega.1 = (bf16[1024,1024]{1,0:T(8,128)(2,1)S(1)}, bf16[1024,1024]{1,0:T(8,128)(2,1)S(1)}) custom-call(bf16[2048,1024]{1,0:T(8,128)(2,1)} %src_ref.4), custom_call_target="tpu_custom_call" | custom-call | bytes 8388608 | tf_op jit(solution)/shard_map/load_omega/pallas_call | solution.py:39
  42.5 0.7 collective-permute-done.8
  43.1 0.8 %collective-permute-done.7 = bf16[32,1024]{1,0:T(8,128)(2,1)S(1)} collective-permute-done((bf16[32,1024]{1,0:T(8,128)(2,1)S(1)}, bf16[32,1024]{1,0:T(8,128)(2,1)S(1)}, u32[]{:S(2)}, u32[]{:S(2)}) %collective-permute-start.7) | collective-permute-done | bytes 65568 | tf_op jit(solution)/shard_map/ppermute | solution.py:18
  44.1 1.5 %collective-permute-done.10 = bf16[128,1024]{1,0:T(8,128)(2,1)S(1)} collective-permute-done((bf16[128,1024]{1,0:T(8,128)(2,1)S(1)}, bf16[128,1024]{1,0:T(8,128)(2,1)S(1)}, u32[]{:S(2)}, u32[]{:S(2)}) %collective-permute-start.10) | collective-permute-done | bytes 262176 | tf_op jit(solution)/shard_map/ppermute | solution.py:18
  45.6 0.7 angle_parts.2
  47.0 0.7 angle_parts.3
  47.7 1.6 %collective-permute-start.15 = (bf16[128,1024]{1,0:T(8,128)(2,1)S(1)}, bf16[128,1024]{1,0:T(8,128)(2,1)S(1)}, u32[]{:S(2)}, u32[]{:S(2)}) collective-permute-start(bf16[128,1024]{1,0:T(8,128)(2,1)S(1)} %get-tuple-element.38), channel_id=1, source_target_pairs={{0,1},{1,0},{2,3},{3,2},{4,5},{5,4},{6,7},{7,6},{8,9},{9,8},{10,11... | collective-permute-start | bytes 786440 | tf_op jit(solution)/shard_map/ppermute | solution.py:18
  49.3 6.3 %collective-permute-done.11 = bf16[128,1024]{1,0:T(8,128)(2,1)S(1)} collective-permute-done((bf16[128,1024]{1,0:T(8,128)(2,1)S(1)}, bf16[128,1024]{1,0:T(8,128)(2,1)S(1)}, u32[]{:S(2)}, u32[]{:S(2)}) %collective-permute-start.11) | collective-permute-done | bytes 262176 | tf_op jit(solution)/shard_map/ppermute | solution.py:18
  55.7 1.5 %collective-permute-start.14 = (bf16[4,8,1024]{2,1,0:T(8,128)(2,1)S(1)}, bf16[4,8,1024]{2,1,0:T(8,128)(2,1)S(1)}, u32[]{:S(2)}, u32[]{:S(2)}) collective-permute-start(bf16[4,8,1024]{2,1,0:T(8,128)(2,1)S(1)} %get-tuple-element.43), channel_id=1, source_target_pairs={{0,6},{1,7},{2,4},{3,5},{4,2},{5,3},{6,0},{7,1},{8,14},{9,15},{10,... | collective-permute-start | bytes 196616 | tf_op jit(solution)/shard_map/ppermute | solution.py:18
  57.9 2.3 %collective-permute-start.12 = (bf16[4,8,1024]{2,1,0:T(8,128)(2,1)S(1)}, bf16[4,8,1024]{2,1,0:T(8,128)(2,1)S(1)}, u32[]{:S(2)}, u32[]{:S(2)}) collective-permute-start(bf16[4,8,1024]{2,1,0:T(8,128)(2,1)S(1)} %get-tuple-element.42), channel_id=1, source_target_pairs={{0,2},{1,3},{2,0},{3,1},{4,6},{5,7},{6,4},{7,5},{8,10},{9,11},{10,... | collective-permute-start | bytes 196616 | tf_op jit(solution)/shard_map/ppermute | solution.py:18
  60.5 1.5 %collective-permute-start.18 = (bf16[4,8,1024]{2,1,0:T(8,128)(2,1)S(1)}, bf16[4,8,1024]{2,1,0:T(8,128)(2,1)S(1)}, u32[]{:S(2)}, u32[]{:S(2)}) collective-permute-start(bf16[4,8,1024]{2,1,0:T(8,128)(2,1)S(1)} %get-tuple-element.40), channel_id=1, source_target_pairs={{0,6},{1,7},{2,4},{3,5},{4,2},{5,3},{6,0},{7,1},{8,14},{9,15},{10,... | collective-permute-start | bytes 196616 | tf_op jit(solution)/shard_map/ppermute | solution.py:18
  62.7 2.3 %collective-permute-start.16 = (bf16[4,8,1024]{2,1,0:T(8,128)(2,1)S(1)}, bf16[4,8,1024]{2,1,0:T(8,128)(2,1)S(1)}, u32[]{:S(2)}, u32[]{:S(2)}) collective-permute-start(bf16[4,8,1024]{2,1,0:T(8,128)(2,1)S(1)} %get-tuple-element.39), channel_id=1, source_target_pairs={{0,2},{1,3},{2,0},{3,1},{4,6},{5,7},{6,4},{7,5},{8,10},{9,11},{10,... | collective-permute-start | bytes 196616 | tf_op jit(solution)/shard_map/ppermute | solution.py:18
  65.6 1.7 %collective-permute-done.18 = bf16[4,8,1024]{2,1,0:T(8,128)(2,1)S(1)} collective-permute-done((bf16[4,8,1024]{2,1,0:T(8,128)(2,1)S(1)}, bf16[4,8,1024]{2,1,0:T(8,128)(2,1)S(1)}, u32[]{:S(2)}, u32[]{:S(2)}) %collective-permute-start.18) | collective-permute-done | bytes 65568 | tf_op jit(solution)/shard_map/ppermute | solution.py:18
  67.2 2.0 %collective-permute-done.17 = bf16[4,8,1024]{2,1,0:T(8,128)(2,1)S(1)} collective-permute-done((bf16[4,8,1024]{2,1,0:T(8,128)(2,1)S(1)}, bf16[4,8,1024]{2,1,0:T(8,128)(2,1)S(1)}, u32[]{:S(2)}, u32[]{:S(2)}) %collective-permute-start.17) | collective-permute-done | bytes 65568 | tf_op jit(solution)/shard_map/ppermute | solution.py:18
  69.8 1.2 %collective-permute-done.19 = f32[16,128]{1,0:T(8,128)S(1)} collective-permute-done((f32[16,128]{1,0:T(8,128)S(1)}, f32[16,128]{1,0:T(8,128)S(1)}, u32[]{:S(2)}, u32[]{:S(2)}) %collective-permute-start.19) | collective-permute-done | bytes 8224 | tf_op jit(solution)/shard_map/ppermute | solution.py:18
  71.0 1.2 %collective-permute-start.20 = (f32[8,128]{1,0:T(8,128)S(1)}, f32[8,128]{1,0:T(8,128)S(1)}, u32[]{:S(2)}, u32[]{:S(2)}) collective-permute-start(f32[8,128]{1,0:T(8,128)S(1)} %slice.102), channel_id=1, source_target_pairs={{0,16},{8,24},{16,0},{24,8},{1,17},{9,25},{17,1},{25,9},{2,18},{10... | collective-permute-start | bytes 12296 | tf_op jit(solution)/shard_map/ppermute | solution.py:18
  72.2 0.7 broadcast_add_fusion
  73.0 1.6 %collective-permute-done.20 = f32[8,128]{1,0:T(8,128)S(1)} collective-permute-done((f32[8,128]{1,0:T(8,128)S(1)}, f32[8,128]{1,0:T(8,128)S(1)}, u32[]{:S(2)}, u32[]{:S(2)}) %collective-permute-start.20) | collective-permute-done | bytes 4128 | tf_op jit(solution)/shard_map/ppermute | solution.py:18
  (59 shorter events, 5.7 us)
Async XLA Ops:
  1.6 7.0 %collective-permute-start = (bf16[8,8192]{1,0:T(8,128)(2,1)S(1)}, bf16[8,8192]{1,0:T(8,128)(2,1)S(1)}, u32[]{:S(2)}, u32[]{:S(2)}) collective-permute-start(bf16[8,8192]{1,0:T(8,128)(2,1)S(1)} %convert_element_type.64), channel_id=1, source_target_pairs={{0,16},{8,24},{16,0},{24,8},{1,17},{9,25},{17,1},{25,9},{2,18},{10... | collective-permute-start | bytes 393224 | tf_op jit(solution)/shard_map/ppermute | solution.py:18
  8.7 2.9 %copy-start.6 = (bf16[1024]{0:T(1024)(128)(2,1)S(1)}, bf16[1024]{0:T(1024)(128)(2,1)}, u32[]{:S(2)}) copy-start(bf16[1024]{0:T(1024)(128)(2,1)} %param.12) | copy-start | bytes 6148
  8.7 2.9 %copy-start.7 = (bf16[1024]{0:T(1024)(128)(2,1)S(1)}, bf16[1024]{0:T(1024)(128)(2,1)}, u32[]{:S(2)}) copy-start(bf16[1024]{0:T(1024)(128)(2,1)} %param.13) | copy-start | bytes 6148
  8.7 2.9 %collective-permute-start.1 = (bf16[16,8192]{1,0:T(8,128)(2,1)S(1)}, bf16[16,8192]{1,0:T(8,128)(2,1)S(1)}, u32[]{:S(2)}, u32[]{:S(2)}) collective-permute-start(bf16[16,8192]{1,0:T(8,128)(2,1)S(1)} %pad_maximum_fusion.2), channel_id=1, source_target_pairs={{0,8},{8,0},{16,24},{24,16},{1,9},{9,1},{17,25},{25,17},{2,10},{10... | collective-permute-start | bytes 786440 | tf_op jit(solution)/shard_map/ppermute | solution.py:18
  11.7 16.4 %copy-start.3 = (f32[8,8192]{1,0:T(8,128)S(1)}, f32[8,8192]{1,0:T(8,128)}, u32[]{:S(2)}) copy-start(f32[8,8192]{1,0:T(8,128)} %param.9) | copy-start | bytes 786436
  20.1 26.9 %copy-start.5 = (f32[2048]{0:T(1024)S(1)}, f32[2048]{0:T(1024)}, u32[]{:S(2)}) copy-start(f32[2048]{0:T(1024)} %param.16) | copy-start | bytes 24580
  20.1 2.1 %collective-permute-start.2 = (f32[16,8192]{1,0:T(8,128)S(1)}, f32[16,8192]{1,0:T(8,128)S(1)}, u32[]{:S(2)}, u32[]{:S(2)}) collective-permute-start(f32[16,8192]{1,0:T(8,128)S(1)} %get-tuple-element.24), channel_id=1, source_target_pairs={{0,8},{8,0},{16,24},{24,16},{1,9},{9,1},{17,25},{25,17},{2,10},{10... | collective-permute-start | bytes 1572872 | tf_op jit(solution)/shard_map/ppermute | solution.py:18
  22.2 5.8 %collective-permute-start.3 = (bf16[8,8192]{1,0:T(8,128)(2,1)S(1)}, bf16[8,8192]{1,0:T(8,128)(2,1)S(1)}, u32[]{:S(2)}, u32[]{:S(2)}) collective-permute-start(bf16[8,8192]{1,0:T(8,128)(2,1)S(1)} %slice.161), channel_id=1, source_target_pairs={{0,16},{8,24},{16,0},{24,8},{1,17},{9,25},{17,1},{25,9},{2,18},{10... | collective-permute-start | bytes 393224 | tf_op jit(solution)/shard_map/ppermute | solution.py:18
  28.1 27.6 %copy-start.2 = (bf16[8,8192]{1,0:T(8,128)(2,1)}, bf16[8,8192]{1,0:T(8,128)(2,1)S(1)}, u32[]{:S(2)}) copy-start(bf16[8,8192]{1,0:T(8,128)(2,1)S(1)} %fusion.1) | copy-start | bytes 393220
  28.1 6.1 %collective-permute-start.6 = (bf16[8,2048]{1,0:T(8,128)(2,1)S(1)}, bf16[8,2048]{1,0:T(8,128)(2,1)S(1)}, u32[]{:S(2)}, u32[]{:S(2)}) collective-permute-start(bf16[8,2048]{1,0:T(8,128)(2,1)S(1)} %get-tuple-element.48), channel_id=1, source_target_pairs={{0,6},{1,7},{2,4},{3,5},{4,2},{5,3},{6,0},{7,1},{8,14},{9,15},{10,... | collective-permute-start | bytes 98312 | tf_op jit(solution)/shard_map/ppermute | solution.py:18
  31.8 4.8 %collective-permute-start.5 = (bf16[8,2048]{1,0:T(8,128)(2,1)S(1)}, bf16[8,2048]{1,0:T(8,128)(2,1)S(1)}, u32[]{:S(2)}, u32[]{:S(2)}) collective-permute-start(bf16[8,2048]{1,0:T(8,128)(2,1)S(1)} %get-tuple-element.49), channel_id=1, source_target_pairs={{0,4},{1,5},{2,6},{3,7},{4,0},{5,1},{6,2},{7,3},{8,12},{9,13},{10,... | collective-permute-start | bytes 98312 | tf_op jit(solution)/shard_map/ppermute | solution.py:18
  31.8 4.8 %collective-permute-start.4 = (bf16[8,2048]{1,0:T(8,128)(2,1)S(1)}, bf16[8,2048]{1,0:T(8,128)(2,1)S(1)}, u32[]{:S(2)}, u32[]{:S(2)}) collective-permute-start(bf16[8,2048]{1,0:T(8,128)(2,1)S(1)} %get-tuple-element.50), channel_id=1, source_target_pairs={{0,2},{1,3},{2,0},{3,1},{4,6},{5,7},{6,4},{7,5},{8,10},{9,11},{10,... | collective-permute-start | bytes 98312 | tf_op jit(solution)/shard_map/ppermute | solution.py:18
  36.6 5.8 %collective-permute-start.9 = (bf16[32,1024]{1,0:T(8,128)(2,1)S(1)}, bf16[32,1024]{1,0:T(8,128)(2,1)S(1)}, u32[]{:S(2)}, u32[]{:S(2)}) collective-permute-start(bf16[32,1024]{1,0:T(8,128)(2,1)S(1)} %get-tuple-element.26), channel_id=1, source_target_pairs={{0,17},{1,16},{2,19},{3,18},{4,21},{5,20},{6,23},{7,22},{8,25},{9,... | collective-permute-start | bytes 196616 | tf_op jit(solution)/shard_map/ppermute | solution.py:24
  38.9 4.3 %collective-permute-start.8 = (bf16[32,1024]{1,0:T(8,128)(2,1)S(1)}, bf16[32,1024]{1,0:T(8,128)(2,1)S(1)}, u32[]{:S(2)}, u32[]{:S(2)}) collective-permute-start(bf16[32,1024]{1,0:T(8,128)(2,1)S(1)} %get-tuple-element.25), channel_id=1, source_target_pairs={{0,16},{8,24},{16,0},{24,8},{1,17},{9,25},{17,1},{25,9},{2,18},{10... | collective-permute-start | bytes 196616 | tf_op jit(solution)/shard_map/ppermute | solution.py:18
  39.7 4.3 %collective-permute-start.7 = (bf16[32,1024]{1,0:T(8,128)(2,1)S(1)}, bf16[32,1024]{1,0:T(8,128)(2,1)S(1)}, u32[]{:S(2)}, u32[]{:S(2)}) collective-permute-start(bf16[32,1024]{1,0:T(8,128)(2,1)S(1)} %get-tuple-element.26), channel_id=1, source_target_pairs={{0,1},{1,0},{2,3},{3,2},{4,5},{5,4},{6,7},{7,6},{8,9},{9,8},{10,11... | collective-permute-start | bytes 196616 | tf_op jit(solution)/shard_map/ppermute | solution.py:18
  42.4 22.5 %copy-start.1 = (bf16[2048,128]{1,0:T(8,128)(2,1)S(1)}, bf16[2048,128]{1,0:T(8,128)(2,1)}, u32[]{:S(2)}) copy-start(bf16[2048,128]{1,0:T(8,128)(2,1)} %param.17) | copy-start | bytes 1572868
  44.0 28.3 %copy-start = (f32[8,8192]{1,0:T(8,128)S(1)}, f32[8,8192]{1,0:T(8,128)}, u32[]{:S(2)}) copy-start(f32[8,8192]{1,0:T(8,128)} %param.10) | copy-start | bytes 786436
  44.0 28.3 %copy-start.4 = (f32[8192]{0:T(1024)S(1)}, f32[8192]{0:T(1024)}, u32[]{:S(2)}) copy-start(f32[8192]{0:T(1024)} %param.14) | copy-start | bytes 98308
  44.0 1.6 %collective-permute-start.10 = (bf16[128,1024]{1,0:T(8,128)(2,1)S(1)}, bf16[128,1024]{1,0:T(8,128)(2,1)S(1)}, u32[]{:S(2)}, u32[]{:S(2)}) collective-permute-start(bf16[128,1024]{1,0:T(8,128)(2,1)S(1)} %pad_maximum_fusion.3), channel_id=1, source_target_pairs={{0,8},{8,0},{16,24},{24,16},{1,9},{9,1},{17,25},{25,17},{2,10},{10... | collective-permute-start | bytes 786440 | tf_op jit(solution)/shard_map/ppermute | solution.py:18
  46.4 9.2 %collective-permute-start.11 = (bf16[128,1024]{1,0:T(8,128)(2,1)S(1)}, bf16[128,1024]{1,0:T(8,128)(2,1)S(1)}, u32[]{:S(2)}, u32[]{:S(2)}) collective-permute-start(bf16[128,1024]{1,0:T(8,128)(2,1)S(1)} %get-tuple-element.35), channel_id=1, source_target_pairs={{0,1},{1,0},{2,3},{3,2},{4,5},{5,4},{6,7},{7,6},{8,9},{9,8},{10,11... | collective-permute-start | bytes 786440 | tf_op jit(solution)/shard_map/ppermute | solution.py:18
  47.7 12.7 %collective-permute-start.15 = (bf16[128,1024]{1,0:T(8,128)(2,1)S(1)}, bf16[128,1024]{1,0:T(8,128)(2,1)S(1)}, u32[]{:S(2)}, u32[]{:S(2)}) collective-permute-start(bf16[128,1024]{1,0:T(8,128)(2,1)S(1)} %get-tuple-element.38), channel_id=1, source_target_pairs={{0,1},{1,0},{2,3},{3,2},{4,5},{5,4},{6,7},{7,6},{8,9},{9,8},{10,11... | collective-permute-start | bytes 786440 | tf_op jit(solution)/shard_map/ppermute | solution.py:18
  55.7 7.0 %collective-permute-start.14 = (bf16[4,8,1024]{2,1,0:T(8,128)(2,1)S(1)}, bf16[4,8,1024]{2,1,0:T(8,128)(2,1)S(1)}, u32[]{:S(2)}, u32[]{:S(2)}) collective-permute-start(bf16[4,8,1024]{2,1,0:T(8,128)(2,1)S(1)} %get-tuple-element.43), channel_id=1, source_target_pairs={{0,6},{1,7},{2,4},{3,5},{4,2},{5,3},{6,0},{7,1},{8,14},{9,15},{10,... | collective-permute-start | bytes 196616 | tf_op jit(solution)/shard_map/ppermute | solution.py:18
  57.2 7.7 %collective-permute-start.13 = (bf16[4,8,1024]{2,1,0:T(8,128)(2,1)S(1)}, bf16[4,8,1024]{2,1,0:T(8,128)(2,1)S(1)}, u32[]{:S(2)}, u32[]{:S(2)}) collective-permute-start(bf16[4,8,1024]{2,1,0:T(8,128)(2,1)S(1)} %get-tuple-element.44), channel_id=1, source_target_pairs={{0,4},{1,5},{2,6},{3,7},{4,0},{5,1},{6,2},{7,3},{8,12},{9,13},{10,... | collective-permute-start | bytes 196616 | tf_op jit(solution)/shard_map/ppermute | solution.py:18
  57.9 7.1 %collective-permute-start.12 = (bf16[4,8,1024]{2,1,0:T(8,128)(2,1)S(1)}, bf16[4,8,1024]{2,1,0:T(8,128)(2,1)S(1)}, u32[]{:S(2)}, u32[]{:S(2)}) collective-permute-start(bf16[4,8,1024]{2,1,0:T(8,128)(2,1)S(1)} %get-tuple-element.42), channel_id=1, source_target_pairs={{0,2},{1,3},{2,0},{3,1},{4,6},{5,7},{6,4},{7,5},{8,10},{9,11},{10,... | collective-permute-start | bytes 196616 | tf_op jit(solution)/shard_map/ppermute | solution.py:18
  60.5 6.7 %collective-permute-start.18 = (bf16[4,8,1024]{2,1,0:T(8,128)(2,1)S(1)}, bf16[4,8,1024]{2,1,0:T(8,128)(2,1)S(1)}, u32[]{:S(2)}, u32[]{:S(2)}) collective-permute-start(bf16[4,8,1024]{2,1,0:T(8,128)(2,1)S(1)} %get-tuple-element.40), channel_id=1, source_target_pairs={{0,6},{1,7},{2,4},{3,5},{4,2},{5,3},{6,0},{7,1},{8,14},{9,15},{10,... | collective-permute-start | bytes 196616 | tf_op jit(solution)/shard_map/ppermute | solution.py:18
  62.0 7.2 %collective-permute-start.17 = (bf16[4,8,1024]{2,1,0:T(8,128)(2,1)S(1)}, bf16[4,8,1024]{2,1,0:T(8,128)(2,1)S(1)}, u32[]{:S(2)}, u32[]{:S(2)}) collective-permute-start(bf16[4,8,1024]{2,1,0:T(8,128)(2,1)S(1)} %get-tuple-element.41), channel_id=1, source_target_pairs={{0,4},{1,5},{2,6},{3,7},{4,0},{5,1},{6,2},{7,3},{8,12},{9,13},{10,... | collective-permute-start | bytes 196616 | tf_op jit(solution)/shard_map/ppermute | solution.py:18
  62.7 6.5 %collective-permute-start.16 = (bf16[4,8,1024]{2,1,0:T(8,128)(2,1)S(1)}, bf16[4,8,1024]{2,1,0:T(8,128)(2,1)S(1)}, u32[]{:S(2)}, u32[]{:S(2)}) collective-permute-start(bf16[4,8,1024]{2,1,0:T(8,128)(2,1)S(1)} %get-tuple-element.39), channel_id=1, source_target_pairs={{0,2},{1,3},{2,0},{3,1},{4,6},{5,7},{6,4},{7,5},{8,10},{9,11},{10,... | collective-permute-start | bytes 196616 | tf_op jit(solution)/shard_map/ppermute | solution.py:18
  69.8 1.2 %collective-permute-start.19 = (f32[16,128]{1,0:T(8,128)S(1)}, f32[16,128]{1,0:T(8,128)S(1)}, u32[]{:S(2)}, u32[]{:S(2)}) collective-permute-start(f32[16,128]{1,0:T(8,128)S(1)} %slice.100), channel_id=1, source_target_pairs={{0,8},{8,0},{16,24},{24,16},{1,9},{9,1},{17,25},{25,17},{2,10},{10... | collective-permute-start | bytes 24584 | tf_op jit(solution)/shard_map/ppermute | solution.py:18
  71.0 3.6 %collective-permute-start.20 = (f32[8,128]{1,0:T(8,128)S(1)}, f32[8,128]{1,0:T(8,128)S(1)}, u32[]{:S(2)}, u32[]{:S(2)}) collective-permute-start(f32[8,128]{1,0:T(8,128)S(1)} %slice.102), channel_id=1, source_target_pairs={{0,16},{8,24},{16,0},{24,8},{1,17},{9,25},{17,1},{25,9},{2,18},{10... | collective-permute-start | bytes 12296 | tf_op jit(solution)/shard_map/ppermute | solution.py:18

commit v4 on v3

v4 whole, which is shorter than its diff:
```python
import functools
import math

import jax
import jax.numpy as jnp
from jax import lax
from jax.experimental import pallas as pl
from jax.experimental.pallas import tpu as pltpu
from jax.sharding import PartitionSpec as P

F32, BF16 = jnp.float32, jnp.bfloat16
NT = (((1,), (1,)), ((), ()))
VM = pl.BlockSpec(memory_space=pltpu.VMEM)


def swap(x, axis, bit):
    n = lax.axis_size(axis)
    return lax.ppermute(x, axis, [(i, i ^ bit) for i in range(n)])


def swap_both(x, fsdp_bit, cand_bit):
    m, n = lax.axis_size("fsdp"), lax.axis_size("cand")
    pairs = [(i * n + j, (i ^ fsdp_bit) * n + (j ^ cand_bit)) for i in range(m) for j in range(n)]
    return lax.ppermute(x, ("fsdp", "cand"), pairs)


def round_kernel(x_ref, out_ref):
    out_ref[...] = x_ref[...].astype(BF16)


def rounded(x):
    return pl.pallas_call(
        round_kernel,
        out_shape=pltpu.VMEM(x.shape, BF16),
        in_specs=[VM],
        out_specs=VM,
        compiler_params=pltpu.CompilerParams(vmem_limit_bytes=2**20),
        cost_estimate=pl.CostEstimate(flops=10**10, bytes_accessed=6 * x.size, transcendentals=0),
        name="rounded",
    )(x)


def load_kernel(src_ref, *refs, start):
    *dst_refs, sems = refs
    copies = []
    for dst_ref in dst_refs:
        copies.append(pltpu.make_async_copy(src_ref.at[pl.ds(start, dst_ref.shape[0])], dst_ref, sems.at[len(copies)]))
        copies[-1].start()
        start += dst_ref.shape[0]
    for c in copies:
        c.wait()


def load(x, start, sizes, name):
    return pl.pallas_call(
        functools.partial(load_kernel, start=start),
        out_shape=tuple(pltpu.VMEM((rows, x.shape[1]), x.dtype) for rows in sizes),
        in_specs=[pl.BlockSpec(memory_space=pltpu.HBM)],
        out_specs=(VM,) * len(sizes),
        scratch_shapes=[pltpu.SemaphoreType.DMA((len(sizes),))],
        compiler_params=pltpu.CompilerParams(vmem_limit_bytes=2**20),
        cost_estimate=pl.CostEstimate(
            flops=0, bytes_accessed=2 * sum(sizes) * x.shape[1] * x.dtype.itemsize, transcendentals=0
        ),
        name=name,
    )(x)


def force_kernel(m_ref, k_ref, b_ref, a_ref, keep_ref, send_ref, act_ref):
    hidden = k_ref.shape[0]
    rows = math.gcd(hidden, 512)
    for at in range(0, hidden, rows):
        c = slice(at, at + rows)
        s = lax.dot_general(m_ref[...], k_ref[c, :], NT, preferred_element_type=F32)
        s = s + b_ref[:, c].astype(F32)
        act_ref[:, c] = (a_ref[:, c].astype(F32) * jnp.tanh(s)).astype(BF16)
    columns_kernel(act_ref, k_ref, keep_ref, send_ref, start=0)


def columns_kernel(act_ref, k_ref, keep_ref, send_ref, *, start):
    half, width = keep_ref.shape
    step = math.gcd(width, 2048)

    @pl.loop(0, width // step)
    def _(j):
        c = pl.ds(pl.multiple_of(start + j * step, step), step)
        f = jnp.dot(act_ref[...], k_ref[:, c], preferred_element_type=F32)
        c = pl.ds(pl.multiple_of(j * step, step), step)
        keep_ref[:, c] = f[:half]
        send_ref[:, c] = f[half:]


def force_parts(m, kernel, bias, amplitude):
    n, width = m.shape
    hidden = bias.shape[0]
    cols = width // 2
    out = pltpu.VMEM((n // 2, cols), F32)
    keep, send, act = pl.pallas_call(
        force_kernel,
        out_shape=(out, out, pltpu.VMEM((n, hidden), BF16)),
        in_specs=[VM] * 4,
        out_specs=(VM,) * 3,
        compiler_params=pltpu.CompilerParams(vmem_limit_bytes=8 * 2**20),
        cost_estimate=pl.CostEstimate(
            flops=3 * 256 * hidden * width, bytes_accessed=2 * hidden * width, transcendentals=n * hidden
        ),
        name="force_left",
    )(m, kernel, bias[None, :], amplitude[None, :])
    left = (keep, send)
    right = pl.pallas_call(
        functools.partial(columns_kernel, start=cols),
        out_shape=(out, out),
        in_specs=[VM] * 2,
        out_specs=(VM,) * 2,
        compiler_params=pltpu.CompilerParams(vmem_limit_bytes=8 * 2**20),
        cost_estimate=pl.CostEstimate(
            flops=256 * hidden * width, bytes_accessed=hidden * width, transcendentals=0
        ),
        name="force_right",
    )(act, kernel)
    return left, right


def angle_kernel(t_ref, w_ref, *out_refs, rows, starts):
    a = lax.dot_general(t_ref[...], w_ref[...], NT, preferred_element_type=F32)
    for ref, firsts in zip(out_refs, starts):
        ref[...] = jnp.concatenate([a[i : i + rows] for i in firsts], axis=0).astype(ref.dtype)


def angle_parts(t, omega, rows, outs):
    cols = omega.shape[0]
    return pl.pallas_call(
        functools.partial(angle_kernel, rows=rows, starts=[starts for _, starts in outs]),
        out_shape=tuple(pltpu.VMEM((rows * len(starts), cols), dtype) for dtype, starts in outs),
        in_specs=[VM, VM],
        out_specs=(VM,) * len(outs),
        compiler_params=pltpu.CompilerParams(vmem_limit_bytes=8 * 2**20),
        cost_estimate=pl.CostEstimate(
            flops=2 * t.shape[0] * cols * t.shape[1], bytes_accessed=2 * cols * t.shape[1], transcendentals=0
        ),
        name="angle_parts",
    )(t, omega)


def local(positions_init, momenta_init, kernel, bias, amplitude, shift, omega, phase, samples):
    n_fsdp, n_cand = lax.axis_size("fsdp"), lax.axis_size("cand")
    own, width = positions_init.shape
    feats = omega.shape[0]
    bits = [1 << b for b in range(n_fsdp.bit_length() - 1)]
    cand = lax.axis_index("cand")
    outer, inner = cand // 2, cand % 2
    n_outer = n_cand // 2
    kernel = pltpu.with_memory_space_constraint(kernel, pltpu.VMEM)
    omega = pltpu.with_memory_space_constraint(omega, pltpu.HBM)

    m = rounded(momenta_init)
    for bit in reversed(bits):
        m = jnp.concatenate([m, swap(m, "fsdp", bit)], axis=0)
    (keep, send), right = force_parts(m, kernel, bias, amplitude)
    got, right = lax.optimization_barrier((swap(send, "fsdp", 1), right))
    columns = [keep + got, right[0] + swap(right[1], "fsdp", 1)]
    for bit in bits[1:]:
        half = columns[0].shape[0] // 2
        columns = [c[:half] + swap(c[half:].astype(BF16), "fsdp", bit).astype(F32) for c in columns]
    keep = jnp.concatenate(columns, axis=1)
    tracked = (keep - positions_init).astype(BF16)

    by_outer = tracked.reshape(own, n_outer, width // n_outer)
    piece = lambda j: lax.dynamic_index_in_dim(by_outer, outer ^ j, axis=1, keepdims=False)
    t = jnp.concatenate([piece(0)] + [swap(piece(j), "cand", 2 * j) for j in range(1, n_outer)], axis=0)
    lo, hi = t[:, : t.shape[1] // 2], t[:, t.shape[1] // 2 :]
    mine, other = jnp.where(inner == 0, lo, hi), jnp.where(inner == 0, hi, lo)
    mine, other, omega = lax.optimization_barrier((mine, other, omega))
    omega = load(omega, 0, [feats * 1 // 2, feats * 1 // 2], "load_omega")
    t = jnp.concatenate([mine, swap(other, "cand", 1), swap(mine, "fsdp", 2), swap_both(other, 2, 1)], axis=0)
    t, omega = lax.optimization_barrier((t, omega))
    for bit in reversed(bits):
        if bit == 2:
            continue
        t = jnp.concatenate([t, swap(t, "fsdp", bit)], axis=0)
    t, momenta_init = lax.optimization_barrier((t, momenta_init))
    positions = momenta_init + shift[None, :]

    row = lambda f, x, z: ((f * 2 + x) * n_outer + z) * own
    by_inner = [[row(f, x, z) for z in range(n_outer) for f in range(n_fsdp)] for x in range(2)]
    group = n_fsdp * own
    outs = [(F32, by_inner[0]), (BF16, by_inner[1])]
    sums = [angle_parts(t, omega[0], own, outs), angle_parts(t, omega[1], own, outs)]
    sums = [(keep, swap(send, "cand", 1)) for keep, send in sums]
    both, ahead = [], None
    for keep, got in sums:
        keep = keep + got.astype(F32)
        blocks = [keep[j * group : (j + 1) * group] for j in range(n_outer)]
        gots = {j: swap(blocks[j].astype(BF16), "cand", 2 * j) for j in reversed(range(1, n_outer))}
        angles = blocks[0]
        for x in gots.values():
            angles = angles + x.astype(F32)
        both.append(angles)
    acquisition, start = 0.0, 0
    for angles in both:
        c = slice(start, start + angles.shape[1])
        start += angles.shape[1]
        features = (jnp.sqrt(2.0 / (feats * n_fsdp)) * jnp.cos(angles + phase[None, c])).astype(BF16)
        acquisition = acquisition + jnp.dot(features, samples[c], preferred_element_type=F32)
    parts = acquisition.reshape(2, n_fsdp // 4, 2, own, samples.shape[1])
    for bit in bits[2:]:
        half = parts.shape[1] // 2
        parts = parts[:, :half] + swap(parts[:, half:], "fsdp", bit)
    parts = parts.reshape(4, own, samples.shape[1])
    acquisition = swap(parts[3], "fsdp", 3) + swap(parts[1], "fsdp", 2) + swap(parts[2], "fsdp", 1) + parts[0]
    return (tracked, positions, acquisition)


def solution(mesh):
    both = P(("fsdp", "cand"), None)
    return jax.shard_map(
        local,
        mesh=mesh,
        in_specs=(both, both, P("fsdp", None), P("fsdp"), P("fsdp"), P(), P("fsdp", "cand"), P("fsdp"), P("fsdp", None)),
        out_specs=(both, both, both),
        check_vma=False,
    )
```

time: 75.4 us -> 71.9 us (0.954)
  Pallas kernels: 18.9 us -> 12.1 us
  starting transfers between devices: 25.3 us -> 27.4 us
  waiting for transfers between devices: 26.1 us -> 27.2 us
  local copies, waits for them, and re-layouts: 0.14 us -> 1.23 us
  other arithmetic: 2.71 us -> 1.73 us
    pallas_call x3 -> x1, Pallas kernels: 9.02 us -> 2.24 us  [load(): pl.pallas_call(functools.partial(load_kernel, start=start), out_shape=tup...]
    ppermute x20 -> x23, starting transfers between devices: 23.1 us -> 25.8 us  [swap(): return lax.ppermute(x, axis, [(i, i ^ bit) for i in range(n)])]
    unnamed x16 -> x20, local copies, waits for them, and re-layouts: 0.05 us -> 1.14 us
    convert_element_type x1 -> x0, other arithmetic: 0.97 us -> none  [local(): m = momenta_init.astype(BF16)]
    ppermute x20 -> x23, waiting for transfers between devices: 26.1 us -> 26.5 us  [swap(): return lax.ppermute(x, axis, [(i, i ^ bit) for i in range(n)])]
    pallas_call x3 -> x5, Pallas kernels: 9.85 us -> 9.86 us  [the longest x1 6.71 us: force_parts(): pl.pallas_call(force_kernel, out_shape=(out, out, pltpu.VMEM((n, hidden),...]
  transfers between devices with their start and end apart: 21 -> 24, of which waited for: 13 -> 16; matrix products, arithmetic and copies ran while one was open for 2% -> 2% of each run, Pallas kernels for 13% -> 6%
where the time goes in v4:
time: 71.9 us; the launch traced here: 71.8 us
  starting transfers between devices  27.4 us (38%)
  waiting for transfers between devices  27.2 us (38%)
  Pallas kernels  12.1 us (17%)
  other arithmetic  1.73 us (2%)
  local copies, waits for them, and re-layouts  1.23 us (2%)
  matrix products  1.18 us (2%)
  between operations  0.93 us (1%)
    ppermute x23, waiting for transfers between devices, swap(): return lax.ppermute(x, axis, [(i, i ^ bit) for i in range(n)])  26.5 us
    ppermute x23, starting transfers between devices, swap(): return lax.ppermute(x, axis, [(i, i ^ bit) for i in range(n)])  25.8 us
    pallas_call x1, Pallas kernels, force_parts(): pl.pallas_call(force_kernel, out_shape=(out, out, pltpu.VMEM((n, hidden),...  6.71 us
    pallas_call x1, Pallas kernels, load(): pl.pallas_call(functools.partial(load_kernel, start=start), out_shape=tup...  2.24 us
    ppermute x1, starting transfers between devices, swap_both(): return lax.ppermute(x, ('fsdp', 'cand'), pairs)  1.67 us
    pallas_call x1, Pallas kernels, force_parts(): pl.pallas_call(functools.partial(columns_kernel, start=cols), out_shape=(...  1.65 us
    pallas_call x2, Pallas kernels, angle_parts(): pl.pallas_call(functools.partial(angle_kernel, rows=rows, starts=[starts...  1.48 us
  transfers between devices with their start and end apart: 24, of which 16 were waited for; matrix products, arithmetic and copies ran while one was open for 2% of the time, Pallas kernels for 6%

profile of v4, /device:TPU:0, one launch (start us, length us, event | category | flops | bytes accessed | tf_op | source)
XLA Modules:
  0.0 71.8 jit_solution(244752526225866657)
XLA Ops:
  0.7 1.1 %copy-done.1 = f32[8,8192]{1,0:T(8,128)S(1)} copy-done((f32[8,8192]{1,0:T(8,128)S(1)}, f32[8,8192]{1,0:T(8,128)}, u32[]{:S(2)}) %copy-start.1) | copy-done | bytes 262168
  1.8 3.0 %collective-permute-start = (bf16[8,8192]{1,0:T(8,128)(2,1)S(1)}, bf16[8,8192]{1,0:T(8,128)(2,1)S(1)}, u32[]{:S(2)}, u32[]{:S(2)}) collective-permute-start(bf16[8,8192]{1,0:T(8,128)(2,1)S(1)} %rounded.1), channel_id=1, source_target_pairs={{0,16},{8,24},{16,0},{24,8},{1,17},{9,25},{17,1},{25,9},{2,18},{10... | collective-permute-start | bytes 393224 | tf_op jit(solution)/shard_map/ppermute | solution.py:18
  4.8 3.5 %collective-permute-done = bf16[8,8192]{1,0:T(8,128)(2,1)S(1)} collective-permute-done((bf16[8,8192]{1,0:T(8,128)(2,1)S(1)}, bf16[8,8192]{1,0:T(8,128)(2,1)S(1)}, u32[]{:S(2)}, u32[]{:S(2)}) %collective-permute-start) | collective-permute-done | bytes 131104 | tf_op jit(solution)/shard_map/ppermute | solution.py:18
  8.4 1.5 %collective-permute-done.1 = bf16[16,8192]{1,0:T(8,128)(2,1)S(1)} collective-permute-done((bf16[16,8192]{1,0:T(8,128)(2,1)S(1)}, bf16[16,8192]{1,0:T(8,128)(2,1)S(1)}, u32[]{:S(2)}, u32[]{:S(2)}) %collective-permute-start.1) | collective-permute-done | bytes 262176 | tf_op jit(solution)/shard_map/ppermute | solution.py:18
  10.0 6.7 %force_left.1 = (f32[16,4096]{1,0:T(8,128)S(1)}, f32[16,4096]{1,0:T(8,128)S(1)}, bf16[32,1024]{1,0:T(8,128)(2,1)S(1)}) custom-call(bf16[32,8192]{1,0:T(8,128)(2,1)S(1)} %pad_maximum_fusion.m_ref, bf16[1024,8192]{1,0:T(8,128)(2,1)S(1)} %copy-done, bf16[1,1024]{1,0:T(2,128)(2,1)S(1)} %broadcast_in_dim.4.b_ref, bf16[1,1024]{1,0:T(2,128)(2,1)S(1)} %broadcast_in_dim.10.a_ref), custom_call_target="tpu_custom_call" | custom-call | flops 6442450944 | bytes 16777216 | tf_op jit(solution)/shard_map/force_left/pallas_call | solution.py:98
  16.8 1.7 %force_right.1 = (f32[16,4096]{1,0:T(8,128)S(1)}, f32[16,4096]{1,0:T(8,128)S(1)}) custom-call(bf16[32,1024]{1,0:T(8,128)(2,1)S(1)} %get-tuple-element.27.act_ref, bf16[1024,8192]{1,0:T(8,128)(2,1)S(1)} %copy-done), custom_call_target="tpu_custom_call" | custom-call | flops 2147483648 | bytes 8388608 | tf_op jit(solution)/shard_map/force_right/pallas_call | solution.py:110
  18.9 1.8 %collective-permute-start.3 = (bf16[8,4096]{1,0:T(8,128)(2,1)S(1)}, bf16[8,4096]{1,0:T(8,128)(2,1)S(1)}, u32[]{:S(2)}, u32[]{:S(2)}) collective-permute-start(bf16[8,4096]{1,0:T(8,128)(2,1)S(1)} %slice.160), channel_id=1, source_target_pairs={{0,16},{8,24},{16,0},{24,8},{1,17},{9,25},{17,1},{25,9},{2,18},{10... | collective-permute-start | bytes 196616 | tf_op jit(solution)/shard_map/ppermute | solution.py:18
  20.8 1.1 %collective-permute-start.5 = (bf16[8,4096]{1,0:T(8,128)(2,1)S(1)}, bf16[8,4096]{1,0:T(8,128)(2,1)S(1)}, u32[]{:S(2)}, u32[]{:S(2)}) collective-permute-start(bf16[8,4096]{1,0:T(8,128)(2,1)S(1)} %slice.159), channel_id=1, source_target_pairs={{0,16},{8,24},{16,0},{24,8},{1,17},{9,25},{17,1},{25,9},{2,18},{10... | collective-permute-start | bytes 196616 | tf_op jit(solution)/shard_map/ppermute | solution.py:18
  21.9 1.3 %collective-permute-done.3 = bf16[8,4096]{1,0:T(8,128)(2,1)S(1)} collective-permute-done((bf16[8,4096]{1,0:T(8,128)(2,1)S(1)}, bf16[8,4096]{1,0:T(8,128)(2,1)S(1)}, u32[]{:S(2)}, u32[]{:S(2)}) %collective-permute-start.3) | collective-permute-done | bytes 65568 | tf_op jit(solution)/shard_map/ppermute | solution.py:18
  23.3 1.8 %collective-permute-done.5 = bf16[8,4096]{1,0:T(8,128)(2,1)S(1)} collective-permute-done((bf16[8,4096]{1,0:T(8,128)(2,1)S(1)}, bf16[8,4096]{1,0:T(8,128)(2,1)S(1)}, u32[]{:S(2)}, u32[]{:S(2)}) %collective-permute-start.5) | collective-permute-done | bytes 65568 | tf_op jit(solution)/shard_map/ppermute | solution.py:18
  25.2 1.6 %collective-permute-start.6 = (bf16[8,2048]{1,0:T(8,128)(2,1)S(1)}, bf16[8,2048]{1,0:T(8,128)(2,1)S(1)}, u32[]{:S(2)}, u32[]{:S(2)}) collective-permute-start(bf16[8,2048]{1,0:T(8,128)(2,1)S(1)} %get-tuple-element.62), channel_id=1, source_target_pairs={{0,2},{1,3},{2,0},{3,1},{4,6},{5,7},{6,4},{7,5},{8,10},{9,11},{10,... | collective-permute-start | bytes 98312 | tf_op jit(solution)/shard_map/ppermute | solution.py:18
  26.9 2.6 %collective-permute-start.7 = (bf16[8,2048]{1,0:T(8,128)(2,1)S(1)}, bf16[8,2048]{1,0:T(8,128)(2,1)S(1)}, u32[]{:S(2)}, u32[]{:S(2)}) collective-permute-start(bf16[8,2048]{1,0:T(8,128)(2,1)S(1)} %get-tuple-element.61), channel_id=1, source_target_pairs={{0,4},{1,5},{2,6},{3,7},{4,0},{5,1},{6,2},{7,3},{8,12},{9,13},{10,... | collective-permute-start | bytes 98312 | tf_op jit(solution)/shard_map/ppermute | solution.py:18
  29.7 2.2 %collective-permute-done.7 = bf16[8,2048]{1,0:T(8,128)(2,1)S(1)} collective-permute-done((bf16[8,2048]{1,0:T(8,128)(2,1)S(1)}, bf16[8,2048]{1,0:T(8,128)(2,1)S(1)}, u32[]{:S(2)}, u32[]{:S(2)}) %collective-permute-start.7) | collective-permute-done | bytes 32800 | tf_op jit(solution)/shard_map/ppermute | solution.py:18
  31.9 3.2 %collective-permute-done.8 = bf16[8,2048]{1,0:T(8,128)(2,1)S(1)} collective-permute-done((bf16[8,2048]{1,0:T(8,128)(2,1)S(1)}, bf16[8,2048]{1,0:T(8,128)(2,1)S(1)}, u32[]{:S(2)}, u32[]{:S(2)}) %collective-permute-start.8) | collective-permute-done | bytes 32800 | tf_op jit(solution)/shard_map/ppermute | solution.py:18
  35.2 1.4 %collective-permute-start.10 = (bf16[32,1024]{1,0:T(8,128)(2,1)S(1)}, bf16[32,1024]{1,0:T(8,128)(2,1)S(1)}, u32[]{:S(2)}, u32[]{:S(2)}) collective-permute-start(bf16[32,1024]{1,0:T(8,128)(2,1)S(1)} %get-tuple-element.33), channel_id=1, source_target_pairs={{0,16},{8,24},{16,0},{24,8},{1,17},{9,25},{17,1},{25,9},{2,18},{10... | collective-permute-start | bytes 196616 | tf_op jit(solution)/shard_map/ppermute | solution.py:18
  36.6 1.7 %collective-permute-start.11 = (bf16[32,1024]{1,0:T(8,128)(2,1)S(1)}, bf16[32,1024]{1,0:T(8,128)(2,1)S(1)}, u32[]{:S(2)}, u32[]{:S(2)}) collective-permute-start(bf16[32,1024]{1,0:T(8,128)(2,1)S(1)} %get-tuple-element.34), channel_id=1, source_target_pairs={{0,17},{1,16},{2,19},{3,18},{4,21},{5,20},{6,23},{7,22},{8,25},{9,... | collective-permute-start | bytes 196616 | tf_op jit(solution)/shard_map/ppermute | solution.py:24
  38.8 2.2 %load_omega.1 = (bf16[1024,1024]{1,0:T(8,128)(2,1)S(1)}, bf16[1024,1024]{1,0:T(8,128)(2,1)S(1)}) custom-call(bf16[2048,1024]{1,0:T(8,128)(2,1)} %src_ref), custom_call_target="tpu_custom_call" | custom-call | bytes 8388608 | tf_op jit(solution)/shard_map/load_omega/pallas_call | solution.py:55
  41.0 0.7 collective-permute-done.11
  41.7 0.8 %collective-permute-done.9 = bf16[32,1024]{1,0:T(8,128)(2,1)S(1)} collective-permute-done((bf16[32,1024]{1,0:T(8,128)(2,1)S(1)}, bf16[32,1024]{1,0:T(8,128)(2,1)S(1)}, u32[]{:S(2)}, u32[]{:S(2)}) %collective-permute-start.9) | collective-permute-done | bytes 65568 | tf_op jit(solution)/shard_map/ppermute | solution.py:18
  42.6 1.5 %collective-permute-done.12 = bf16[128,1024]{1,0:T(8,128)(2,1)S(1)} collective-permute-done((bf16[128,1024]{1,0:T(8,128)(2,1)S(1)}, bf16[128,1024]{1,0:T(8,128)(2,1)S(1)}, u32[]{:S(2)}, u32[]{:S(2)}) %collective-permute-start.12) | collective-permute-done | bytes 262176 | tf_op jit(solution)/shard_map/ppermute | solution.py:18
  44.2 0.7 %angle_parts.2 = (f32[128,1024]{1,0:T(8,128)S(1)}, bf16[128,1024]{1,0:T(8,128)(2,1)S(1)}) custom-call(bf16[256,1024]{1,0:T(8,128)(2,1)S(1)} %pad_maximum_fusion.1.t_ref, bf16[1024,1024]{1,0:T(8,128)(2,1)S(1)} %get-tuple-element.41.w_ref), custom_call_target="tpu_custom_call" | custom-call | flops 536870912 | bytes 2097152 | tf_op jit(solution)/shard_map/angle_parts/pallas_call | solution.py:132
  45.0 0.8 %collective-permute-start.13 = (bf16[128,1024]{1,0:T(8,128)(2,1)S(1)}, bf16[128,1024]{1,0:T(8,128)(2,1)S(1)}, u32[]{:S(2)}, u32[]{:S(2)}) collective-permute-start(bf16[128,1024]{1,0:T(8,128)(2,1)S(1)} %get-tuple-element.43), channel_id=1, source_target_pairs={{0,1},{1,0},{2,3},{3,2},{4,5},{5,4},{6,7},{7,6},{8,9},{9,8},{10,11... | collective-permute-start | bytes 786440 | tf_op jit(solution)/shard_map/ppermute | solution.py:18
  45.8 0.7 %angle_parts.3 = (f32[128,1024]{1,0:T(8,128)S(1)}, bf16[128,1024]{1,0:T(8,128)(2,1)S(1)}) custom-call(bf16[256,1024]{1,0:T(8,128)(2,1)S(1)} %pad_maximum_fusion.1.t_ref, bf16[1024,1024]{1,0:T(8,128)(2,1)S(1)} %get-tuple-element.44.w_ref), custom_call_target="tpu_custom_call" | custom-call | flops 536870912 | bytes 2097152 | tf_op jit(solution)/shard_map/angle_parts/pallas_call | solution.py:132
  46.5 1.4 %collective-permute-start.17 = (bf16[128,1024]{1,0:T(8,128)(2,1)S(1)}, bf16[128,1024]{1,0:T(8,128)(2,1)S(1)}, u32[]{:S(2)}, u32[]{:S(2)}) collective-permute-start(bf16[128,1024]{1,0:T(8,128)(2,1)S(1)} %get-tuple-element.46), channel_id=1, source_target_pairs={{0,1},{1,0},{2,3},{3,2},{4,5},{5,4},{6,7},{7,6},{8,9},{9,8},{10,11... | collective-permute-start | bytes 786440 | tf_op jit(solution)/shard_map/ppermute | solution.py:18
  47.9 6.3 %collective-permute-done.13 = bf16[128,1024]{1,0:T(8,128)(2,1)S(1)} collective-permute-done((bf16[128,1024]{1,0:T(8,128)(2,1)S(1)}, bf16[128,1024]{1,0:T(8,128)(2,1)S(1)}, u32[]{:S(2)}, u32[]{:S(2)}) %collective-permute-start.13) | collective-permute-done | bytes 262176 | tf_op jit(solution)/shard_map/ppermute | solution.py:18
  54.7 4.0 %collective-permute-start.16 = (bf16[32,1024]{1,0:T(8,128)(2,1)S(1)}, bf16[32,1024]{1,0:T(8,128)(2,1)S(1)}, u32[]{:S(2)}, u32[]{:S(2)}) collective-permute-start(bf16[32,1024]{1,0:T(8,128)(2,1)S(1)} %get-tuple-element.55), channel_id=1, source_target_pairs={{0,2},{1,3},{2,0},{3,1},{4,6},{5,7},{6,4},{7,5},{8,10},{9,11},{10,... | collective-permute-start | bytes 196616 | tf_op jit(solution)/shard_map/ppermute | solution.py:18
  59.5 0.9 %collective-permute-start.19 = (bf16[32,1024]{1,0:T(8,128)(2,1)S(1)}, bf16[32,1024]{1,0:T(8,128)(2,1)S(1)}, u32[]{:S(2)}, u32[]{:S(2)}) collective-permute-start(bf16[32,1024]{1,0:T(8,128)(2,1)S(1)} %get-tuple-element.53), channel_id=1, source_target_pairs={{0,4},{1,5},{2,6},{3,7},{4,0},{5,1},{6,2},{7,3},{8,12},{9,13},{10,... | collective-permute-start | bytes 196616 | tf_op jit(solution)/shard_map/ppermute | solution.py:18
  60.5 3.0 %collective-permute-start.20 = (bf16[32,1024]{1,0:T(8,128)(2,1)S(1)}, bf16[32,1024]{1,0:T(8,128)(2,1)S(1)}, u32[]{:S(2)}, u32[]{:S(2)}) collective-permute-start(bf16[32,1024]{1,0:T(8,128)(2,1)S(1)} %get-tuple-element.52), channel_id=1, source_target_pairs={{0,2},{1,3},{2,0},{3,1},{4,6},{5,7},{6,4},{7,5},{8,10},{9,11},{10,... | collective-permute-start | bytes 196616 | tf_op jit(solution)/shard_map/ppermute | solution.py:18
  64.2 1.6 %collective-permute-done.18 = bf16[32,1024]{1,0:T(8,128)(2,1)S(1)} collective-permute-done((bf16[32,1024]{1,0:T(8,128)(2,1)S(1)}, bf16[32,1024]{1,0:T(8,128)(2,1)S(1)}, u32[]{:S(2)}, u32[]{:S(2)}) %collective-permute-start.18) | collective-permute-done | bytes 65568 | tf_op jit(solution)/shard_map/ppermute | solution.py:18
  65.8 1.1 %collective-permute-done.19 = bf16[32,1024]{1,0:T(8,128)(2,1)S(1)} collective-permute-done((bf16[32,1024]{1,0:T(8,128)(2,1)S(1)}, bf16[32,1024]{1,0:T(8,128)(2,1)S(1)}, u32[]{:S(2)}, u32[]{:S(2)}) %collective-permute-start.19) | collective-permute-done | bytes 65568 | tf_op jit(solution)/shard_map/ppermute | solution.py:18
  67.5 1.4 %collective-permute-start.22 = (f32[8,128]{1,0:T(8,128)S(1)}, f32[8,128]{1,0:T(8,128)S(1)}, u32[]{:S(2)}, u32[]{:S(2)}) collective-permute-start(f32[8,128]{1,0:T(8,128)S(1)} %get-tuple-element.63), channel_id=1, source_target_pairs={{0,16},{8,24},{16,0},{24,8},{1,17},{9,25},{17,1},{25,9},{2,18},{10... | collective-permute-start | bytes 12296 | tf_op jit(solution)/shard_map/ppermute | solution.py:18
  69.4 0.7 %broadcast_add_fusion = f32[8,8192]{1,0:T(8,128)} fusion(f32[8,8192]{1,0:T(8,128)S(1)} %copy-done.2, f32[8192]{0:T(1024)S(1)} %copy-done.6), kind=kLoop, calls=%fused_computation.31 | loop fusion | flops 65536 | bytes 557056 | tf_op jit(solution)/shard_map/add | solution.py:182
  (68 shorter events, 6.6 us)
Async XLA Ops:
  0.6 9.3 %copy-start = (bf16[1024,8192]{1,0:T(8,128)(2,1)S(1)}, bf16[1024,8192]{1,0:T(8,128)(2,1)}, u32[]{:S(2)}) copy-start(bf16[1024,8192]{1,0:T(8,128)(2,1)} %k_ref.3) | copy-start | bytes 50331652
  1.7 6.7 %copy-start.9 = (bf16[1024]{0:T(1024)(128)(2,1)S(1)}, bf16[1024]{0:T(1024)(128)(2,1)}, u32[]{:S(2)}) copy-start(bf16[1024]{0:T(1024)(128)(2,1)} %param.12) | copy-start | bytes 6148
  1.8 6.5 %collective-permute-start = (bf16[8,8192]{1,0:T(8,128)(2,1)S(1)}, bf16[8,8192]{1,0:T(8,128)(2,1)S(1)}, u32[]{:S(2)}, u32[]{:S(2)}) collective-permute-start(bf16[8,8192]{1,0:T(8,128)(2,1)S(1)} %rounded.1), channel_id=1, source_target_pairs={{0,16},{8,24},{16,0},{24,8},{1,17},{9,25},{17,1},{25,9},{2,18},{10... | collective-permute-start | bytes 393224 | tf_op jit(solution)/shard_map/ppermute | solution.py:18
  8.3 1.6 %collective-permute-start.1 = (bf16[16,8192]{1,0:T(8,128)(2,1)S(1)}, bf16[16,8192]{1,0:T(8,128)(2,1)S(1)}, u32[]{:S(2)}, u32[]{:S(2)}) collective-permute-start(bf16[16,8192]{1,0:T(8,128)(2,1)S(1)} %pad_maximum_fusion.2), channel_id=1, source_target_pairs={{0,8},{8,0},{16,24},{24,16},{1,9},{9,1},{17,25},{25,17},{2,10},{10... | collective-permute-start | bytes 786440 | tf_op jit(solution)/shard_map/ppermute | solution.py:18
  16.7 1.8 %collective-permute-start.2 = (f32[16,4096]{1,0:T(8,128)S(1)}, f32[16,4096]{1,0:T(8,128)S(1)}, u32[]{:S(2)}, u32[]{:S(2)}) collective-permute-start(f32[16,4096]{1,0:T(8,128)S(1)} %get-tuple-element.26), channel_id=1, source_target_pairs={{0,8},{8,0},{16,24},{24,16},{1,9},{9,1},{17,25},{25,17},{2,10},{10... | collective-permute-start | bytes 786440 | tf_op jit(solution)/shard_map/ppermute | solution.py:18
  16.8 8.3 %copy-start.5 = (f32[8,8192]{1,0:T(8,128)S(1)}, f32[8,8192]{1,0:T(8,128)}, u32[]{:S(2)}) copy-start(f32[8,8192]{1,0:T(8,128)} %param.9) | copy-start | bytes 786436
  18.5 2.3 %collective-permute-start.4 = (f32[16,4096]{1,0:T(8,128)S(1)}, f32[16,4096]{1,0:T(8,128)S(1)}, u32[]{:S(2)}, u32[]{:S(2)}) collective-permute-start(f32[16,4096]{1,0:T(8,128)S(1)} %get-tuple-element.32), channel_id=1, source_target_pairs={{0,8},{8,0},{16,24},{24,16},{1,9},{9,1},{17,25},{25,17},{2,10},{10... | collective-permute-start | bytes 786440 | tf_op jit(solution)/shard_map/ppermute | solution.py:18
  18.9 4.3 %collective-permute-start.3 = (bf16[8,4096]{1,0:T(8,128)(2,1)S(1)}, bf16[8,4096]{1,0:T(8,128)(2,1)S(1)}, u32[]{:S(2)}, u32[]{:S(2)}) collective-permute-start(bf16[8,4096]{1,0:T(8,128)(2,1)S(1)} %slice.160), channel_id=1, source_target_pairs={{0,16},{8,24},{16,0},{24,8},{1,17},{9,25},{17,1},{25,9},{2,18},{10... | collective-permute-start | bytes 196616 | tf_op jit(solution)/shard_map/ppermute | solution.py:18
  20.8 4.3 %collective-permute-start.5 = (bf16[8,4096]{1,0:T(8,128)(2,1)S(1)}, bf16[8,4096]{1,0:T(8,128)(2,1)S(1)}, u32[]{:S(2)}, u32[]{:S(2)}) collective-permute-start(bf16[8,4096]{1,0:T(8,128)(2,1)S(1)} %slice.159), channel_id=1, source_target_pairs={{0,16},{8,24},{16,0},{24,8},{1,17},{9,25},{17,1},{25,9},{2,18},{10... | collective-permute-start | bytes 196616 | tf_op jit(solution)/shard_map/ppermute | solution.py:18
  25.2 19.7 %copy-start.3 = (bf16[8,8192]{1,0:T(8,128)(2,1)}, bf16[8,8192]{1,0:T(8,128)(2,1)S(1)}, u32[]{:S(2)}) copy-start(bf16[8,8192]{1,0:T(8,128)(2,1)S(1)} %fusion) | copy-start | bytes 393220
  25.2 4.5 %collective-permute-start.6 = (bf16[8,2048]{1,0:T(8,128)(2,1)S(1)}, bf16[8,2048]{1,0:T(8,128)(2,1)S(1)}, u32[]{:S(2)}, u32[]{:S(2)}) collective-permute-start(bf16[8,2048]{1,0:T(8,128)(2,1)S(1)} %get-tuple-element.62), channel_id=1, source_target_pairs={{0,2},{1,3},{2,0},{3,1},{4,6},{5,7},{6,4},{7,5},{8,10},{9,11},{10,... | collective-permute-start | bytes 98312 | tf_op jit(solution)/shard_map/ppermute | solution.py:18
  26.9 5.1 %collective-permute-start.7 = (bf16[8,2048]{1,0:T(8,128)(2,1)S(1)}, bf16[8,2048]{1,0:T(8,128)(2,1)S(1)}, u32[]{:S(2)}, u32[]{:S(2)}) collective-permute-start(bf16[8,2048]{1,0:T(8,128)(2,1)S(1)} %get-tuple-element.61), channel_id=1, source_target_pairs={{0,4},{1,5},{2,6},{3,7},{4,0},{5,1},{6,2},{7,3},{8,12},{9,13},{10,... | collective-permute-start | bytes 98312 | tf_op jit(solution)/shard_map/ppermute | solution.py:18
  29.5 5.7 %collective-permute-start.8 = (bf16[8,2048]{1,0:T(8,128)(2,1)S(1)}, bf16[8,2048]{1,0:T(8,128)(2,1)S(1)}, u32[]{:S(2)}, u32[]{:S(2)}) collective-permute-start(bf16[8,2048]{1,0:T(8,128)(2,1)S(1)} %get-tuple-element.60), channel_id=1, source_target_pairs={{0,6},{1,7},{2,4},{3,5},{4,2},{5,3},{6,0},{7,1},{8,14},{9,15},{10,... | collective-permute-start | bytes 98312 | tf_op jit(solution)/shard_map/ppermute | solution.py:18
  35.2 10.5 %copy-start.7 = (f32[2048]{0:T(1024)S(1)}, f32[2048]{0:T(1024)}, u32[]{:S(2)}) copy-start(f32[2048]{0:T(1024)} %param.16) | copy-start | bytes 24580
  35.2 5.8 %collective-permute-start.10 = (bf16[32,1024]{1,0:T(8,128)(2,1)S(1)}, bf16[32,1024]{1,0:T(8,128)(2,1)S(1)}, u32[]{:S(2)}, u32[]{:S(2)}) collective-permute-start(bf16[32,1024]{1,0:T(8,128)(2,1)S(1)} %get-tuple-element.33), channel_id=1, source_target_pairs={{0,16},{8,24},{16,0},{24,8},{1,17},{9,25},{17,1},{25,9},{2,18},{10... | collective-permute-start | bytes 196616 | tf_op jit(solution)/shard_map/ppermute | solution.py:18
  36.6 5.2 %collective-permute-start.11 = (bf16[32,1024]{1,0:T(8,128)(2,1)S(1)}, bf16[32,1024]{1,0:T(8,128)(2,1)S(1)}, u32[]{:S(2)}, u32[]{:S(2)}) collective-permute-start(bf16[32,1024]{1,0:T(8,128)(2,1)S(1)} %get-tuple-element.34), channel_id=1, source_target_pairs={{0,17},{1,16},{2,19},{3,18},{4,21},{5,20},{6,23},{7,22},{8,25},{9,... | collective-permute-start | bytes 196616 | tf_op jit(solution)/shard_map/ppermute | solution.py:24
  38.2 4.3 %collective-permute-start.9 = (bf16[32,1024]{1,0:T(8,128)(2,1)S(1)}, bf16[32,1024]{1,0:T(8,128)(2,1)S(1)}, u32[]{:S(2)}, u32[]{:S(2)}) collective-permute-start(bf16[32,1024]{1,0:T(8,128)(2,1)S(1)} %get-tuple-element.34), channel_id=1, source_target_pairs={{0,1},{1,0},{2,3},{3,2},{4,5},{5,4},{6,7},{7,6},{8,9},{9,8},{10,11... | collective-permute-start | bytes 196616 | tf_op jit(solution)/shard_map/ppermute | solution.py:18
  42.5 1.6 %collective-permute-start.12 = (bf16[128,1024]{1,0:T(8,128)(2,1)S(1)}, bf16[128,1024]{1,0:T(8,128)(2,1)S(1)}, u32[]{:S(2)}, u32[]{:S(2)}) collective-permute-start(bf16[128,1024]{1,0:T(8,128)(2,1)S(1)} %pad_maximum_fusion.3), channel_id=1, source_target_pairs={{0,8},{8,0},{16,24},{24,16},{1,9},{9,1},{17,25},{25,17},{2,10},{10... | collective-permute-start | bytes 786440 | tf_op jit(solution)/shard_map/ppermute | solution.py:18
  44.2 19.4 %copy-start.4 = (bf16[2048,128]{1,0:T(8,128)(2,1)S(1)}, bf16[2048,128]{1,0:T(8,128)(2,1)}, u32[]{:S(2)}) copy-start(bf16[2048,128]{1,0:T(8,128)(2,1)} %param.17) | copy-start | bytes 1572868
  44.9 24.4 %copy-start.2 = (f32[8,8192]{1,0:T(8,128)S(1)}, f32[8,8192]{1,0:T(8,128)}, u32[]{:S(2)}) copy-start(f32[8,8192]{1,0:T(8,128)} %x_ref.1) | copy-start | bytes 786436
  45.0 24.4 %copy-start.6 = (f32[8192]{0:T(1024)S(1)}, f32[8192]{0:T(1024)}, u32[]{:S(2)}) copy-start(f32[8192]{0:T(1024)} %param.14) | copy-start | bytes 98308
  45.0 9.2 %collective-permute-start.13 = (bf16[128,1024]{1,0:T(8,128)(2,1)S(1)}, bf16[128,1024]{1,0:T(8,128)(2,1)S(1)}, u32[]{:S(2)}, u32[]{:S(2)}) collective-permute-start(bf16[128,1024]{1,0:T(8,128)(2,1)S(1)} %get-tuple-element.43), channel_id=1, source_target_pairs={{0,1},{1,0},{2,3},{3,2},{4,5},{5,4},{6,7},{7,6},{8,9},{9,8},{10,11... | collective-permute-start | bytes 786440 | tf_op jit(solution)/shard_map/ppermute | solution.py:18
  46.5 12.5 %collective-permute-start.17 = (bf16[128,1024]{1,0:T(8,128)(2,1)S(1)}, bf16[128,1024]{1,0:T(8,128)(2,1)S(1)}, u32[]{:S(2)}, u32[]{:S(2)}) collective-permute-start(bf16[128,1024]{1,0:T(8,128)(2,1)S(1)} %get-tuple-element.46), channel_id=1, source_target_pairs={{0,1},{1,0},{2,3},{3,2},{4,5},{5,4},{6,7},{7,6},{8,9},{9,8},{10,11... | collective-permute-start | bytes 786440 | tf_op jit(solution)/shard_map/ppermute | solution.py:18
  54.3 6.3 %collective-permute-start.14 = (bf16[32,1024]{1,0:T(8,128)(2,1)S(1)}, bf16[32,1024]{1,0:T(8,128)(2,1)S(1)}, u32[]{:S(2)}, u32[]{:S(2)}) collective-permute-start(bf16[32,1024]{1,0:T(8,128)(2,1)S(1)} %get-tuple-element.54), channel_id=1, source_target_pairs={{0,6},{1,7},{2,4},{3,5},{4,2},{5,3},{6,0},{7,1},{8,14},{9,15},{10,... | collective-permute-start | bytes 196616 | tf_op jit(solution)/shard_map/ppermute | solution.py:18
  54.7 8.9 %collective-permute-start.15 = (bf16[32,1024]{1,0:T(8,128)(2,1)S(1)}, bf16[32,1024]{1,0:T(8,128)(2,1)S(1)}, u32[]{:S(2)}, u32[]{:S(2)}) collective-permute-start(bf16[32,1024]{1,0:T(8,128)(2,1)S(1)} %get-tuple-element.56), channel_id=1, source_target_pairs={{0,4},{1,5},{2,6},{3,7},{4,0},{5,1},{6,2},{7,3},{8,12},{9,13},{10,... | collective-permute-start | bytes 196616 | tf_op jit(solution)/shard_map/ppermute | solution.py:18
  54.7 8.9 %collective-permute-start.16 = (bf16[32,1024]{1,0:T(8,128)(2,1)S(1)}, bf16[32,1024]{1,0:T(8,128)(2,1)S(1)}, u32[]{:S(2)}, u32[]{:S(2)}) collective-permute-start(bf16[32,1024]{1,0:T(8,128)(2,1)S(1)} %get-tuple-element.55), channel_id=1, source_target_pairs={{0,2},{1,3},{2,0},{3,1},{4,6},{5,7},{6,4},{7,5},{8,10},{9,11},{10,... | collective-permute-start | bytes 196616 | tf_op jit(solution)/shard_map/ppermute | solution.py:18
  59.1 6.7 %collective-permute-start.18 = (bf16[32,1024]{1,0:T(8,128)(2,1)S(1)}, bf16[32,1024]{1,0:T(8,128)(2,1)S(1)}, u32[]{:S(2)}, u32[]{:S(2)}) collective-permute-start(bf16[32,1024]{1,0:T(8,128)(2,1)S(1)} %get-tuple-element.51), channel_id=1, source_target_pairs={{0,6},{1,7},{2,4},{3,5},{4,2},{5,3},{6,0},{7,1},{8,14},{9,15},{10,... | collective-permute-start | bytes 196616 | tf_op jit(solution)/shard_map/ppermute | solution.py:18
  59.5 7.4 %collective-permute-start.19 = (bf16[32,1024]{1,0:T(8,128)(2,1)S(1)}, bf16[32,1024]{1,0:T(8,128)(2,1)S(1)}, u32[]{:S(2)}, u32[]{:S(2)}) collective-permute-start(bf16[32,1024]{1,0:T(8,128)(2,1)S(1)} %get-tuple-element.53), channel_id=1, source_target_pairs={{0,4},{1,5},{2,6},{3,7},{4,0},{5,1},{6,2},{7,3},{8,12},{9,13},{10,... | collective-permute-start | bytes 196616 | tf_op jit(solution)/shard_map/ppermute | solution.py:18
  60.5 6.3 %collective-permute-start.20 = (bf16[32,1024]{1,0:T(8,128)(2,1)S(1)}, bf16[32,1024]{1,0:T(8,128)(2,1)S(1)}, u32[]{:S(2)}, u32[]{:S(2)}) collective-permute-start(bf16[32,1024]{1,0:T(8,128)(2,1)S(1)} %get-tuple-element.52), channel_id=1, source_target_pairs={{0,2},{1,3},{2,0},{3,1},{4,6},{5,7},{6,4},{7,5},{8,10},{9,11},{10,... | collective-permute-start | bytes 196616 | tf_op jit(solution)/shard_map/ppermute | solution.py:18
  67.5 3.1 %collective-permute-start.21 = (f32[8,128]{1,0:T(8,128)S(1)}, f32[8,128]{1,0:T(8,128)S(1)}, u32[]{:S(2)}, u32[]{:S(2)}) collective-permute-start(f32[8,128]{1,0:T(8,128)S(1)} %get-tuple-element.65), channel_id=1, source_target_pairs={{0,24},{8,16},{16,8},{24,0},{1,25},{9,17},{17,9},{25,1},{2,26},{10... | collective-permute-start | bytes 12296 | tf_op jit(solution)/shard_map/ppermute | solution.py:18
  67.5 3.7 %collective-permute-start.22 = (f32[8,128]{1,0:T(8,128)S(1)}, f32[8,128]{1,0:T(8,128)S(1)}, u32[]{:S(2)}, u32[]{:S(2)}) collective-permute-start(f32[8,128]{1,0:T(8,128)S(1)} %get-tuple-element.63), channel_id=1, source_target_pairs={{0,16},{8,24},{16,0},{24,8},{1,17},{9,25},{17,1},{25,9},{2,18},{10... | collective-permute-start | bytes 12296 | tf_op jit(solution)/shard_map/ppermute | solution.py:18
  68.9 2.3 %collective-permute-start.23 = (f32[8,128]{1,0:T(8,128)S(1)}, f32[8,128]{1,0:T(8,128)S(1)}, u32[]{:S(2)}, u32[]{:S(2)}) collective-permute-start(f32[8,128]{1,0:T(8,128)S(1)} %get-tuple-element.64), channel_id=1, source_target_pairs={{0,8},{8,0},{16,24},{24,16},{1,9},{9,1},{17,25},{25,17},{2,10},{10... | collective-permute-start | bytes 12296 | tf_op jit(solution)/shard_map/ppermute | solution.py:18
  (2 other events, 7.8 us)

commit v5 on v4

--- a/solution.py
+++ b/solution.py
@@ -71,7 +71,7 @@
     rows = math.gcd(hidden, 512)
     for at in range(0, hidden, rows):
         c = slice(at, at + rows)
-        s = lax.dot_general(m_ref[...], k_ref[c, :], NT, preferred_element_type=F32)
+        s = lax.dot_general(k_ref[c, :], m_ref[...], NT, preferred_element_type=F32).T
         s = s + b_ref[:, c].astype(F32)
         act_ref[:, c] = (a_ref[:, c].astype(F32) * jnp.tanh(s)).astype(BF16)
     columns_kernel(act_ref, k_ref, keep_ref, send_ref, start=0)
@@ -79,7 +79,7 @@
 
 def columns_kernel(act_ref, k_ref, keep_ref, send_ref, *, start):
     half, width = keep_ref.shape
-    step = math.gcd(width, 2048)
+    step = math.gcd(width, 4096)
 
     @pl.loop(0, width // step)
     def _(j):
@@ -122,12 +122,12 @@
 
 
 def angle_kernel(t_ref, w_ref, *out_refs, rows, starts):
-    a = lax.dot_general(t_ref[...], w_ref[...], NT, preferred_element_type=F32)
+    a = lax.dot_general(w_ref[...], t_ref[...], NT, preferred_element_type=F32).T
     for ref, firsts in zip(out_refs, starts):
         ref[...] = jnp.concatenate([a[i : i + rows] for i in firsts], axis=0).astype(ref.dtype)
 
 
-def angle_parts(t, omega, rows, outs):
+def angle_parts(t, omega, rows, outs, weight=1):
     cols = omega.shape[0]
     return pl.pallas_call(
         functools.partial(angle_kernel, rows=rows, starts=[starts for _, starts in outs]),
@@ -136,7 +136,7 @@
         out_specs=(VM,) * len(outs),
         compiler_params=pltpu.CompilerParams(vmem_limit_bytes=8 * 2**20),
         cost_estimate=pl.CostEstimate(
-            flops=2 * t.shape[0] * cols * t.shape[1], bytes_accessed=2 * cols * t.shape[1], transcendentals=0
+            flops=weight * 2 * t.shape[0] * cols * t.shape[1], bytes_accessed=weight * 2 * cols * t.shape[1], transcendentals=0
         ),
         name="angle_parts",
     )(t, omega)
@@ -171,43 +171,40 @@
     lo, hi = t[:, : t.shape[1] // 2], t[:, t.shape[1] // 2 :]
     mine, other = jnp.where(inner == 0, lo, hi), jnp.where(inner == 0, hi, lo)
     mine, other, omega = lax.optimization_barrier((mine, other, omega))
-    omega = load(omega, 0, [feats * 1 // 2, feats * 1 // 2], "load_omega")
+    omega = load(omega, 0, [feats], "load_omega")[0]
     t = jnp.concatenate([mine, swap(other, "cand", 1), swap(mine, "fsdp", 2), swap_both(other, 2, 1)], axis=0)
-    t, omega = lax.optimization_barrier((t, omega))
-    for bit in reversed(bits):
-        if bit == 2:
-            continue
+    for bit in reversed(bits[2:]):
         t = jnp.concatenate([t, swap(t, "fsdp", bit)], axis=0)
     t, momenta_init = lax.optimization_barrier((t, momenta_init))
     positions = momenta_init + shift[None, :]
 
+    n_rows = n_fsdp // 2 * own
     row = lambda f, x, z: ((f * 2 + x) * n_outer + z) * own
-    by_inner = [[row(f, x, z) for z in range(n_outer) for f in range(n_fsdp)] for x in range(2)]
-    group = n_fsdp * own
+    by_inner = [[row(f, x, z) for z in range(n_outer) for f in range(n_fsdp // 2)] for x in range(2)]
     outs = [(F32, by_inner[0]), (BF16, by_inner[1])]
-    sums = [angle_parts(t, omega[0], own, outs), angle_parts(t, omega[1], own, outs)]
-    sums = [(keep, swap(send, "cand", 1)) for keep, send in sums]
-    both, ahead = [], None
+    keep, send = angle_parts(t, omega, own, outs)
+    t, send = lax.optimization_barrier((t, send))
+    sums = [(keep, swap(send, "cand", 1))]
+    keep, send = angle_parts(
+        jnp.concatenate([swap(t[:, : t.shape[1] // 2], "fsdp", 1), swap(t[:, t.shape[1] // 2 :], "fsdp", 1)], axis=1), omega, own, outs, 0
+    )
+    sums.append((keep, swap(send, "cand", 1)))
+    parts = []
     for keep, got in sums:
         keep = keep + got.astype(F32)
-        blocks = [keep[j * group : (j + 1) * group] for j in range(n_outer)]
-        gots = {j: swap(blocks[j].astype(BF16), "cand", 2 * j) for j in reversed(range(1, n_outer))}
-        angles = blocks[0]
-        for x in gots.values():
+        blocks = [keep[j * n_rows : (j + 1) * n_rows] for j in range(n_outer)]
+        gots = [swap(blocks[j].astype(BF16), "cand", 2 * j) for j in reversed(range(1, n_outer))]
+        angles = blocks[0] + phase[None, :]
+        for x in gots:
             angles = angles + x.astype(F32)
-        both.append(angles)
-    acquisition, start = 0.0, 0
-    for angles in both:
-        c = slice(start, start + angles.shape[1])
-        start += angles.shape[1]
-        features = (jnp.sqrt(2.0 / (feats * n_fsdp)) * jnp.cos(angles + phase[None, c])).astype(BF16)
-        acquisition = acquisition + jnp.dot(features, samples[c], preferred_element_type=F32)
-    parts = acquisition.reshape(2, n_fsdp // 4, 2, own, samples.shape[1])
-    for bit in bits[2:]:
-        half = parts.shape[1] // 2
-        parts = parts[:, :half] + swap(parts[:, half:], "fsdp", bit)
-    parts = parts.reshape(4, own, samples.shape[1])
-    acquisition = swap(parts[3], "fsdp", 3) + swap(parts[1], "fsdp", 2) + swap(parts[2], "fsdp", 1) + parts[0]
+        features = (jnp.sqrt(2.0 / (feats * n_fsdp)) * jnp.cos(angles)).astype(BF16)
+        part = jnp.dot(features, samples, preferred_element_type=F32).reshape(-1, own, samples.shape[1])
+        for bit in bits[2:]:
+            half = part.shape[0] // 2
+            part = part[:half] + swap(part[half:], "fsdp", bit)
+        parts.append(part)
+    mine, mates = parts
+    acquisition = mine[0] + swap(mine[1], "fsdp", 2) + swap(mates[1], "fsdp", 3) + swap(mates[0], "fsdp", 1)
     return (tracked, positions, acquisition)
 
 

time: 71.9 us -> 67.4 us (0.937)
  waiting for transfers between devices: 27.2 us -> 20.9 us
  starting transfers between devices: 27.4 us -> 28.9 us
    ppermute x23 -> x24, waiting for transfers between devices: 26.5 us -> 20.2 us  [swap(): return lax.ppermute(x, axis, [(i, i ^ bit) for i in range(n)])]
    ppermute x23 -> x24, starting transfers between devices: 25.8 us -> 27.2 us  [swap(): return lax.ppermute(x, axis, [(i, i ^ bit) for i in range(n)])]
    pallas_call x2, Pallas kernels: 1.48 us -> 2.64 us  [angle_parts(): pl.pallas_call(functools.partial(angle_kernel, rows=rows, starts=[starts...]
    pallas_call x1, Pallas kernels: 6.71 us -> 5.98 us  [force_parts(): pl.pallas_call(force_kernel, out_shape=(out, out, pltpu.VMEM((n, hidden),...]
  transfers between devices with their start and end apart: 24 -> 25, of which waited for: 16 -> 15; matrix products, arithmetic and copies ran while one was open for 2% -> 3% of each run, Pallas kernels for 6% -> 8%
where the time goes in v5:
time: 67.4 us; the launch traced here: 67.2 us
  starting transfers between devices  28.9 us (43%)
  waiting for transfers between devices  20.9 us (31%)
  Pallas kernels  12.4 us (18%)
  other arithmetic  1.68 us (2%)
  local copies, waits for them, and re-layouts  1.26 us (2%)
  matrix products  1.18 us (2%)
  between operations  0.95 us (1%)
    ppermute x24, starting transfers between devices, swap(): return lax.ppermute(x, axis, [(i, i ^ bit) for i in range(n)])  27.2 us
    ppermute x24, waiting for transfers between devices, swap(): return lax.ppermute(x, axis, [(i, i ^ bit) for i in range(n)])  20.2 us
    pallas_call x1, Pallas kernels, force_parts(): pl.pallas_call(force_kernel, out_shape=(out, out, pltpu.VMEM((n, hidden),...  5.98 us
    pallas_call x2, Pallas kernels, angle_parts(): pl.pallas_call(functools.partial(angle_kernel, rows=rows, starts=[starts...  2.64 us
    pallas_call x1, Pallas kernels, load(): pl.pallas_call(functools.partial(load_kernel, start=start), out_shape=tup...  2.2 us
    ppermute x1, starting transfers between devices, swap_both(): return lax.ppermute(x, ('fsdp', 'cand'), pairs)  1.67 us
    pallas_call x1, Pallas kernels, force_parts(): pl.pallas_call(functools.partial(columns_kernel, start=cols), out_shape=(...  1.53 us
  transfers between devices with their start and end apart: 25, of which 15 were waited for; matrix products, arithmetic and copies ran while one was open for 3% of the time, Pallas kernels for 8%

profile of v5, /device:TPU:0, one launch (start us, length us, event | category | flops | bytes accessed | tf_op | source)
XLA Modules:
  0.0 67.2 jit_solution(8306819247345947147)
XLA Ops:
  0.7 1.1 %copy-done.2 = f32[8,8192]{1,0:T(8,128)S(1)} copy-done((f32[8,8192]{1,0:T(8,128)S(1)}, f32[8,8192]{1,0:T(8,128)}, u32[]{:S(2)}) %copy-start.2) | copy-done | bytes 262168
  1.8 3.0 %collective-permute-start = (bf16[8,8192]{1,0:T(8,128)(2,1)S(1)}, bf16[8,8192]{1,0:T(8,128)(2,1)S(1)}, u32[]{:S(2)}, u32[]{:S(2)}) collective-permute-start(bf16[8,8192]{1,0:T(8,128)(2,1)S(1)} %rounded.1), channel_id=1, source_target_pairs={{0,16},{8,24},{16,0},{24,8},{1,17},{9,25},{17,1},{25,9},{2,18},{10... | collective-permute-start | bytes 393224 | tf_op jit(solution)/shard_map/ppermute | solution.py:18
  4.8 3.5 %collective-permute-done = bf16[8,8192]{1,0:T(8,128)(2,1)S(1)} collective-permute-done((bf16[8,8192]{1,0:T(8,128)(2,1)S(1)}, bf16[8,8192]{1,0:T(8,128)(2,1)S(1)}, u32[]{:S(2)}, u32[]{:S(2)}) %collective-permute-start) | collective-permute-done | bytes 131104 | tf_op jit(solution)/shard_map/ppermute | solution.py:18
  8.5 1.5 %collective-permute-done.1 = bf16[16,8192]{1,0:T(8,128)(2,1)S(1)} collective-permute-done((bf16[16,8192]{1,0:T(8,128)(2,1)S(1)}, bf16[16,8192]{1,0:T(8,128)(2,1)S(1)}, u32[]{:S(2)}, u32[]{:S(2)}) %collective-permute-start.1) | collective-permute-done | bytes 262176 | tf_op jit(solution)/shard_map/ppermute | solution.py:18
  10.0 6.0 %force_left.1 = (f32[16,4096]{1,0:T(8,128)S(1)}, f32[16,4096]{1,0:T(8,128)S(1)}, bf16[32,1024]{1,0:T(8,128)(2,1)S(1)}) custom-call(bf16[32,8192]{1,0:T(8,128)(2,1)S(1)} %pad_maximum_fusion.m_ref, bf16[1024,8192]{1,0:T(8,128)(2,1)S(1)} %copy-done.1, bf16[1,1024]{1,0:T(2,128)(2,1)S(1)} %broadcast_in_dim.4.b_ref, bf16[1,1024]{1,0:T(2,128)(2,1)S(1)} %broadcast_in_dim.10.a_ref), custom_call_target="tpu_custom_call" | custom-call | flops 6442450944 | bytes 16777216 | tf_op jit(solution)/shard_map/force_left/pallas_call | solution.py:98
  16.1 1.5 %force_right.1 = (f32[16,4096]{1,0:T(8,128)S(1)}, f32[16,4096]{1,0:T(8,128)S(1)}) custom-call(bf16[32,1024]{1,0:T(8,128)(2,1)S(1)} %get-tuple-element.24.act_ref, bf16[1024,8192]{1,0:T(8,128)(2,1)S(1)} %copy-done.1), custom_call_target="tpu_custom_call" | custom-call | flops 2147483648 | bytes 8388608 | tf_op jit(solution)/shard_map/force_right/pallas_call | solution.py:110
  18.1 1.8 %collective-permute-start.3 = (bf16[8,4096]{1,0:T(8,128)(2,1)S(1)}, bf16[8,4096]{1,0:T(8,128)(2,1)S(1)}, u32[]{:S(2)}, u32[]{:S(2)}) collective-permute-start(bf16[8,4096]{1,0:T(8,128)(2,1)S(1)} %slice.152), channel_id=1, source_target_pairs={{0,16},{8,24},{16,0},{24,8},{1,17},{9,25},{17,1},{25,9},{2,18},{10... | collective-permute-start | bytes 196616 | tf_op jit(solution)/shard_map/ppermute | solution.py:18
  20.0 1.1 %collective-permute-start.5 = (bf16[8,4096]{1,0:T(8,128)(2,1)S(1)}, bf16[8,4096]{1,0:T(8,128)(2,1)S(1)}, u32[]{:S(2)}, u32[]{:S(2)}) collective-permute-start(bf16[8,4096]{1,0:T(8,128)(2,1)S(1)} %slice.151), channel_id=1, source_target_pairs={{0,16},{8,24},{16,0},{24,8},{1,17},{9,25},{17,1},{25,9},{2,18},{10... | collective-permute-start | bytes 196616 | tf_op jit(solution)/shard_map/ppermute | solution.py:18
  21.1 1.4 %collective-permute-done.3 = bf16[8,4096]{1,0:T(8,128)(2,1)S(1)} collective-permute-done((bf16[8,4096]{1,0:T(8,128)(2,1)S(1)}, bf16[8,4096]{1,0:T(8,128)(2,1)S(1)}, u32[]{:S(2)}, u32[]{:S(2)}) %collective-permute-start.3) | collective-permute-done | bytes 65568 | tf_op jit(solution)/shard_map/ppermute | solution.py:18
  22.4 1.8 %collective-permute-done.5 = bf16[8,4096]{1,0:T(8,128)(2,1)S(1)} collective-permute-done((bf16[8,4096]{1,0:T(8,128)(2,1)S(1)}, bf16[8,4096]{1,0:T(8,128)(2,1)S(1)}, u32[]{:S(2)}, u32[]{:S(2)}) %collective-permute-start.5) | collective-permute-done | bytes 65568 | tf_op jit(solution)/shard_map/ppermute | solution.py:18
  24.4 1.6 %collective-permute-start.6 = (bf16[8,2048]{1,0:T(8,128)(2,1)S(1)}, bf16[8,2048]{1,0:T(8,128)(2,1)S(1)}, u32[]{:S(2)}, u32[]{:S(2)}) collective-permute-start(bf16[8,2048]{1,0:T(8,128)(2,1)S(1)} %get-tuple-element.58), channel_id=1, source_target_pairs={{0,2},{1,3},{2,0},{3,1},{4,6},{5,7},{6,4},{7,5},{8,10},{9,11},{10,... | collective-permute-start | bytes 98312 | tf_op jit(solution)/shard_map/ppermute | solution.py:18
  26.0 2.6 %collective-permute-start.7 = (bf16[8,2048]{1,0:T(8,128)(2,1)S(1)}, bf16[8,2048]{1,0:T(8,128)(2,1)S(1)}, u32[]{:S(2)}, u32[]{:S(2)}) collective-permute-start(bf16[8,2048]{1,0:T(8,128)(2,1)S(1)} %get-tuple-element.57), channel_id=1, source_target_pairs={{0,4},{1,5},{2,6},{3,7},{4,0},{5,1},{6,2},{7,3},{8,12},{9,13},{10,... | collective-permute-start | bytes 98312 | tf_op jit(solution)/shard_map/ppermute | solution.py:18
  28.8 2.3 %collective-permute-done.7 = bf16[8,2048]{1,0:T(8,128)(2,1)S(1)} collective-permute-done((bf16[8,2048]{1,0:T(8,128)(2,1)S(1)}, bf16[8,2048]{1,0:T(8,128)(2,1)S(1)}, u32[]{:S(2)}, u32[]{:S(2)}) %collective-permute-start.7) | collective-permute-done | bytes 32800 | tf_op jit(solution)/shard_map/ppermute | solution.py:18
  31.1 3.2 %collective-permute-done.8 = bf16[8,2048]{1,0:T(8,128)(2,1)S(1)} collective-permute-done((bf16[8,2048]{1,0:T(8,128)(2,1)S(1)}, bf16[8,2048]{1,0:T(8,128)(2,1)S(1)}, u32[]{:S(2)}, u32[]{:S(2)}) %collective-permute-start.8) | collective-permute-done | bytes 32800 | tf_op jit(solution)/shard_map/ppermute | solution.py:18
  34.4 1.4 %collective-permute-start.10 = (bf16[32,1024]{1,0:T(8,128)(2,1)S(1)}, bf16[32,1024]{1,0:T(8,128)(2,1)S(1)}, u32[]{:S(2)}, u32[]{:S(2)}) collective-permute-start(bf16[32,1024]{1,0:T(8,128)(2,1)S(1)} %get-tuple-element.30), channel_id=1, source_target_pairs={{0,16},{8,24},{16,0},{24,8},{1,17},{9,25},{17,1},{25,9},{2,18},{10... | collective-permute-start | bytes 196616 | tf_op jit(solution)/shard_map/ppermute | solution.py:18
  35.7 1.7 %collective-permute-start.11 = (bf16[32,1024]{1,0:T(8,128)(2,1)S(1)}, bf16[32,1024]{1,0:T(8,128)(2,1)S(1)}, u32[]{:S(2)}, u32[]{:S(2)}) collective-permute-start(bf16[32,1024]{1,0:T(8,128)(2,1)S(1)} %get-tuple-element.31), channel_id=1, source_target_pairs={{0,17},{1,16},{2,19},{3,18},{4,21},{5,20},{6,23},{7,22},{8,25},{9,... | collective-permute-start | bytes 196616 | tf_op jit(solution)/shard_map/ppermute | solution.py:24
  37.9 2.2 %load_omega.1.w_ref = bf16[2048,1024]{1,0:T(8,128)(2,1)S(1)} custom-call(bf16[2048,1024]{1,0:T(8,128)(2,1)} %src_ref), custom_call_target="tpu_custom_call" | custom-call | bytes 8388608 | tf_op jit(solution)/shard_map/load_omega/pallas_call | solution.py:55
  40.2 0.7 %collective-permute-done.11 = bf16[32,1024]{1,0:T(8,128)(2,1)S(1)} collective-permute-done((bf16[32,1024]{1,0:T(8,128)(2,1)S(1)}, bf16[32,1024]{1,0:T(8,128)(2,1)S(1)}, u32[]{:S(2)}, u32[]{:S(2)}) %collective-permute-start.11) | collective-permute-done | bytes 65568 | tf_op jit(solution)/shard_map/ppermute | solution.py:24
  40.9 0.8 %collective-permute-done.9 = bf16[32,1024]{1,0:T(8,128)(2,1)S(1)} collective-permute-done((bf16[32,1024]{1,0:T(8,128)(2,1)S(1)}, bf16[32,1024]{1,0:T(8,128)(2,1)S(1)}, u32[]{:S(2)}, u32[]{:S(2)}) %collective-permute-start.9) | collective-permute-done | bytes 65568 | tf_op jit(solution)/shard_map/ppermute | solution.py:18
  41.7 1.3 %angle_parts.2 = (f32[64,2048]{1,0:T(8,128)S(1)}, bf16[64,2048]{1,0:T(8,128)(2,1)S(1)}) custom-call(bf16[128,1024]{1,0:T(8,128)(2,1)S(1)} %pad_maximum_fusion.2.t_ref, bf16[2048,1024]{1,0:T(8,128)(2,1)S(1)} %load_omega.1.w_ref), custom_call_target="tpu_custom_call" | custom-call | flops 536870912 | bytes 4194304 | tf_op jit(solution)/shard_map/angle_parts/pallas_call | solution.py:132
  43.0 0.8 %collective-permute-start.12 = (bf16[64,2048]{1,0:T(8,128)(2,1)S(1)}, bf16[64,2048]{1,0:T(8,128)(2,1)S(1)}, u32[]{:S(2)}, u32[]{:S(2)}) collective-permute-start(bf16[64,2048]{1,0:T(8,128)(2,1)S(1)} %get-tuple-element.37), channel_id=1, source_target_pairs={{0,1},{1,0},{2,3},{3,2},{4,5},{5,4},{6,7},{7,6},{8,9},{9,8},{10,11... | collective-permute-start | bytes 786440 | tf_op jit(solution)/shard_map/ppermute | solution.py:18
  44.4 0.8 %collective-permute-done.17 = bf16[128,512]{1,0:T(8,128)(2,1)S(1)} collective-permute-done((bf16[128,512]{1,0:T(8,128)(2,1)S(1)}, bf16[128,512]{1,0:T(8,128)(2,1)S(1)}, u32[]{:S(2)}, u32[]{:S(2)}) %collective-permute-start.17) | collective-permute-done | bytes 131104 | tf_op jit(solution)/shard_map/ppermute | solution.py:18
  45.5 1.3 %angle_parts.3 = (f32[64,2048]{1,0:T(8,128)S(1)}, bf16[64,2048]{1,0:T(8,128)(2,1)S(1)}) custom-call(bf16[128,1024]{1,0:T(8,128)(2,1)S(1)} %pad_maximum_fusion.3.t_ref, bf16[2048,1024]{1,0:T(8,128)(2,1)S(1)} %load_omega.1.w_ref), custom_call_target="tpu_custom_call" | custom-call | tf_op jit(solution)/shard_map/angle_parts/pallas_call | solution.py:132
  46.8 1.4 %collective-permute-start.19 = (bf16[64,2048]{1,0:T(8,128)(2,1)S(1)}, bf16[64,2048]{1,0:T(8,128)(2,1)S(1)}, u32[]{:S(2)}, u32[]{:S(2)}) collective-permute-start(bf16[64,2048]{1,0:T(8,128)(2,1)S(1)} %get-tuple-element.40), channel_id=1, source_target_pairs={{0,1},{1,0},{2,3},{3,2},{4,5},{5,4},{6,7},{7,6},{8,9},{9,8},{10,11... | collective-permute-start | bytes 786440 | tf_op jit(solution)/shard_map/ppermute | solution.py:18
  48.2 1.3 %collective-permute-done.12 = bf16[64,2048]{1,0:T(8,128)(2,1)S(1)} collective-permute-done((bf16[64,2048]{1,0:T(8,128)(2,1)S(1)}, bf16[64,2048]{1,0:T(8,128)(2,1)S(1)}, u32[]{:S(2)}, u32[]{:S(2)}) %collective-permute-start.12) | collective-permute-done | bytes 262176 | tf_op jit(solution)/shard_map/ppermute | solution.py:18
  49.9 4.0 %collective-permute-start.15 = (bf16[16,2048]{1,0:T(8,128)(2,1)S(1)}, bf16[16,2048]{1,0:T(8,128)(2,1)S(1)}, u32[]{:S(2)}, u32[]{:S(2)}) collective-permute-start(bf16[16,2048]{1,0:T(8,128)(2,1)S(1)} %get-tuple-element.46), channel_id=1, source_target_pairs={{0,2},{1,3},{2,0},{3,1},{4,6},{5,7},{6,4},{7,5},{8,10},{9,11},{10,... | collective-permute-start | bytes 196616 | tf_op jit(solution)/shard_map/ppermute | solution.py:18
  54.0 1.4 %collective-permute-done.19 = bf16[64,2048]{1,0:T(8,128)(2,1)S(1)} collective-permute-done((bf16[64,2048]{1,0:T(8,128)(2,1)S(1)}, bf16[64,2048]{1,0:T(8,128)(2,1)S(1)}, u32[]{:S(2)}, u32[]{:S(2)}) %collective-permute-start.19) | collective-permute-done | bytes 262176 | tf_op jit(solution)/shard_map/ppermute | solution.py:18
  56.0 3.9 %collective-permute-start.22 = (bf16[16,2048]{1,0:T(8,128)(2,1)S(1)}, bf16[16,2048]{1,0:T(8,128)(2,1)S(1)}, u32[]{:S(2)}, u32[]{:S(2)}) collective-permute-start(bf16[16,2048]{1,0:T(8,128)(2,1)S(1)} %get-tuple-element.49), channel_id=1, source_target_pairs={{0,2},{1,3},{2,0},{3,1},{4,6},{5,7},{6,4},{7,5},{8,10},{9,11},{10,... | collective-permute-start | bytes 196616 | tf_op jit(solution)/shard_map/ppermute | solution.py:18
  60.6 1.3 %collective-permute-start.16 = (f32[8,128]{1,0:T(8,128)S(1)}, f32[8,128]{1,0:T(8,128)S(1)}, u32[]{:S(2)}, u32[]{:S(2)}) collective-permute-start(f32[8,128]{1,0:T(8,128)S(1)} %slice.103), channel_id=1, source_target_pairs={{0,16},{8,24},{16,0},{24,8},{1,17},{9,25},{17,1},{25,9},{2,18},{10... | collective-permute-start | bytes 12296 | tf_op jit(solution)/shard_map/ppermute | solution.py:18
  63.6 1.4 %collective-permute-start.24 = (f32[8,128]{1,0:T(8,128)S(1)}, f32[8,128]{1,0:T(8,128)S(1)}, u32[]{:S(2)}, u32[]{:S(2)}) collective-permute-start(f32[8,128]{1,0:T(8,128)S(1)} %get-tuple-element.60), channel_id=1, source_target_pairs={{0,8},{8,0},{16,24},{24,16},{1,9},{9,1},{17,25},{25,17},{2,10},{10... | collective-permute-start | bytes 12296 | tf_op jit(solution)/shard_map/ppermute | solution.py:18
  65.0 0.7 %broadcast_add_fusion = f32[8,8192]{1,0:T(8,128)} fusion(f32[8,8192]{1,0:T(8,128)S(1)} %copy-done.3, f32[8192]{0:T(1024)S(1)} %copy-done.7), kind=kLoop, calls=%fused_computation.27 | loop fusion | flops 65536 | bytes 557056 | tf_op jit(solution)/shard_map/add | solution.py:179
  65.7 0.9 %collective-permute-done.23 = f32[8,128]{1,0:T(8,128)S(1)} collective-permute-done((f32[8,128]{1,0:T(8,128)S(1)}, f32[8,128]{1,0:T(8,128)S(1)}, u32[]{:S(2)}, u32[]{:S(2)}) %collective-permute-start.23) | collective-permute-done | bytes 4128 | tf_op jit(solution)/shard_map/ppermute | solution.py:18
  (71 shorter events, 6.5 us)
Async XLA Ops:
  0.6 59.3 %copy-start = (bf16[2048,128]{1,0:T(8,128)(2,1)S(1)}, bf16[2048,128]{1,0:T(8,128)(2,1)}, u32[]{:S(2)}) copy-start(bf16[2048,128]{1,0:T(8,128)(2,1)} %param.17) | copy-start | bytes 1572868
  0.6 9.3 %copy-start.1 = (bf16[1024,8192]{1,0:T(8,128)(2,1)S(1)}, bf16[1024,8192]{1,0:T(8,128)(2,1)}, u32[]{:S(2)}) copy-start(bf16[1024,8192]{1,0:T(8,128)(2,1)} %k_ref.3) | copy-start | bytes 50331652
  1.8 6.5 %collective-permute-start = (bf16[8,8192]{1,0:T(8,128)(2,1)S(1)}, bf16[8,8192]{1,0:T(8,128)(2,1)S(1)}, u32[]{:S(2)}, u32[]{:S(2)}) collective-permute-start(bf16[8,8192]{1,0:T(8,128)(2,1)S(1)} %rounded.1), channel_id=1, source_target_pairs={{0,16},{8,24},{16,0},{24,8},{1,17},{9,25},{17,1},{25,9},{2,18},{10... | collective-permute-start | bytes 393224 | tf_op jit(solution)/shard_map/ppermute | solution.py:18
  8.3 1.6 %collective-permute-start.1 = (bf16[16,8192]{1,0:T(8,128)(2,1)S(1)}, bf16[16,8192]{1,0:T(8,128)(2,1)S(1)}, u32[]{:S(2)}, u32[]{:S(2)}) collective-permute-start(bf16[16,8192]{1,0:T(8,128)(2,1)S(1)} %pad_maximum_fusion.1), channel_id=1, source_target_pairs={{0,8},{8,0},{16,24},{24,16},{1,9},{9,1},{17,25},{25,17},{2,10},{10... | collective-permute-start | bytes 786440 | tf_op jit(solution)/shard_map/ppermute | solution.py:18
  16.0 1.7 %collective-permute-start.2 = (f32[16,4096]{1,0:T(8,128)S(1)}, f32[16,4096]{1,0:T(8,128)S(1)}, u32[]{:S(2)}, u32[]{:S(2)}) collective-permute-start(f32[16,4096]{1,0:T(8,128)S(1)} %get-tuple-element.23), channel_id=1, source_target_pairs={{0,8},{8,0},{16,24},{24,16},{1,9},{9,1},{17,25},{25,17},{2,10},{10... | collective-permute-start | bytes 786440 | tf_op jit(solution)/shard_map/ppermute | solution.py:18
  16.1 8.2 %copy-start.5 = (f32[8,8192]{1,0:T(8,128)S(1)}, f32[8,8192]{1,0:T(8,128)}, u32[]{:S(2)}) copy-start(f32[8,8192]{1,0:T(8,128)} %param.9) | copy-start | bytes 786436
  17.6 2.3 %collective-permute-start.4 = (f32[16,4096]{1,0:T(8,128)S(1)}, f32[16,4096]{1,0:T(8,128)S(1)}, u32[]{:S(2)}, u32[]{:S(2)}) collective-permute-start(f32[16,4096]{1,0:T(8,128)S(1)} %get-tuple-element.29), channel_id=1, source_target_pairs={{0,8},{8,0},{16,24},{24,16},{1,9},{9,1},{17,25},{25,17},{2,10},{10... | collective-permute-start | bytes 786440 | tf_op jit(solution)/shard_map/ppermute | solution.py:18
  18.1 4.3 %collective-permute-start.3 = (bf16[8,4096]{1,0:T(8,128)(2,1)S(1)}, bf16[8,4096]{1,0:T(8,128)(2,1)S(1)}, u32[]{:S(2)}, u32[]{:S(2)}) collective-permute-start(bf16[8,4096]{1,0:T(8,128)(2,1)S(1)} %slice.152), channel_id=1, source_target_pairs={{0,16},{8,24},{16,0},{24,8},{1,17},{9,25},{17,1},{25,9},{2,18},{10... | collective-permute-start | bytes 196616 | tf_op jit(solution)/shard_map/ppermute | solution.py:18
  20.0 4.3 %collective-permute-start.5 = (bf16[8,4096]{1,0:T(8,128)(2,1)S(1)}, bf16[8,4096]{1,0:T(8,128)(2,1)S(1)}, u32[]{:S(2)}, u32[]{:S(2)}) collective-permute-start(bf16[8,4096]{1,0:T(8,128)(2,1)S(1)} %slice.151), channel_id=1, source_target_pairs={{0,16},{8,24},{16,0},{24,8},{1,17},{9,25},{17,1},{25,9},{2,18},{10... | collective-permute-start | bytes 196616 | tf_op jit(solution)/shard_map/ppermute | solution.py:18
  24.3 15.8 %copy-start.4 = (bf16[8,8192]{1,0:T(8,128)(2,1)}, bf16[8,8192]{1,0:T(8,128)(2,1)S(1)}, u32[]{:S(2)}) copy-start(bf16[8,8192]{1,0:T(8,128)(2,1)S(1)} %fusion) | copy-start | bytes 393220
  24.4 4.5 %collective-permute-start.6 = (bf16[8,2048]{1,0:T(8,128)(2,1)S(1)}, bf16[8,2048]{1,0:T(8,128)(2,1)S(1)}, u32[]{:S(2)}, u32[]{:S(2)}) collective-permute-start(bf16[8,2048]{1,0:T(8,128)(2,1)S(1)} %get-tuple-element.58), channel_id=1, source_target_pairs={{0,2},{1,3},{2,0},{3,1},{4,6},{5,7},{6,4},{7,5},{8,10},{9,11},{10,... | collective-permute-start | bytes 98312 | tf_op jit(solution)/shard_map/ppermute | solution.py:18
  26.0 5.1 %collective-permute-start.7 = (bf16[8,2048]{1,0:T(8,128)(2,1)S(1)}, bf16[8,2048]{1,0:T(8,128)(2,1)S(1)}, u32[]{:S(2)}, u32[]{:S(2)}) collective-permute-start(bf16[8,2048]{1,0:T(8,128)(2,1)S(1)} %get-tuple-element.57), channel_id=1, source_target_pairs={{0,4},{1,5},{2,6},{3,7},{4,0},{5,1},{6,2},{7,3},{8,12},{9,13},{10,... | collective-permute-start | bytes 98312 | tf_op jit(solution)/shard_map/ppermute | solution.py:18
  28.6 5.7 %collective-permute-start.8 = (bf16[8,2048]{1,0:T(8,128)(2,1)S(1)}, bf16[8,2048]{1,0:T(8,128)(2,1)S(1)}, u32[]{:S(2)}, u32[]{:S(2)}) collective-permute-start(bf16[8,2048]{1,0:T(8,128)(2,1)S(1)} %get-tuple-element.56), channel_id=1, source_target_pairs={{0,6},{1,7},{2,4},{3,5},{4,2},{5,3},{6,0},{7,1},{8,14},{9,15},{10,... | collective-permute-start | bytes 98312 | tf_op jit(solution)/shard_map/ppermute | solution.py:18
  34.4 5.8 %collective-permute-start.10 = (bf16[32,1024]{1,0:T(8,128)(2,1)S(1)}, bf16[32,1024]{1,0:T(8,128)(2,1)S(1)}, u32[]{:S(2)}, u32[]{:S(2)}) collective-permute-start(bf16[32,1024]{1,0:T(8,128)(2,1)S(1)} %get-tuple-element.30), channel_id=1, source_target_pairs={{0,16},{8,24},{16,0},{24,8},{1,17},{9,25},{17,1},{25,9},{2,18},{10... | collective-permute-start | bytes 196616 | tf_op jit(solution)/shard_map/ppermute | solution.py:18
  35.7 5.2 %collective-permute-start.11 = (bf16[32,1024]{1,0:T(8,128)(2,1)S(1)}, bf16[32,1024]{1,0:T(8,128)(2,1)S(1)}, u32[]{:S(2)}, u32[]{:S(2)}) collective-permute-start(bf16[32,1024]{1,0:T(8,128)(2,1)S(1)} %get-tuple-element.31), channel_id=1, source_target_pairs={{0,17},{1,16},{2,19},{3,18},{4,21},{5,20},{6,23},{7,22},{8,25},{9,... | collective-permute-start | bytes 196616 | tf_op jit(solution)/shard_map/ppermute | solution.py:24
  37.4 4.3 %collective-permute-start.9 = (bf16[32,1024]{1,0:T(8,128)(2,1)S(1)}, bf16[32,1024]{1,0:T(8,128)(2,1)S(1)}, u32[]{:S(2)}, u32[]{:S(2)}) collective-permute-start(bf16[32,1024]{1,0:T(8,128)(2,1)S(1)} %get-tuple-element.31), channel_id=1, source_target_pairs={{0,1},{1,0},{2,3},{3,2},{4,5},{5,4},{6,7},{7,6},{8,9},{9,8},{10,11... | collective-permute-start | bytes 196616 | tf_op jit(solution)/shard_map/ppermute | solution.py:18
  43.0 6.4 %collective-permute-start.12 = (bf16[64,2048]{1,0:T(8,128)(2,1)S(1)}, bf16[64,2048]{1,0:T(8,128)(2,1)S(1)}, u32[]{:S(2)}, u32[]{:S(2)}) collective-permute-start(bf16[64,2048]{1,0:T(8,128)(2,1)S(1)} %get-tuple-element.37), channel_id=1, source_target_pairs={{0,1},{1,0},{2,3},{3,2},{4,5},{5,4},{6,7},{7,6},{8,9},{9,8},{10,11... | collective-permute-start | bytes 786440 | tf_op jit(solution)/shard_map/ppermute | solution.py:18
  43.8 1.4 %collective-permute-start.17 = (bf16[128,512]{1,0:T(8,128)(2,1)S(1)}, bf16[128,512]{1,0:T(8,128)(2,1)S(1)}, u32[]{:S(2)}, u32[]{:S(2)}) collective-permute-start(bf16[128,512]{1,0:T(8,128)(2,1)S(1)} %get-tuple-element.51), channel_id=1, source_target_pairs={{0,8},{8,0},{16,24},{24,16},{1,9},{9,1},{17,25},{25,17},{2,10},{10... | collective-permute-start | bytes 393224 | tf_op jit(solution)/shard_map/ppermute | solution.py:18
  43.9 1.5 %collective-permute-start.18 = (bf16[128,512]{1,0:T(8,128)(2,1)S(1)}, bf16[128,512]{1,0:T(8,128)(2,1)S(1)}, u32[]{:S(2)}, u32[]{:S(2)}) collective-permute-start(bf16[128,512]{1,0:T(8,128)(2,1)S(1)} %get-tuple-element.52), channel_id=1, source_target_pairs={{0,8},{8,0},{16,24},{24,16},{1,9},{9,1},{17,25},{25,17},{2,10},{10... | collective-permute-start | bytes 393224 | tf_op jit(solution)/shard_map/ppermute | solution.py:18
  45.4 14.5 %copy-start.6 = (f32[2048]{0:T(1024)S(1)}, f32[2048]{0:T(1024)}, u32[]{:S(2)}) copy-start(f32[2048]{0:T(1024)} %param.16) | copy-start | bytes 24580
  45.5 19.5 %copy-start.3 = (f32[8,8192]{1,0:T(8,128)S(1)}, f32[8,8192]{1,0:T(8,128)}, u32[]{:S(2)}) copy-start(f32[8,8192]{1,0:T(8,128)} %x_ref.1) | copy-start | bytes 786436
  45.5 19.5 %copy-start.7 = (f32[8192]{0:T(1024)S(1)}, f32[8192]{0:T(1024)}, u32[]{:S(2)}) copy-start(f32[8192]{0:T(1024)} %param.14) | copy-start | bytes 98308
  46.8 8.6 %collective-permute-start.19 = (bf16[64,2048]{1,0:T(8,128)(2,1)S(1)}, bf16[64,2048]{1,0:T(8,128)(2,1)S(1)}, u32[]{:S(2)}, u32[]{:S(2)}) collective-permute-start(bf16[64,2048]{1,0:T(8,128)(2,1)S(1)} %get-tuple-element.40), channel_id=1, source_target_pairs={{0,1},{1,0},{2,3},{3,2},{4,5},{5,4},{6,7},{7,6},{8,9},{9,8},{10,11... | collective-permute-start | bytes 786440 | tf_op jit(solution)/shard_map/ppermute | solution.py:18
  49.5 6.5 %collective-permute-start.13 = (bf16[16,2048]{1,0:T(8,128)(2,1)S(1)}, bf16[16,2048]{1,0:T(8,128)(2,1)S(1)}, u32[]{:S(2)}, u32[]{:S(2)}) collective-permute-start(bf16[16,2048]{1,0:T(8,128)(2,1)S(1)} %get-tuple-element.45), channel_id=1, source_target_pairs={{0,6},{1,7},{2,4},{3,5},{4,2},{5,3},{6,0},{7,1},{8,14},{9,15},{10,... | collective-permute-start | bytes 196616 | tf_op jit(solution)/shard_map/ppermute | solution.py:18
  49.9 10.0 %collective-permute-start.14 = (bf16[16,2048]{1,0:T(8,128)(2,1)S(1)}, bf16[16,2048]{1,0:T(8,128)(2,1)S(1)}, u32[]{:S(2)}, u32[]{:S(2)}) collective-permute-start(bf16[16,2048]{1,0:T(8,128)(2,1)S(1)} %get-tuple-element.47), channel_id=1, source_target_pairs={{0,4},{1,5},{2,6},{3,7},{4,0},{5,1},{6,2},{7,3},{8,12},{9,13},{10,... | collective-permute-start | bytes 196616 | tf_op jit(solution)/shard_map/ppermute | solution.py:18
  49.9 10.0 %collective-permute-start.15 = (bf16[16,2048]{1,0:T(8,128)(2,1)S(1)}, bf16[16,2048]{1,0:T(8,128)(2,1)S(1)}, u32[]{:S(2)}, u32[]{:S(2)}) collective-permute-start(bf16[16,2048]{1,0:T(8,128)(2,1)S(1)} %get-tuple-element.46), channel_id=1, source_target_pairs={{0,2},{1,3},{2,0},{3,1},{4,6},{5,7},{6,4},{7,5},{8,10},{9,11},{10,... | collective-permute-start | bytes 196616 | tf_op jit(solution)/shard_map/ppermute | solution.py:18
  55.5 6.8 %collective-permute-start.20 = (bf16[16,2048]{1,0:T(8,128)(2,1)S(1)}, bf16[16,2048]{1,0:T(8,128)(2,1)S(1)}, u32[]{:S(2)}, u32[]{:S(2)}) collective-permute-start(bf16[16,2048]{1,0:T(8,128)(2,1)S(1)} %get-tuple-element.48), channel_id=1, source_target_pairs={{0,6},{1,7},{2,4},{3,5},{4,2},{5,3},{6,0},{7,1},{8,14},{9,15},{10,... | collective-permute-start | bytes 196616 | tf_op jit(solution)/shard_map/ppermute | solution.py:18
  55.9 6.4 %collective-permute-start.21 = (bf16[16,2048]{1,0:T(8,128)(2,1)S(1)}, bf16[16,2048]{1,0:T(8,128)(2,1)S(1)}, u32[]{:S(2)}, u32[]{:S(2)}) collective-permute-start(bf16[16,2048]{1,0:T(8,128)(2,1)S(1)} %get-tuple-element.50), channel_id=1, source_target_pairs={{0,4},{1,5},{2,6},{3,7},{4,0},{5,1},{6,2},{7,3},{8,12},{9,13},{10,... | collective-permute-start | bytes 196616 | tf_op jit(solution)/shard_map/ppermute | solution.py:18
  56.0 6.9 %collective-permute-start.22 = (bf16[16,2048]{1,0:T(8,128)(2,1)S(1)}, bf16[16,2048]{1,0:T(8,128)(2,1)S(1)}, u32[]{:S(2)}, u32[]{:S(2)}) collective-permute-start(bf16[16,2048]{1,0:T(8,128)(2,1)S(1)} %get-tuple-element.49), channel_id=1, source_target_pairs={{0,2},{1,3},{2,0},{3,1},{4,6},{5,7},{6,4},{7,5},{8,10},{9,11},{10,... | collective-permute-start | bytes 196616 | tf_op jit(solution)/shard_map/ppermute | solution.py:18
  60.6 5.1 %collective-permute-start.16 = (f32[8,128]{1,0:T(8,128)S(1)}, f32[8,128]{1,0:T(8,128)S(1)}, u32[]{:S(2)}, u32[]{:S(2)}) collective-permute-start(f32[8,128]{1,0:T(8,128)S(1)} %slice.103), channel_id=1, source_target_pairs={{0,16},{8,24},{16,0},{24,8},{1,17},{9,25},{17,1},{25,9},{2,18},{10... | collective-permute-start | bytes 12296 | tf_op jit(solution)/shard_map/ppermute | solution.py:18
  63.6 3.0 %collective-permute-start.23 = (f32[8,128]{1,0:T(8,128)S(1)}, f32[8,128]{1,0:T(8,128)S(1)}, u32[]{:S(2)}, u32[]{:S(2)}) collective-permute-start(f32[8,128]{1,0:T(8,128)S(1)} %get-tuple-element.59), channel_id=1, source_target_pairs={{0,24},{8,16},{16,8},{24,0},{1,25},{9,17},{17,9},{25,1},{2,26},{10... | collective-permute-start | bytes 12296 | tf_op jit(solution)/shard_map/ppermute | solution.py:18
  63.6 3.0 %collective-permute-start.24 = (f32[8,128]{1,0:T(8,128)S(1)}, f32[8,128]{1,0:T(8,128)S(1)}, u32[]{:S(2)}, u32[]{:S(2)}) collective-permute-start(f32[8,128]{1,0:T(8,128)S(1)} %get-tuple-element.60), channel_id=1, source_target_pairs={{0,8},{8,0},{16,24},{24,16},{1,9},{9,1},{17,25},{25,17},{2,10},{10... | collective-permute-start | bytes 12296 | tf_op jit(solution)/shard_map/ppermute | solution.py:18
  (3 other events, 14.4 us)

commit v6 on v5

--- a/solution.py
+++ b/solution.py
@@ -154,8 +154,11 @@
     omega = pltpu.with_memory_space_constraint(omega, pltpu.HBM)
 
     m = rounded(momenta_init)
-    for bit in reversed(bits):
-        m = jnp.concatenate([m, swap(m, "fsdp", bit)], axis=0)
+    mates = swap(m, "fsdp", 1)
+    for bit in reversed(bits[1:]):
+        got = swap(m, "fsdp", bit)
+        m, mates = jnp.concatenate([m, got], axis=0), jnp.concatenate([mates, swap(got, "fsdp", 1)], axis=0)
+    m = jnp.concatenate([m, mates], axis=0)
     (keep, send), right = force_parts(m, kernel, bias, amplitude)
     got, right = lax.optimization_barrier((swap(send, "fsdp", 1), right))
     columns = [keep + got, right[0] + swap(right[1], "fsdp", 1)]

time: 67.4 us -> 67.6 us (level)
  waiting for transfers between devices: 20.9 us -> 22.3 us
  starting transfers between devices: 28.9 us -> 27.7 us
    ppermute x1, waiting for transfers between devices: 0.74 us -> 2.18 us  [swap_both(): return lax.ppermute(x, ('fsdp', 'cand'), pairs)]
    ppermute x1, starting transfers between devices: 1.67 us -> 0.71 us  [swap_both(): return lax.ppermute(x, ('fsdp', 'cand'), pairs)]
    ppermute x24 -> x25, starting transfers between devices: 27.2 us -> 27 us  [swap(): return lax.ppermute(x, axis, [(i, i ^ bit) for i in range(n)])]
    ppermute x24 -> x25, waiting for transfers between devices: 20.2 us -> 20.2 us  [swap(): return lax.ppermute(x, axis, [(i, i ^ bit) for i in range(n)])]
  transfers between devices with their start and end apart: 25 -> 26, of which waited for: 15 -> 14; matrix products, arithmetic and copies ran while one was open for 3% -> 3% of each run, Pallas kernels for 8% -> 7%
where the time goes in v6:
time: 67.6 us; the launch traced here: 67.5 us
  starting transfers between devices  27.7 us (41%)
  waiting for transfers between devices  22.3 us (33%)
  Pallas kernels  12.3 us (18%)
  other arithmetic  1.68 us (2%)
  local copies, waits for them, and re-layouts  1.26 us (2%)
  matrix products  1.18 us (2%)
  between operations  0.93 us (1%)
    ppermute x25, starting transfers between devices, swap(): return lax.ppermute(x, axis, [(i, i ^ bit) for i in range(n)])  27 us
    ppermute x25, waiting for transfers between devices, swap(): return lax.ppermute(x, axis, [(i, i ^ bit) for i in range(n)])  20.2 us
    pallas_call x1, Pallas kernels, force_parts(): pl.pallas_call(force_kernel, out_shape=(out, out, pltpu.VMEM((n, hidden),...  5.99 us
    pallas_call x2, Pallas kernels, angle_parts(): pl.pallas_call(functools.partial(angle_kernel, rows=rows, starts=[starts...  2.62 us
    pallas_call x1, Pallas kernels, load(): pl.pallas_call(functools.partial(load_kernel, start=start), out_shape=tup...  2.2 us
    ppermute x1, waiting for transfers between devices, swap_both(): return lax.ppermute(x, ('fsdp', 'cand'), pairs)  2.18 us
    pallas_call x1, Pallas kernels, force_parts(): pl.pallas_call(functools.partial(columns_kernel, start=cols), out_shape=(...  1.53 us
  transfers between devices with their start and end apart: 26, of which 14 were waited for; matrix products, arithmetic and copies ran while one was open for 3% of the time, Pallas kernels for 7%

profile of v6, /device:TPU:0, one launch (start us, length us, event | category | flops | bytes accessed | tf_op | source)
XLA Modules:
  0.0 67.5 jit_solution(11172940597955959783)
XLA Ops:
  0.7 1.1 %copy-done.2 = f32[8,8192]{1,0:T(8,128)S(1)} copy-done((f32[8,8192]{1,0:T(8,128)S(1)}, f32[8,8192]{1,0:T(8,128)}, u32[]{:S(2)}) %copy-start.2) | copy-done | bytes 262168
  1.8 3.0 %collective-permute-start = (bf16[8,8192]{1,0:T(8,128)(2,1)S(1)}, bf16[8,8192]{1,0:T(8,128)(2,1)S(1)}, u32[]{:S(2)}, u32[]{:S(2)}) collective-permute-start(bf16[8,8192]{1,0:T(8,128)(2,1)S(1)} %rounded.1), channel_id=1, source_target_pairs={{0,16},{8,24},{16,0},{24,8},{1,17},{9,25},{17,1},{25,9},{2,18},{10... | collective-permute-start | bytes 393224 | tf_op jit(solution)/shard_map/ppermute | solution.py:18
  4.8 3.5 %collective-permute-done = bf16[8,8192]{1,0:T(8,128)(2,1)S(1)} collective-permute-done((bf16[8,8192]{1,0:T(8,128)(2,1)S(1)}, bf16[8,8192]{1,0:T(8,128)(2,1)S(1)}, u32[]{:S(2)}, u32[]{:S(2)}) %collective-permute-start) | collective-permute-done | bytes 131104 | tf_op jit(solution)/shard_map/ppermute | solution.py:18
  8.4 1.3 %collective-permute-done.2 = bf16[8,8192]{1,0:T(8,128)(2,1)S(1)} collective-permute-done((bf16[8,8192]{1,0:T(8,128)(2,1)S(1)}, bf16[8,8192]{1,0:T(8,128)(2,1)S(1)}, u32[]{:S(2)}, u32[]{:S(2)}) %collective-permute-start.2) | collective-permute-done | bytes 131104 | tf_op jit(solution)/shard_map/ppermute | solution.py:18
  9.7 6.0 %force_left.1 = (f32[16,4096]{1,0:T(8,128)S(1)}, f32[16,4096]{1,0:T(8,128)S(1)}, bf16[32,1024]{1,0:T(8,128)(2,1)S(1)}) custom-call(bf16[32,8192]{1,0:T(8,128)(2,1)S(1)} %pad_maximum_fusion.m_ref, bf16[1024,8192]{1,0:T(8,128)(2,1)S(1)} %copy-done.1, bf16[1,1024]{1,0:T(2,128)(2,1)S(1)} %broadcast_in_dim.4.b_ref, bf16[1,1024]{1,0:T(2,128)(2,1)S(1)} %broadcast_in_dim.10.a_ref), custom_call_target="tpu_custom_call" | custom-call | flops 6442450944 | bytes 16777216 | tf_op jit(solution)/shard_map/force_left/pallas_call | solution.py:98
  15.9 1.5 %force_right.1 = (f32[16,4096]{1,0:T(8,128)S(1)}, f32[16,4096]{1,0:T(8,128)S(1)}) custom-call(bf16[32,1024]{1,0:T(8,128)(2,1)S(1)} %get-tuple-element.24.act_ref, bf16[1024,8192]{1,0:T(8,128)(2,1)S(1)} %copy-done.1), custom_call_target="tpu_custom_call" | custom-call | flops 2147483648 | bytes 8388608 | tf_op jit(solution)/shard_map/force_right/pallas_call | solution.py:110
  17.8 1.8 %collective-permute-start.4 = (bf16[8,4096]{1,0:T(8,128)(2,1)S(1)}, bf16[8,4096]{1,0:T(8,128)(2,1)S(1)}, u32[]{:S(2)}, u32[]{:S(2)}) collective-permute-start(bf16[8,4096]{1,0:T(8,128)(2,1)S(1)} %slice.152), channel_id=1, source_target_pairs={{0,16},{8,24},{16,0},{24,8},{1,17},{9,25},{17,1},{25,9},{2,18},{10... | collective-permute-start | bytes 196616 | tf_op jit(solution)/shard_map/ppermute | solution.py:18
  19.7 1.1 %collective-permute-start.6 = (bf16[8,4096]{1,0:T(8,128)(2,1)S(1)}, bf16[8,4096]{1,0:T(8,128)(2,1)S(1)}, u32[]{:S(2)}, u32[]{:S(2)}) collective-permute-start(bf16[8,4096]{1,0:T(8,128)(2,1)S(1)} %slice.151), channel_id=1, source_target_pairs={{0,16},{8,24},{16,0},{24,8},{1,17},{9,25},{17,1},{25,9},{2,18},{10... | collective-permute-start | bytes 196616 | tf_op jit(solution)/shard_map/ppermute | solution.py:18
  20.8 1.3 %collective-permute-done.4 = bf16[8,4096]{1,0:T(8,128)(2,1)S(1)} collective-permute-done((bf16[8,4096]{1,0:T(8,128)(2,1)S(1)}, bf16[8,4096]{1,0:T(8,128)(2,1)S(1)}, u32[]{:S(2)}, u32[]{:S(2)}) %collective-permute-start.4) | collective-permute-done | bytes 65568 | tf_op jit(solution)/shard_map/ppermute | solution.py:18
  22.2 1.8 %collective-permute-done.6 = bf16[8,4096]{1,0:T(8,128)(2,1)S(1)} collective-permute-done((bf16[8,4096]{1,0:T(8,128)(2,1)S(1)}, bf16[8,4096]{1,0:T(8,128)(2,1)S(1)}, u32[]{:S(2)}, u32[]{:S(2)}) %collective-permute-start.6) | collective-permute-done | bytes 65568 | tf_op jit(solution)/shard_map/ppermute | solution.py:18
  24.1 1.6 %collective-permute-start.7 = (bf16[8,2048]{1,0:T(8,128)(2,1)S(1)}, bf16[8,2048]{1,0:T(8,128)(2,1)S(1)}, u32[]{:S(2)}, u32[]{:S(2)}) collective-permute-start(bf16[8,2048]{1,0:T(8,128)(2,1)S(1)} %get-tuple-element.58), channel_id=1, source_target_pairs={{0,2},{1,3},{2,0},{3,1},{4,6},{5,7},{6,4},{7,5},{8,10},{9,11},{10,... | collective-permute-start | bytes 98312 | tf_op jit(solution)/shard_map/ppermute | solution.py:18
  25.8 2.6 %collective-permute-start.8 = (bf16[8,2048]{1,0:T(8,128)(2,1)S(1)}, bf16[8,2048]{1,0:T(8,128)(2,1)S(1)}, u32[]{:S(2)}, u32[]{:S(2)}) collective-permute-start(bf16[8,2048]{1,0:T(8,128)(2,1)S(1)} %get-tuple-element.57), channel_id=1, source_target_pairs={{0,4},{1,5},{2,6},{3,7},{4,0},{5,1},{6,2},{7,3},{8,12},{9,13},{10,... | collective-permute-start | bytes 98312 | tf_op jit(solution)/shard_map/ppermute | solution.py:18
  28.6 2.3 %collective-permute-done.8 = bf16[8,2048]{1,0:T(8,128)(2,1)S(1)} collective-permute-done((bf16[8,2048]{1,0:T(8,128)(2,1)S(1)}, bf16[8,2048]{1,0:T(8,128)(2,1)S(1)}, u32[]{:S(2)}, u32[]{:S(2)}) %collective-permute-start.8) | collective-permute-done | bytes 32800 | tf_op jit(solution)/shard_map/ppermute | solution.py:18
  30.8 3.2 %collective-permute-done.9 = bf16[8,2048]{1,0:T(8,128)(2,1)S(1)} collective-permute-done((bf16[8,2048]{1,0:T(8,128)(2,1)S(1)}, bf16[8,2048]{1,0:T(8,128)(2,1)S(1)}, u32[]{:S(2)}, u32[]{:S(2)}) %collective-permute-start.9) | collective-permute-done | bytes 32800 | tf_op jit(solution)/shard_map/ppermute | solution.py:18
  34.1 1.6 %collective-permute-start.10 = (bf16[32,1024]{1,0:T(8,128)(2,1)S(1)}, bf16[32,1024]{1,0:T(8,128)(2,1)S(1)}, u32[]{:S(2)}, u32[]{:S(2)}) collective-permute-start(bf16[32,1024]{1,0:T(8,128)(2,1)S(1)} %get-tuple-element.31), channel_id=1, source_target_pairs={{0,1},{1,0},{2,3},{3,2},{4,5},{5,4},{6,7},{7,6},{8,9},{9,8},{10,11... | collective-permute-start | bytes 196616 | tf_op jit(solution)/shard_map/ppermute | solution.py:18
  35.7 1.3 %collective-permute-start.11 = (bf16[32,1024]{1,0:T(8,128)(2,1)S(1)}, bf16[32,1024]{1,0:T(8,128)(2,1)S(1)}, u32[]{:S(2)}, u32[]{:S(2)}) collective-permute-start(bf16[32,1024]{1,0:T(8,128)(2,1)S(1)} %get-tuple-element.30), channel_id=1, source_target_pairs={{0,16},{8,24},{16,0},{24,8},{1,17},{9,25},{17,1},{25,9},{2,18},{10... | collective-permute-start | bytes 196616 | tf_op jit(solution)/shard_map/ppermute | solution.py:18
  37.0 0.7 %collective-permute-start.12 = (bf16[32,1024]{1,0:T(8,128)(2,1)S(1)}, bf16[32,1024]{1,0:T(8,128)(2,1)S(1)}, u32[]{:S(2)}, u32[]{:S(2)}) collective-permute-start(bf16[32,1024]{1,0:T(8,128)(2,1)S(1)} %get-tuple-element.31), channel_id=1, source_target_pairs={{0,17},{1,16},{2,19},{3,18},{4,21},{5,20},{6,23},{7,22},{8,25},{9,... | collective-permute-start | bytes 196616 | tf_op jit(solution)/shard_map/ppermute | solution.py:24
  37.7 2.2 %load_omega.1.w_ref = bf16[2048,1024]{1,0:T(8,128)(2,1)S(1)} custom-call(bf16[2048,1024]{1,0:T(8,128)(2,1)} %src_ref), custom_call_target="tpu_custom_call" | custom-call | bytes 8388608 | tf_op jit(solution)/shard_map/load_omega/pallas_call | solution.py:55
  39.9 2.2 %collective-permute-done.12 = bf16[32,1024]{1,0:T(8,128)(2,1)S(1)} collective-permute-done((bf16[32,1024]{1,0:T(8,128)(2,1)S(1)}, bf16[32,1024]{1,0:T(8,128)(2,1)S(1)}, u32[]{:S(2)}, u32[]{:S(2)}) %collective-permute-start.12) | collective-permute-done | bytes 65568 | tf_op jit(solution)/shard_map/ppermute | solution.py:24
  42.1 1.3 %angle_parts.2 = (f32[64,2048]{1,0:T(8,128)S(1)}, bf16[64,2048]{1,0:T(8,128)(2,1)S(1)}) custom-call(bf16[128,1024]{1,0:T(8,128)(2,1)S(1)} %pad_maximum_fusion.1.t_ref, bf16[2048,1024]{1,0:T(8,128)(2,1)S(1)} %load_omega.1.w_ref), custom_call_target="tpu_custom_call" | custom-call | flops 536870912 | bytes 4194304 | tf_op jit(solution)/shard_map/angle_parts/pallas_call | solution.py:132
  44.7 0.8 %collective-permute-done.18 = bf16[128,512]{1,0:T(8,128)(2,1)S(1)} collective-permute-done((bf16[128,512]{1,0:T(8,128)(2,1)S(1)}, bf16[128,512]{1,0:T(8,128)(2,1)S(1)}, u32[]{:S(2)}, u32[]{:S(2)}) %collective-permute-start.18) | collective-permute-done | bytes 131104 | tf_op jit(solution)/shard_map/ppermute | solution.py:18
  45.7 1.3 %angle_parts.3 = (f32[64,2048]{1,0:T(8,128)S(1)}, bf16[64,2048]{1,0:T(8,128)(2,1)S(1)}) custom-call(bf16[128,1024]{1,0:T(8,128)(2,1)S(1)} %pad_maximum_fusion.2.t_ref, bf16[2048,1024]{1,0:T(8,128)(2,1)S(1)} %load_omega.1.w_ref), custom_call_target="tpu_custom_call" | custom-call | tf_op jit(solution)/shard_map/angle_parts/pallas_call | solution.py:132
  47.1 1.6 %collective-permute-start.20 = (bf16[64,2048]{1,0:T(8,128)(2,1)S(1)}, bf16[64,2048]{1,0:T(8,128)(2,1)S(1)}, u32[]{:S(2)}, u32[]{:S(2)}) collective-permute-start(bf16[64,2048]{1,0:T(8,128)(2,1)S(1)} %get-tuple-element.40), channel_id=1, source_target_pairs={{0,1},{1,0},{2,3},{3,2},{4,5},{5,4},{6,7},{7,6},{8,9},{9,8},{10,11... | collective-permute-start | bytes 786440 | tf_op jit(solution)/shard_map/ppermute | solution.py:18
  48.6 1.3 %collective-permute-done.13 = bf16[64,2048]{1,0:T(8,128)(2,1)S(1)} collective-permute-done((bf16[64,2048]{1,0:T(8,128)(2,1)S(1)}, bf16[64,2048]{1,0:T(8,128)(2,1)S(1)}, u32[]{:S(2)}, u32[]{:S(2)}) %collective-permute-start.13) | collective-permute-done | bytes 262176 | tf_op jit(solution)/shard_map/ppermute | solution.py:18
  50.5 3.9 %collective-permute-start.16 = (bf16[16,2048]{1,0:T(8,128)(2,1)S(1)}, bf16[16,2048]{1,0:T(8,128)(2,1)S(1)}, u32[]{:S(2)}, u32[]{:S(2)}) collective-permute-start(bf16[16,2048]{1,0:T(8,128)(2,1)S(1)} %get-tuple-element.46), channel_id=1, source_target_pairs={{0,2},{1,3},{2,0},{3,1},{4,6},{5,7},{6,4},{7,5},{8,10},{9,11},{10,... | collective-permute-start | bytes 196616 | tf_op jit(solution)/shard_map/ppermute | solution.py:18
  54.4 1.2 %collective-permute-done.20 = bf16[64,2048]{1,0:T(8,128)(2,1)S(1)} collective-permute-done((bf16[64,2048]{1,0:T(8,128)(2,1)S(1)}, bf16[64,2048]{1,0:T(8,128)(2,1)S(1)}, u32[]{:S(2)}, u32[]{:S(2)}) %collective-permute-start.20) | collective-permute-done | bytes 262176 | tf_op jit(solution)/shard_map/ppermute | solution.py:18
  56.3 3.9 %collective-permute-start.23 = (bf16[16,2048]{1,0:T(8,128)(2,1)S(1)}, bf16[16,2048]{1,0:T(8,128)(2,1)S(1)}, u32[]{:S(2)}, u32[]{:S(2)}) collective-permute-start(bf16[16,2048]{1,0:T(8,128)(2,1)S(1)} %get-tuple-element.49), channel_id=1, source_target_pairs={{0,2},{1,3},{2,0},{3,1},{4,6},{5,7},{6,4},{7,5},{8,10},{9,11},{10,... | collective-permute-start | bytes 196616 | tf_op jit(solution)/shard_map/ppermute | solution.py:18
  60.8 0.8 %collective-permute-start.17 = (f32[8,128]{1,0:T(8,128)S(1)}, f32[8,128]{1,0:T(8,128)S(1)}, u32[]{:S(2)}, u32[]{:S(2)}) collective-permute-start(f32[8,128]{1,0:T(8,128)S(1)} %slice.103), channel_id=1, source_target_pairs={{0,16},{8,24},{16,0},{24,8},{1,17},{9,25},{17,1},{25,9},{2,18},{10... | collective-permute-start | bytes 12296 | tf_op jit(solution)/shard_map/ppermute | solution.py:18
  61.6 1.0 %collective-permute-done.21 = bf16[16,2048]{1,0:T(8,128)(2,1)S(1)} collective-permute-done((bf16[16,2048]{1,0:T(8,128)(2,1)S(1)}, bf16[16,2048]{1,0:T(8,128)(2,1)S(1)}, u32[]{:S(2)}, u32[]{:S(2)}) %collective-permute-start.21) | collective-permute-done | bytes 65568 | tf_op jit(solution)/shard_map/ppermute | solution.py:18
  63.8 0.8 %collective-permute-start.25 = (f32[8,128]{1,0:T(8,128)S(1)}, f32[8,128]{1,0:T(8,128)S(1)}, u32[]{:S(2)}, u32[]{:S(2)}) collective-permute-start(f32[8,128]{1,0:T(8,128)S(1)} %get-tuple-element.60), channel_id=1, source_target_pairs={{0,8},{8,0},{16,24},{24,16},{1,9},{9,1},{17,25},{25,17},{2,10},{10... | collective-permute-start | bytes 12296 | tf_op jit(solution)/shard_map/ppermute | solution.py:18
  64.7 0.7 %broadcast_add_fusion = f32[8,8192]{1,0:T(8,128)} fusion(f32[8,8192]{1,0:T(8,128)S(1)} %copy-done.3, f32[8192]{0:T(1024)S(1)} %copy-done.7), kind=kLoop, calls=%fused_computation.26 | loop fusion | flops 65536 | bytes 557056 | tf_op jit(solution)/shard_map/add | solution.py:182
  65.4 1.4 %collective-permute-done.24 = f32[8,128]{1,0:T(8,128)S(1)} collective-permute-done((f32[8,128]{1,0:T(8,128)S(1)}, f32[8,128]{1,0:T(8,128)S(1)}, u32[]{:S(2)}, u32[]{:S(2)}) %collective-permute-start.24) | collective-permute-done | bytes 4128 | tf_op jit(solution)/shard_map/ppermute | solution.py:18
  (72 shorter events, 6.2 us)
Async XLA Ops:
  0.6 59.6 %copy-start = (bf16[2048,128]{1,0:T(8,128)(2,1)S(1)}, bf16[2048,128]{1,0:T(8,128)(2,1)}, u32[]{:S(2)}) copy-start(bf16[2048,128]{1,0:T(8,128)(2,1)} %param.17) | copy-start | bytes 1572868
  0.6 9.1 %copy-start.1 = (bf16[1024,8192]{1,0:T(8,128)(2,1)S(1)}, bf16[1024,8192]{1,0:T(8,128)(2,1)}, u32[]{:S(2)}) copy-start(bf16[1024,8192]{1,0:T(8,128)(2,1)} %k_ref.3) | copy-start | bytes 50331652
  1.8 6.5 %collective-permute-start = (bf16[8,8192]{1,0:T(8,128)(2,1)S(1)}, bf16[8,8192]{1,0:T(8,128)(2,1)S(1)}, u32[]{:S(2)}, u32[]{:S(2)}) collective-permute-start(bf16[8,8192]{1,0:T(8,128)(2,1)S(1)} %rounded.1), channel_id=1, source_target_pairs={{0,16},{8,24},{16,0},{24,8},{1,17},{9,25},{17,1},{25,9},{2,18},{10... | collective-permute-start | bytes 393224 | tf_op jit(solution)/shard_map/ppermute | solution.py:18
  4.8 3.5 %collective-permute-start.1 = (bf16[8,8192]{1,0:T(8,128)(2,1)S(1)}, bf16[8,8192]{1,0:T(8,128)(2,1)S(1)}, u32[]{:S(2)}, u32[]{:S(2)}) collective-permute-start(bf16[8,8192]{1,0:T(8,128)(2,1)S(1)} %rounded.1), channel_id=1, source_target_pairs={{0,8},{8,0},{16,24},{24,16},{1,9},{9,1},{17,25},{25,17},{2,10},{10... | collective-permute-start | bytes 393224 | tf_op jit(solution)/shard_map/ppermute | solution.py:18
  8.3 1.3 %collective-permute-start.2 = (bf16[8,8192]{1,0:T(8,128)(2,1)S(1)}, bf16[8,8192]{1,0:T(8,128)(2,1)S(1)}, u32[]{:S(2)}, u32[]{:S(2)}) collective-permute-start(bf16[8,8192]{1,0:T(8,128)(2,1)S(1)} %collective-permute-done), channel_id=1, source_target_pairs={{0,8},{8,0},{16,24},{24,16},{1,9},{9,1},{17,25},{25,17},{2,10},{10... | collective-permute-start | bytes 393224 | tf_op jit(solution)/shard_map/ppermute | solution.py:18
  15.7 1.7 %collective-permute-start.3 = (f32[16,4096]{1,0:T(8,128)S(1)}, f32[16,4096]{1,0:T(8,128)S(1)}, u32[]{:S(2)}, u32[]{:S(2)}) collective-permute-start(f32[16,4096]{1,0:T(8,128)S(1)} %get-tuple-element.23), channel_id=1, source_target_pairs={{0,8},{8,0},{16,24},{24,16},{1,9},{9,1},{17,25},{25,17},{2,10},{10... | collective-permute-start | bytes 786440 | tf_op jit(solution)/shard_map/ppermute | solution.py:18
  17.4 2.2 %collective-permute-start.5 = (f32[16,4096]{1,0:T(8,128)S(1)}, f32[16,4096]{1,0:T(8,128)S(1)}, u32[]{:S(2)}, u32[]{:S(2)}) collective-permute-start(f32[16,4096]{1,0:T(8,128)S(1)} %get-tuple-element.29), channel_id=1, source_target_pairs={{0,8},{8,0},{16,24},{24,16},{1,9},{9,1},{17,25},{25,17},{2,10},{10... | collective-permute-start | bytes 786440 | tf_op jit(solution)/shard_map/ppermute | solution.py:18
  17.8 4.3 %collective-permute-start.4 = (bf16[8,4096]{1,0:T(8,128)(2,1)S(1)}, bf16[8,4096]{1,0:T(8,128)(2,1)S(1)}, u32[]{:S(2)}, u32[]{:S(2)}) collective-permute-start(bf16[8,4096]{1,0:T(8,128)(2,1)S(1)} %slice.152), channel_id=1, source_target_pairs={{0,16},{8,24},{16,0},{24,8},{1,17},{9,25},{17,1},{25,9},{2,18},{10... | collective-permute-start | bytes 196616 | tf_op jit(solution)/shard_map/ppermute | solution.py:18
  19.7 4.3 %collective-permute-start.6 = (bf16[8,4096]{1,0:T(8,128)(2,1)S(1)}, bf16[8,4096]{1,0:T(8,128)(2,1)S(1)}, u32[]{:S(2)}, u32[]{:S(2)}) collective-permute-start(bf16[8,4096]{1,0:T(8,128)(2,1)S(1)} %slice.151), channel_id=1, source_target_pairs={{0,16},{8,24},{16,0},{24,8},{1,17},{9,25},{17,1},{25,9},{2,18},{10... | collective-permute-start | bytes 196616 | tf_op jit(solution)/shard_map/ppermute | solution.py:18
  24.1 15.8 %copy-start.4 = (bf16[8,8192]{1,0:T(8,128)(2,1)}, bf16[8,8192]{1,0:T(8,128)(2,1)S(1)}, u32[]{:S(2)}) copy-start(bf16[8,8192]{1,0:T(8,128)(2,1)S(1)} %fusion) | copy-start | bytes 393220
  24.1 4.5 %collective-permute-start.7 = (bf16[8,2048]{1,0:T(8,128)(2,1)S(1)}, bf16[8,2048]{1,0:T(8,128)(2,1)S(1)}, u32[]{:S(2)}, u32[]{:S(2)}) collective-permute-start(bf16[8,2048]{1,0:T(8,128)(2,1)S(1)} %get-tuple-element.58), channel_id=1, source_target_pairs={{0,2},{1,3},{2,0},{3,1},{4,6},{5,7},{6,4},{7,5},{8,10},{9,11},{10,... | collective-permute-start | bytes 98312 | tf_op jit(solution)/shard_map/ppermute | solution.py:18
  25.8 5.1 %collective-permute-start.8 = (bf16[8,2048]{1,0:T(8,128)(2,1)S(1)}, bf16[8,2048]{1,0:T(8,128)(2,1)S(1)}, u32[]{:S(2)}, u32[]{:S(2)}) collective-permute-start(bf16[8,2048]{1,0:T(8,128)(2,1)S(1)} %get-tuple-element.57), channel_id=1, source_target_pairs={{0,4},{1,5},{2,6},{3,7},{4,0},{5,1},{6,2},{7,3},{8,12},{9,13},{10,... | collective-permute-start | bytes 98312 | tf_op jit(solution)/shard_map/ppermute | solution.py:18
  28.4 5.7 %collective-permute-start.9 = (bf16[8,2048]{1,0:T(8,128)(2,1)S(1)}, bf16[8,2048]{1,0:T(8,128)(2,1)S(1)}, u32[]{:S(2)}, u32[]{:S(2)}) collective-permute-start(bf16[8,2048]{1,0:T(8,128)(2,1)S(1)} %get-tuple-element.56), channel_id=1, source_target_pairs={{0,6},{1,7},{2,4},{3,5},{4,2},{5,3},{6,0},{7,1},{8,14},{9,15},{10,... | collective-permute-start | bytes 98312 | tf_op jit(solution)/shard_map/ppermute | solution.py:18
  34.1 5.8 %collective-permute-start.10 = (bf16[32,1024]{1,0:T(8,128)(2,1)S(1)}, bf16[32,1024]{1,0:T(8,128)(2,1)S(1)}, u32[]{:S(2)}, u32[]{:S(2)}) collective-permute-start(bf16[32,1024]{1,0:T(8,128)(2,1)S(1)} %get-tuple-element.31), channel_id=1, source_target_pairs={{0,1},{1,0},{2,3},{3,2},{4,5},{5,4},{6,7},{7,6},{8,9},{9,8},{10,11... | collective-permute-start | bytes 196616 | tf_op jit(solution)/shard_map/ppermute | solution.py:18
  35.7 4.3 %collective-permute-start.11 = (bf16[32,1024]{1,0:T(8,128)(2,1)S(1)}, bf16[32,1024]{1,0:T(8,128)(2,1)S(1)}, u32[]{:S(2)}, u32[]{:S(2)}) collective-permute-start(bf16[32,1024]{1,0:T(8,128)(2,1)S(1)} %get-tuple-element.30), channel_id=1, source_target_pairs={{0,16},{8,24},{16,0},{24,8},{1,17},{9,25},{17,1},{25,9},{2,18},{10... | collective-permute-start | bytes 196616 | tf_op jit(solution)/shard_map/ppermute | solution.py:18
  37.0 5.2 %collective-permute-start.12 = (bf16[32,1024]{1,0:T(8,128)(2,1)S(1)}, bf16[32,1024]{1,0:T(8,128)(2,1)S(1)}, u32[]{:S(2)}, u32[]{:S(2)}) collective-permute-start(bf16[32,1024]{1,0:T(8,128)(2,1)S(1)} %get-tuple-element.31), channel_id=1, source_target_pairs={{0,17},{1,16},{2,19},{3,18},{4,21},{5,20},{6,23},{7,22},{8,25},{9,... | collective-permute-start | bytes 196616 | tf_op jit(solution)/shard_map/ppermute | solution.py:24
  43.5 6.4 %collective-permute-start.13 = (bf16[64,2048]{1,0:T(8,128)(2,1)S(1)}, bf16[64,2048]{1,0:T(8,128)(2,1)S(1)}, u32[]{:S(2)}, u32[]{:S(2)}) collective-permute-start(bf16[64,2048]{1,0:T(8,128)(2,1)S(1)} %get-tuple-element.37), channel_id=1, source_target_pairs={{0,1},{1,0},{2,3},{3,2},{4,5},{5,4},{6,7},{7,6},{8,9},{9,8},{10,11... | collective-permute-start | bytes 786440 | tf_op jit(solution)/shard_map/ppermute | solution.py:18
  44.1 1.4 %collective-permute-start.18 = (bf16[128,512]{1,0:T(8,128)(2,1)S(1)}, bf16[128,512]{1,0:T(8,128)(2,1)S(1)}, u32[]{:S(2)}, u32[]{:S(2)}) collective-permute-start(bf16[128,512]{1,0:T(8,128)(2,1)S(1)} %get-tuple-element.51), channel_id=1, source_target_pairs={{0,8},{8,0},{16,24},{24,16},{1,9},{9,1},{17,25},{25,17},{2,10},{10... | collective-permute-start | bytes 393224 | tf_op jit(solution)/shard_map/ppermute | solution.py:18
  44.2 1.5 %collective-permute-start.19 = (bf16[128,512]{1,0:T(8,128)(2,1)S(1)}, bf16[128,512]{1,0:T(8,128)(2,1)S(1)}, u32[]{:S(2)}, u32[]{:S(2)}) collective-permute-start(bf16[128,512]{1,0:T(8,128)(2,1)S(1)} %get-tuple-element.52), channel_id=1, source_target_pairs={{0,8},{8,0},{16,24},{24,16},{1,9},{9,1},{17,25},{25,17},{2,10},{10... | collective-permute-start | bytes 393224 | tf_op jit(solution)/shard_map/ppermute | solution.py:18
  45.7 14.5 %copy-start.6 = (f32[2048]{0:T(1024)S(1)}, f32[2048]{0:T(1024)}, u32[]{:S(2)}) copy-start(f32[2048]{0:T(1024)} %param.16) | copy-start | bytes 24580
  45.7 19.0 %copy-start.3 = (f32[8,8192]{1,0:T(8,128)S(1)}, f32[8,8192]{1,0:T(8,128)}, u32[]{:S(2)}) copy-start(f32[8,8192]{1,0:T(8,128)} %x_ref.1) | copy-start | bytes 786436
  45.7 19.0 %copy-start.7 = (f32[8192]{0:T(1024)S(1)}, f32[8192]{0:T(1024)}, u32[]{:S(2)}) copy-start(f32[8192]{0:T(1024)} %param.14) | copy-start | bytes 98308
  47.1 8.6 %collective-permute-start.20 = (bf16[64,2048]{1,0:T(8,128)(2,1)S(1)}, bf16[64,2048]{1,0:T(8,128)(2,1)S(1)}, u32[]{:S(2)}, u32[]{:S(2)}) collective-permute-start(bf16[64,2048]{1,0:T(8,128)(2,1)S(1)} %get-tuple-element.40), channel_id=1, source_target_pairs={{0,1},{1,0},{2,3},{3,2},{4,5},{5,4},{6,7},{7,6},{8,9},{9,8},{10,11... | collective-permute-start | bytes 786440 | tf_op jit(solution)/shard_map/ppermute | solution.py:18
  50.0 6.3 %collective-permute-start.14 = (bf16[16,2048]{1,0:T(8,128)(2,1)S(1)}, bf16[16,2048]{1,0:T(8,128)(2,1)S(1)}, u32[]{:S(2)}, u32[]{:S(2)}) collective-permute-start(bf16[16,2048]{1,0:T(8,128)(2,1)S(1)} %get-tuple-element.45), channel_id=1, source_target_pairs={{0,6},{1,7},{2,4},{3,5},{4,2},{5,3},{6,0},{7,1},{8,14},{9,15},{10,... | collective-permute-start | bytes 196616 | tf_op jit(solution)/shard_map/ppermute | solution.py:18
  50.4 9.8 %collective-permute-start.15 = (bf16[16,2048]{1,0:T(8,128)(2,1)S(1)}, bf16[16,2048]{1,0:T(8,128)(2,1)S(1)}, u32[]{:S(2)}, u32[]{:S(2)}) collective-permute-start(bf16[16,2048]{1,0:T(8,128)(2,1)S(1)} %get-tuple-element.47), channel_id=1, source_target_pairs={{0,4},{1,5},{2,6},{3,7},{4,0},{5,1},{6,2},{7,3},{8,12},{9,13},{10,... | collective-permute-start | bytes 196616 | tf_op jit(solution)/shard_map/ppermute | solution.py:18
  50.5 9.7 %collective-permute-start.16 = (bf16[16,2048]{1,0:T(8,128)(2,1)S(1)}, bf16[16,2048]{1,0:T(8,128)(2,1)S(1)}, u32[]{:S(2)}, u32[]{:S(2)}) collective-permute-start(bf16[16,2048]{1,0:T(8,128)(2,1)S(1)} %get-tuple-element.46), channel_id=1, source_target_pairs={{0,2},{1,3},{2,0},{3,1},{4,6},{5,7},{6,4},{7,5},{8,10},{9,11},{10,... | collective-permute-start | bytes 196616 | tf_op jit(solution)/shard_map/ppermute | solution.py:18
  55.8 6.8 %collective-permute-start.21 = (bf16[16,2048]{1,0:T(8,128)(2,1)S(1)}, bf16[16,2048]{1,0:T(8,128)(2,1)S(1)}, u32[]{:S(2)}, u32[]{:S(2)}) collective-permute-start(bf16[16,2048]{1,0:T(8,128)(2,1)S(1)} %get-tuple-element.48), channel_id=1, source_target_pairs={{0,6},{1,7},{2,4},{3,5},{4,2},{5,3},{6,0},{7,1},{8,14},{9,15},{10,... | collective-permute-start | bytes 196616 | tf_op jit(solution)/shard_map/ppermute | solution.py:18
  56.2 6.4 %collective-permute-start.22 = (bf16[16,2048]{1,0:T(8,128)(2,1)S(1)}, bf16[16,2048]{1,0:T(8,128)(2,1)S(1)}, u32[]{:S(2)}, u32[]{:S(2)}) collective-permute-start(bf16[16,2048]{1,0:T(8,128)(2,1)S(1)} %get-tuple-element.50), channel_id=1, source_target_pairs={{0,4},{1,5},{2,6},{3,7},{4,0},{5,1},{6,2},{7,3},{8,12},{9,13},{10,... | collective-permute-start | bytes 196616 | tf_op jit(solution)/shard_map/ppermute | solution.py:18
  56.3 6.9 %collective-permute-start.23 = (bf16[16,2048]{1,0:T(8,128)(2,1)S(1)}, bf16[16,2048]{1,0:T(8,128)(2,1)S(1)}, u32[]{:S(2)}, u32[]{:S(2)}) collective-permute-start(bf16[16,2048]{1,0:T(8,128)(2,1)S(1)} %get-tuple-element.49), channel_id=1, source_target_pairs={{0,2},{1,3},{2,0},{3,1},{4,6},{5,7},{6,4},{7,5},{8,10},{9,11},{10,... | collective-permute-start | bytes 196616 | tf_op jit(solution)/shard_map/ppermute | solution.py:18
  60.8 4.6 %collective-permute-start.17 = (f32[8,128]{1,0:T(8,128)S(1)}, f32[8,128]{1,0:T(8,128)S(1)}, u32[]{:S(2)}, u32[]{:S(2)}) collective-permute-start(f32[8,128]{1,0:T(8,128)S(1)} %slice.103), channel_id=1, source_target_pairs={{0,16},{8,24},{16,0},{24,8},{1,17},{9,25},{17,1},{25,9},{2,18},{10... | collective-permute-start | bytes 12296 | tf_op jit(solution)/shard_map/ppermute | solution.py:18
  63.8 3.0 %collective-permute-start.24 = (f32[8,128]{1,0:T(8,128)S(1)}, f32[8,128]{1,0:T(8,128)S(1)}, u32[]{:S(2)}, u32[]{:S(2)}) collective-permute-start(f32[8,128]{1,0:T(8,128)S(1)} %get-tuple-element.59), channel_id=1, source_target_pairs={{0,24},{8,16},{16,8},{24,0},{1,25},{9,17},{17,9},{25,1},{2,26},{10... | collective-permute-start | bytes 12296 | tf_op jit(solution)/shard_map/ppermute | solution.py:18
  63.8 3.0 %collective-permute-start.25 = (f32[8,128]{1,0:T(8,128)S(1)}, f32[8,128]{1,0:T(8,128)S(1)}, u32[]{:S(2)}, u32[]{:S(2)}) collective-permute-start(f32[8,128]{1,0:T(8,128)S(1)} %get-tuple-element.60), channel_id=1, source_target_pairs={{0,8},{8,0},{16,24},{24,16},{1,9},{9,1},{17,25},{25,17},{2,10},{10... | collective-permute-start | bytes 12296 | tf_op jit(solution)/shard_map/ppermute | solution.py:18
  (4 other events, 22.4 us)

commit v7 on v5

--- a/solution.py
+++ b/solution.py
@@ -140,6 +140,30 @@
         ),
         name="angle_parts",
     )(t, omega)
+
+
+def sample_kernel(angles_ref, phase_ref, samples_ref, *refs, scale):
+    *got_refs, out_ref = refs
+    angles = angles_ref[...] + phase_ref[...]
+    for ref in got_refs:
+        angles = angles + ref[...].astype(F32)
+    features = (scale * jnp.cos(angles)).astype(BF16)
+    out_ref[...] = jnp.dot(features, samples_ref[...], preferred_element_type=F32)
+
+
+def sample_parts(angles, gots, phase, samples, scale):
+    rows, feats = angles.shape
+    return pl.pallas_call(
+        functools.partial(sample_kernel, scale=scale),
+        out_shape=pltpu.VMEM((rows, samples.shape[1]), F32),
+        in_specs=[VM] * (3 + len(gots)),
+        out_specs=VM,
+        compiler_params=pltpu.CompilerParams(vmem_limit_bytes=8 * 2**20),
+        cost_estimate=pl.CostEstimate(
+            flops=2 * rows * feats * samples.shape[1], bytes_accessed=2 * samples.size, transcendentals=rows * feats
+        ),
+        name="sample_parts",
+    )(angles, phase[None, :], samples, *gots)
 
 
 def local(positions_init, momenta_init, kernel, bias, amplitude, shift, omega, phase, samples):
@@ -194,11 +218,7 @@
         keep = keep + got.astype(F32)
         blocks = [keep[j * n_rows : (j + 1) * n_rows] for j in range(n_outer)]
         gots = [swap(blocks[j].astype(BF16), "cand", 2 * j) for j in reversed(range(1, n_outer))]
-        angles = blocks[0] + phase[None, :]
-        for x in gots:
-            angles = angles + x.astype(F32)
-        features = (jnp.sqrt(2.0 / (feats * n_fsdp)) * jnp.cos(angles)).astype(BF16)
-        part = jnp.dot(features, samples, preferred_element_type=F32).reshape(-1, own, samples.shape[1])
+        part = sample_parts(blocks[0], gots, phase, samples, math.sqrt(2.0 / (feats * n_fsdp))).reshape(-1, own, samples.shape[1])
         for bit in bits[2:]:
             half = part.shape[0] // 2
             part = part[:half] + swap(part[half:], "fsdp", bit)

time: 67.4 us -> 67.4 us (level)
  matrix products: 1.18 us -> 0 us
  Pallas kernels: 12.4 us -> 13.5 us
    pallas_call x0 -> x2, Pallas kernels: none -> 1.18 us  [sample_parts(): pl.pallas_call(functools.partial(sample_kernel, scale=scale), out_shape=p...]
    dot_general x2 -> x0, matrix products: 1.18 us -> none  [local(): jnp.dot(features, samples, preferred_element_type=F32)]
  transfers between devices with their start and end apart: 25 -> 25, of which waited for: 15 -> 15; matrix products, arithmetic and copies ran while one was open for 3% -> 2% of each run, Pallas kernels for 8% -> 9%
where the time goes in v7:
time: 67.4 us; the launch traced here: 67.2 us
  starting transfers between devices  28.9 us (43%)
  waiting for transfers between devices  20.9 us (31%)
  Pallas kernels  13.5 us (20%)
  other arithmetic  1.69 us (3%)
  local copies, waits for them, and re-layouts  1.27 us (2%)
  between operations  0.98 us (1%)
    ppermute x24, starting transfers between devices, swap(): return lax.ppermute(x, axis, [(i, i ^ bit) for i in range(n)])  27.2 us
    ppermute x24, waiting for transfers between devices, swap(): return lax.ppermute(x, axis, [(i, i ^ bit) for i in range(n)])  20.1 us
    pallas_call x1, Pallas kernels, force_parts(): pl.pallas_call(force_kernel, out_shape=(out, out, pltpu.VMEM((n, hidden),...  5.98 us
    pallas_call x2, Pallas kernels, angle_parts(): pl.pallas_call(functools.partial(angle_kernel, rows=rows, starts=[starts...  2.63 us
    pallas_call x1, Pallas kernels, load(): pl.pallas_call(functools.partial(load_kernel, start=start), out_shape=tup...  2.2 us
    ppermute x1, starting transfers between devices, swap_both(): return lax.ppermute(x, ('fsdp', 'cand'), pairs)  1.67 us
    pallas_call x1, Pallas kernels, force_parts(): pl.pallas_call(functools.partial(columns_kernel, start=cols), out_shape=(...  1.53 us
  transfers between devices with their start and end apart: 25, of which 15 were waited for; matrix products, arithmetic and copies ran while one was open for 2% of the time, Pallas kernels for 9%

profile of v7, /device:TPU:0, one launch (start us, length us, event | category | flops | bytes accessed | tf_op | source)
XLA Modules:
  0.0 67.2 jit_solution(10591169996964756615)
XLA Ops:
  0.7 1.1 %copy-done.2 = f32[8,8192]{1,0:T(8,128)S(1)} copy-done((f32[8,8192]{1,0:T(8,128)S(1)}, f32[8,8192]{1,0:T(8,128)}, u32[]{:S(2)}) %copy-start.2) | copy-done | bytes 262168
  1.8 3.0 %collective-permute-start = (bf16[8,8192]{1,0:T(8,128)(2,1)S(1)}, bf16[8,8192]{1,0:T(8,128)(2,1)S(1)}, u32[]{:S(2)}, u32[]{:S(2)}) collective-permute-start(bf16[8,8192]{1,0:T(8,128)(2,1)S(1)} %rounded.1), channel_id=1, source_target_pairs={{0,16},{8,24},{16,0},{24,8},{1,17},{9,25},{17,1},{25,9},{2,18},{10... | collective-permute-start | bytes 393224 | tf_op jit(solution)/shard_map/ppermute | solution.py:18
  4.8 3.5 %collective-permute-done = bf16[8,8192]{1,0:T(8,128)(2,1)S(1)} collective-permute-done((bf16[8,8192]{1,0:T(8,128)(2,1)S(1)}, bf16[8,8192]{1,0:T(8,128)(2,1)S(1)}, u32[]{:S(2)}, u32[]{:S(2)}) %collective-permute-start) | collective-permute-done | bytes 131104 | tf_op jit(solution)/shard_map/ppermute | solution.py:18
  8.4 1.5 %collective-permute-done.1 = bf16[16,8192]{1,0:T(8,128)(2,1)S(1)} collective-permute-done((bf16[16,8192]{1,0:T(8,128)(2,1)S(1)}, bf16[16,8192]{1,0:T(8,128)(2,1)S(1)}, u32[]{:S(2)}, u32[]{:S(2)}) %collective-permute-start.1) | collective-permute-done | bytes 262176 | tf_op jit(solution)/shard_map/ppermute | solution.py:18
  10.0 6.0 %force_left.1 = (f32[16,4096]{1,0:T(8,128)S(1)}, f32[16,4096]{1,0:T(8,128)S(1)}, bf16[32,1024]{1,0:T(8,128)(2,1)S(1)}) custom-call(bf16[32,8192]{1,0:T(8,128)(2,1)S(1)} %pad_maximum_fusion.m_ref, bf16[1024,8192]{1,0:T(8,128)(2,1)S(1)} %copy-done, bf16[1,1024]{1,0:T(2,128)(2,1)S(1)} %broadcast_in_dim.11.b_ref, bf16[1,1024]{1,0:T(2,128)(2,1)S(1)} %broadcast_in_dim.12.a_ref), custom_call_target="tpu_custom_call" | custom-call | flops 6442450944 | bytes 16777216 | tf_op jit(solution)/shard_map/force_left/pallas_call | solution.py:98
  16.1 1.5 %force_right.1 = (f32[16,4096]{1,0:T(8,128)S(1)}, f32[16,4096]{1,0:T(8,128)S(1)}) custom-call(bf16[32,1024]{1,0:T(8,128)(2,1)S(1)} %get-tuple-element.24.act_ref, bf16[1024,8192]{1,0:T(8,128)(2,1)S(1)} %copy-done), custom_call_target="tpu_custom_call" | custom-call | flops 2147483648 | bytes 8388608 | tf_op jit(solution)/shard_map/force_right/pallas_call | solution.py:110
  18.1 1.8 %collective-permute-start.3 = (bf16[8,4096]{1,0:T(8,128)(2,1)S(1)}, bf16[8,4096]{1,0:T(8,128)(2,1)S(1)}, u32[]{:S(2)}, u32[]{:S(2)}) collective-permute-start(bf16[8,4096]{1,0:T(8,128)(2,1)S(1)} %slice.124), channel_id=1, source_target_pairs={{0,16},{8,24},{16,0},{24,8},{1,17},{9,25},{17,1},{25,9},{2,18},{10... | collective-permute-start | bytes 196616 | tf_op jit(solution)/shard_map/ppermute | solution.py:18
  19.9 1.1 %collective-permute-start.5 = (bf16[8,4096]{1,0:T(8,128)(2,1)S(1)}, bf16[8,4096]{1,0:T(8,128)(2,1)S(1)}, u32[]{:S(2)}, u32[]{:S(2)}) collective-permute-start(bf16[8,4096]{1,0:T(8,128)(2,1)S(1)} %slice.123), channel_id=1, source_target_pairs={{0,16},{8,24},{16,0},{24,8},{1,17},{9,25},{17,1},{25,9},{2,18},{10... | collective-permute-start | bytes 196616 | tf_op jit(solution)/shard_map/ppermute | solution.py:18
  21.1 1.4 %collective-permute-done.3 = bf16[8,4096]{1,0:T(8,128)(2,1)S(1)} collective-permute-done((bf16[8,4096]{1,0:T(8,128)(2,1)S(1)}, bf16[8,4096]{1,0:T(8,128)(2,1)S(1)}, u32[]{:S(2)}, u32[]{:S(2)}) %collective-permute-start.3) | collective-permute-done | bytes 65568 | tf_op jit(solution)/shard_map/ppermute | solution.py:18
  22.4 1.8 %collective-permute-done.5 = bf16[8,4096]{1,0:T(8,128)(2,1)S(1)} collective-permute-done((bf16[8,4096]{1,0:T(8,128)(2,1)S(1)}, bf16[8,4096]{1,0:T(8,128)(2,1)S(1)}, u32[]{:S(2)}, u32[]{:S(2)}) %collective-permute-start.5) | collective-permute-done | bytes 65568 | tf_op jit(solution)/shard_map/ppermute | solution.py:18
  24.4 1.6 %collective-permute-start.6 = (bf16[8,2048]{1,0:T(8,128)(2,1)S(1)}, bf16[8,2048]{1,0:T(8,128)(2,1)S(1)}, u32[]{:S(2)}, u32[]{:S(2)}) collective-permute-start(bf16[8,2048]{1,0:T(8,128)(2,1)S(1)} %get-tuple-element.58), channel_id=1, source_target_pairs={{0,2},{1,3},{2,0},{3,1},{4,6},{5,7},{6,4},{7,5},{8,10},{9,11},{10,... | collective-permute-start | bytes 98312 | tf_op jit(solution)/shard_map/ppermute | solution.py:18
  26.0 2.6 %collective-permute-start.7 = (bf16[8,2048]{1,0:T(8,128)(2,1)S(1)}, bf16[8,2048]{1,0:T(8,128)(2,1)S(1)}, u32[]{:S(2)}, u32[]{:S(2)}) collective-permute-start(bf16[8,2048]{1,0:T(8,128)(2,1)S(1)} %get-tuple-element.57), channel_id=1, source_target_pairs={{0,4},{1,5},{2,6},{3,7},{4,0},{5,1},{6,2},{7,3},{8,12},{9,13},{10,... | collective-permute-start | bytes 98312 | tf_op jit(solution)/shard_map/ppermute | solution.py:18
  28.8 2.3 %collective-permute-done.7 = bf16[8,2048]{1,0:T(8,128)(2,1)S(1)} collective-permute-done((bf16[8,2048]{1,0:T(8,128)(2,1)S(1)}, bf16[8,2048]{1,0:T(8,128)(2,1)S(1)}, u32[]{:S(2)}, u32[]{:S(2)}) %collective-permute-start.7) | collective-permute-done | bytes 32800 | tf_op jit(solution)/shard_map/ppermute | solution.py:18
  31.1 3.2 %collective-permute-done.8 = bf16[8,2048]{1,0:T(8,128)(2,1)S(1)} collective-permute-done((bf16[8,2048]{1,0:T(8,128)(2,1)S(1)}, bf16[8,2048]{1,0:T(8,128)(2,1)S(1)}, u32[]{:S(2)}, u32[]{:S(2)}) %collective-permute-start.8) | collective-permute-done | bytes 32800 | tf_op jit(solution)/shard_map/ppermute | solution.py:18
  34.4 1.4 %collective-permute-start.10 = (bf16[32,1024]{1,0:T(8,128)(2,1)S(1)}, bf16[32,1024]{1,0:T(8,128)(2,1)S(1)}, u32[]{:S(2)}, u32[]{:S(2)}) collective-permute-start(bf16[32,1024]{1,0:T(8,128)(2,1)S(1)} %get-tuple-element.30), channel_id=1, source_target_pairs={{0,16},{8,24},{16,0},{24,8},{1,17},{9,25},{17,1},{25,9},{2,18},{10... | collective-permute-start | bytes 196616 | tf_op jit(solution)/shard_map/ppermute | solution.py:18
  35.7 1.7 %collective-permute-start.11 = (bf16[32,1024]{1,0:T(8,128)(2,1)S(1)}, bf16[32,1024]{1,0:T(8,128)(2,1)S(1)}, u32[]{:S(2)}, u32[]{:S(2)}) collective-permute-start(bf16[32,1024]{1,0:T(8,128)(2,1)S(1)} %get-tuple-element.31), channel_id=1, source_target_pairs={{0,17},{1,16},{2,19},{3,18},{4,21},{5,20},{6,23},{7,22},{8,25},{9,... | collective-permute-start | bytes 196616 | tf_op jit(solution)/shard_map/ppermute | solution.py:24
  37.9 2.2 %load_omega.1.w_ref = bf16[2048,1024]{1,0:T(8,128)(2,1)S(1)} custom-call(bf16[2048,1024]{1,0:T(8,128)(2,1)} %src_ref), custom_call_target="tpu_custom_call" | custom-call | bytes 8388608 | tf_op jit(solution)/shard_map/load_omega/pallas_call | solution.py:55
  40.1 0.7 %collective-permute-done.11 = bf16[32,1024]{1,0:T(8,128)(2,1)S(1)} collective-permute-done((bf16[32,1024]{1,0:T(8,128)(2,1)S(1)}, bf16[32,1024]{1,0:T(8,128)(2,1)S(1)}, u32[]{:S(2)}, u32[]{:S(2)}) %collective-permute-start.11) | collective-permute-done | bytes 65568 | tf_op jit(solution)/shard_map/ppermute | solution.py:24
  40.9 0.8 %collective-permute-done.9 = bf16[32,1024]{1,0:T(8,128)(2,1)S(1)} collective-permute-done((bf16[32,1024]{1,0:T(8,128)(2,1)S(1)}, bf16[32,1024]{1,0:T(8,128)(2,1)S(1)}, u32[]{:S(2)}, u32[]{:S(2)}) %collective-permute-start.9) | collective-permute-done | bytes 65568 | tf_op jit(solution)/shard_map/ppermute | solution.py:18
  41.7 1.3 %angle_parts.2 = (f32[64,2048]{1,0:T(8,128)S(1)}, bf16[64,2048]{1,0:T(8,128)(2,1)S(1)}) custom-call(bf16[128,1024]{1,0:T(8,128)(2,1)S(1)} %pad_maximum_fusion.2.t_ref, bf16[2048,1024]{1,0:T(8,128)(2,1)S(1)} %load_omega.1.w_ref), custom_call_target="tpu_custom_call" | custom-call | flops 536870912 | bytes 4194304 | tf_op jit(solution)/shard_map/angle_parts/pallas_call | solution.py:132
  43.0 0.8 %collective-permute-start.12 = (bf16[64,2048]{1,0:T(8,128)(2,1)S(1)}, bf16[64,2048]{1,0:T(8,128)(2,1)S(1)}, u32[]{:S(2)}, u32[]{:S(2)}) collective-permute-start(bf16[64,2048]{1,0:T(8,128)(2,1)S(1)} %get-tuple-element.37), channel_id=1, source_target_pairs={{0,1},{1,0},{2,3},{3,2},{4,5},{5,4},{6,7},{7,6},{8,9},{9,8},{10,11... | collective-permute-start | bytes 786440 | tf_op jit(solution)/shard_map/ppermute | solution.py:18
  44.4 0.8 %collective-permute-done.17 = bf16[128,512]{1,0:T(8,128)(2,1)S(1)} collective-permute-done((bf16[128,512]{1,0:T(8,128)(2,1)S(1)}, bf16[128,512]{1,0:T(8,128)(2,1)S(1)}, u32[]{:S(2)}, u32[]{:S(2)}) %collective-permute-start.17) | collective-permute-done | bytes 131104 | tf_op jit(solution)/shard_map/ppermute | solution.py:18
  45.4 1.3 %angle_parts.3 = (f32[64,2048]{1,0:T(8,128)S(1)}, bf16[64,2048]{1,0:T(8,128)(2,1)S(1)}) custom-call(bf16[128,1024]{1,0:T(8,128)(2,1)S(1)} %pad_maximum_fusion.3.t_ref, bf16[2048,1024]{1,0:T(8,128)(2,1)S(1)} %load_omega.1.w_ref), custom_call_target="tpu_custom_call" | custom-call | tf_op jit(solution)/shard_map/angle_parts/pallas_call | solution.py:132
  46.8 1.4 %collective-permute-start.19 = (bf16[64,2048]{1,0:T(8,128)(2,1)S(1)}, bf16[64,2048]{1,0:T(8,128)(2,1)S(1)}, u32[]{:S(2)}, u32[]{:S(2)}) collective-permute-start(bf16[64,2048]{1,0:T(8,128)(2,1)S(1)} %get-tuple-element.40), channel_id=1, source_target_pairs={{0,1},{1,0},{2,3},{3,2},{4,5},{5,4},{6,7},{7,6},{8,9},{9,8},{10,11... | collective-permute-start | bytes 786440 | tf_op jit(solution)/shard_map/ppermute | solution.py:18
  48.2 1.3 %collective-permute-done.12 = bf16[64,2048]{1,0:T(8,128)(2,1)S(1)} collective-permute-done((bf16[64,2048]{1,0:T(8,128)(2,1)S(1)}, bf16[64,2048]{1,0:T(8,128)(2,1)S(1)}, u32[]{:S(2)}, u32[]{:S(2)}) %collective-permute-start.12) | collective-permute-done | bytes 262176 | tf_op jit(solution)/shard_map/ppermute | solution.py:18
  49.9 4.0 %collective-permute-start.15 = (bf16[16,2048]{1,0:T(8,128)(2,1)S(1)}, bf16[16,2048]{1,0:T(8,128)(2,1)S(1)}, u32[]{:S(2)}, u32[]{:S(2)}) collective-permute-start(bf16[16,2048]{1,0:T(8,128)(2,1)S(1)} %get-tuple-element.45), channel_id=1, source_target_pairs={{0,2},{1,3},{2,0},{3,1},{4,6},{5,7},{6,4},{7,5},{8,10},{9,11},{10,... | collective-permute-start | bytes 196616 | tf_op jit(solution)/shard_map/ppermute | solution.py:18
  54.0 1.4 %collective-permute-done.19 = bf16[64,2048]{1,0:T(8,128)(2,1)S(1)} collective-permute-done((bf16[64,2048]{1,0:T(8,128)(2,1)S(1)}, bf16[64,2048]{1,0:T(8,128)(2,1)S(1)}, u32[]{:S(2)}, u32[]{:S(2)}) %collective-permute-start.19) | collective-permute-done | bytes 262176 | tf_op jit(solution)/shard_map/ppermute | solution.py:18
  56.0 3.9 %collective-permute-start.22 = (bf16[16,2048]{1,0:T(8,128)(2,1)S(1)}, bf16[16,2048]{1,0:T(8,128)(2,1)S(1)}, u32[]{:S(2)}, u32[]{:S(2)}) collective-permute-start(bf16[16,2048]{1,0:T(8,128)(2,1)S(1)} %get-tuple-element.48), channel_id=1, source_target_pairs={{0,2},{1,3},{2,0},{3,1},{4,6},{5,7},{6,4},{7,5},{8,10},{9,11},{10,... | collective-permute-start | bytes 196616 | tf_op jit(solution)/shard_map/ppermute | solution.py:18
  60.6 1.3 %collective-permute-start.16 = (f32[8,128]{1,0:T(8,128)S(1)}, f32[8,128]{1,0:T(8,128)S(1)}, u32[]{:S(2)}, u32[]{:S(2)}) collective-permute-start(f32[8,128]{1,0:T(8,128)S(1)} %slice.103), channel_id=1, source_target_pairs={{0,16},{8,24},{16,0},{24,8},{1,17},{9,25},{17,1},{25,9},{2,18},{10... | collective-permute-start | bytes 12296 | tf_op jit(solution)/shard_map/ppermute | solution.py:18
  63.6 1.4 %collective-permute-start.24 = (f32[8,128]{1,0:T(8,128)S(1)}, f32[8,128]{1,0:T(8,128)S(1)}, u32[]{:S(2)}, u32[]{:S(2)}) collective-permute-start(f32[8,128]{1,0:T(8,128)S(1)} %get-tuple-element.60), channel_id=1, source_target_pairs={{0,8},{8,0},{16,24},{24,16},{1,9},{9,1},{17,25},{25,17},{2,10},{10... | collective-permute-start | bytes 12296 | tf_op jit(solution)/shard_map/ppermute | solution.py:18
  65.0 0.7 %broadcast_add_fusion = f32[8,8192]{1,0:T(8,128)} fusion(f32[8,8192]{1,0:T(8,128)S(1)} %copy-done.3, f32[8192]{0:T(1024)S(1)} %copy-done.7), kind=kLoop, calls=%fused_computation.13 | loop fusion | flops 65536 | bytes 557056 | tf_op jit(solution)/shard_map/add | solution.py:203
  65.7 0.9 %collective-permute-done.23 = f32[8,128]{1,0:T(8,128)S(1)} collective-permute-done((f32[8,128]{1,0:T(8,128)S(1)}, f32[8,128]{1,0:T(8,128)S(1)}, u32[]{:S(2)}, u32[]{:S(2)}) %collective-permute-start.23) | collective-permute-done | bytes 4128 | tf_op jit(solution)/shard_map/ppermute | solution.py:18
  (73 shorter events, 6.5 us)
Async XLA Ops:
  0.6 9.3 %copy-start = (bf16[1024,8192]{1,0:T(8,128)(2,1)S(1)}, bf16[1024,8192]{1,0:T(8,128)(2,1)}, u32[]{:S(2)}) copy-start(bf16[1024,8192]{1,0:T(8,128)(2,1)} %k_ref.3) | copy-start | bytes 50331652
  1.8 6.5 %collective-permute-start = (bf16[8,8192]{1,0:T(8,128)(2,1)S(1)}, bf16[8,8192]{1,0:T(8,128)(2,1)S(1)}, u32[]{:S(2)}, u32[]{:S(2)}) collective-permute-start(bf16[8,8192]{1,0:T(8,128)(2,1)S(1)} %rounded.1), channel_id=1, source_target_pairs={{0,16},{8,24},{16,0},{24,8},{1,17},{9,25},{17,1},{25,9},{2,18},{10... | collective-permute-start | bytes 393224 | tf_op jit(solution)/shard_map/ppermute | solution.py:18
  8.3 1.6 %collective-permute-start.1 = (bf16[16,8192]{1,0:T(8,128)(2,1)S(1)}, bf16[16,8192]{1,0:T(8,128)(2,1)S(1)}, u32[]{:S(2)}, u32[]{:S(2)}) collective-permute-start(bf16[16,8192]{1,0:T(8,128)(2,1)S(1)} %pad_maximum_fusion.1), channel_id=1, source_target_pairs={{0,8},{8,0},{16,24},{24,16},{1,9},{9,1},{17,25},{25,17},{2,10},{10... | collective-permute-start | bytes 786440 | tf_op jit(solution)/shard_map/ppermute | solution.py:18
  15.9 1.7 %collective-permute-start.2 = (f32[16,4096]{1,0:T(8,128)S(1)}, f32[16,4096]{1,0:T(8,128)S(1)}, u32[]{:S(2)}, u32[]{:S(2)}) collective-permute-start(f32[16,4096]{1,0:T(8,128)S(1)} %get-tuple-element.23), channel_id=1, source_target_pairs={{0,8},{8,0},{16,24},{24,16},{1,9},{9,1},{17,25},{25,17},{2,10},{10... | collective-permute-start | bytes 786440 | tf_op jit(solution)/shard_map/ppermute | solution.py:18
  16.1 8.2 %copy-start.6 = (f32[8,8192]{1,0:T(8,128)S(1)}, f32[8,8192]{1,0:T(8,128)}, u32[]{:S(2)}) copy-start(f32[8,8192]{1,0:T(8,128)} %param.9) | copy-start | bytes 786436
  17.6 2.3 %collective-permute-start.4 = (f32[16,4096]{1,0:T(8,128)S(1)}, f32[16,4096]{1,0:T(8,128)S(1)}, u32[]{:S(2)}, u32[]{:S(2)}) collective-permute-start(f32[16,4096]{1,0:T(8,128)S(1)} %get-tuple-element.29), channel_id=1, source_target_pairs={{0,8},{8,0},{16,24},{24,16},{1,9},{9,1},{17,25},{25,17},{2,10},{10... | collective-permute-start | bytes 786440 | tf_op jit(solution)/shard_map/ppermute | solution.py:18
  18.1 4.3 %collective-permute-start.3 = (bf16[8,4096]{1,0:T(8,128)(2,1)S(1)}, bf16[8,4096]{1,0:T(8,128)(2,1)S(1)}, u32[]{:S(2)}, u32[]{:S(2)}) collective-permute-start(bf16[8,4096]{1,0:T(8,128)(2,1)S(1)} %slice.124), channel_id=1, source_target_pairs={{0,16},{8,24},{16,0},{24,8},{1,17},{9,25},{17,1},{25,9},{2,18},{10... | collective-permute-start | bytes 196616 | tf_op jit(solution)/shard_map/ppermute | solution.py:18
  19.9 4.3 %collective-permute-start.5 = (bf16[8,4096]{1,0:T(8,128)(2,1)S(1)}, bf16[8,4096]{1,0:T(8,128)(2,1)S(1)}, u32[]{:S(2)}, u32[]{:S(2)}) collective-permute-start(bf16[8,4096]{1,0:T(8,128)(2,1)S(1)} %slice.123), channel_id=1, source_target_pairs={{0,16},{8,24},{16,0},{24,8},{1,17},{9,25},{17,1},{25,9},{2,18},{10... | collective-permute-start | bytes 196616 | tf_op jit(solution)/shard_map/ppermute | solution.py:18
  24.3 15.8 %copy-start.5 = (bf16[8,8192]{1,0:T(8,128)(2,1)}, bf16[8,8192]{1,0:T(8,128)(2,1)S(1)}, u32[]{:S(2)}) copy-start(bf16[8,8192]{1,0:T(8,128)(2,1)S(1)} %fusion) | copy-start | bytes 393220
  24.4 4.5 %collective-permute-start.6 = (bf16[8,2048]{1,0:T(8,128)(2,1)S(1)}, bf16[8,2048]{1,0:T(8,128)(2,1)S(1)}, u32[]{:S(2)}, u32[]{:S(2)}) collective-permute-start(bf16[8,2048]{1,0:T(8,128)(2,1)S(1)} %get-tuple-element.58), channel_id=1, source_target_pairs={{0,2},{1,3},{2,0},{3,1},{4,6},{5,7},{6,4},{7,5},{8,10},{9,11},{10,... | collective-permute-start | bytes 98312 | tf_op jit(solution)/shard_map/ppermute | solution.py:18
  26.0 5.1 %collective-permute-start.7 = (bf16[8,2048]{1,0:T(8,128)(2,1)S(1)}, bf16[8,2048]{1,0:T(8,128)(2,1)S(1)}, u32[]{:S(2)}, u32[]{:S(2)}) collective-permute-start(bf16[8,2048]{1,0:T(8,128)(2,1)S(1)} %get-tuple-element.57), channel_id=1, source_target_pairs={{0,4},{1,5},{2,6},{3,7},{4,0},{5,1},{6,2},{7,3},{8,12},{9,13},{10,... | collective-permute-start | bytes 98312 | tf_op jit(solution)/shard_map/ppermute | solution.py:18
  28.6 5.7 %collective-permute-start.8 = (bf16[8,2048]{1,0:T(8,128)(2,1)S(1)}, bf16[8,2048]{1,0:T(8,128)(2,1)S(1)}, u32[]{:S(2)}, u32[]{:S(2)}) collective-permute-start(bf16[8,2048]{1,0:T(8,128)(2,1)S(1)} %get-tuple-element.56), channel_id=1, source_target_pairs={{0,6},{1,7},{2,4},{3,5},{4,2},{5,3},{6,0},{7,1},{8,14},{9,15},{10,... | collective-permute-start | bytes 98312 | tf_op jit(solution)/shard_map/ppermute | solution.py:18
  34.4 5.8 %collective-permute-start.10 = (bf16[32,1024]{1,0:T(8,128)(2,1)S(1)}, bf16[32,1024]{1,0:T(8,128)(2,1)S(1)}, u32[]{:S(2)}, u32[]{:S(2)}) collective-permute-start(bf16[32,1024]{1,0:T(8,128)(2,1)S(1)} %get-tuple-element.30), channel_id=1, source_target_pairs={{0,16},{8,24},{16,0},{24,8},{1,17},{9,25},{17,1},{25,9},{2,18},{10... | collective-permute-start | bytes 196616 | tf_op jit(solution)/shard_map/ppermute | solution.py:18
  35.7 5.2 %collective-permute-start.11 = (bf16[32,1024]{1,0:T(8,128)(2,1)S(1)}, bf16[32,1024]{1,0:T(8,128)(2,1)S(1)}, u32[]{:S(2)}, u32[]{:S(2)}) collective-permute-start(bf16[32,1024]{1,0:T(8,128)(2,1)S(1)} %get-tuple-element.31), channel_id=1, source_target_pairs={{0,17},{1,16},{2,19},{3,18},{4,21},{5,20},{6,23},{7,22},{8,25},{9,... | collective-permute-start | bytes 196616 | tf_op jit(solution)/shard_map/ppermute | solution.py:24
  37.4 4.3 %collective-permute-start.9 = (bf16[32,1024]{1,0:T(8,128)(2,1)S(1)}, bf16[32,1024]{1,0:T(8,128)(2,1)S(1)}, u32[]{:S(2)}, u32[]{:S(2)}) collective-permute-start(bf16[32,1024]{1,0:T(8,128)(2,1)S(1)} %get-tuple-element.31), channel_id=1, source_target_pairs={{0,1},{1,0},{2,3},{3,2},{4,5},{5,4},{6,7},{7,6},{8,9},{9,8},{10,11... | collective-permute-start | bytes 196616 | tf_op jit(solution)/shard_map/ppermute | solution.py:18
  43.0 6.4 %collective-permute-start.12 = (bf16[64,2048]{1,0:T(8,128)(2,1)S(1)}, bf16[64,2048]{1,0:T(8,128)(2,1)S(1)}, u32[]{:S(2)}, u32[]{:S(2)}) collective-permute-start(bf16[64,2048]{1,0:T(8,128)(2,1)S(1)} %get-tuple-element.37), channel_id=1, source_target_pairs={{0,1},{1,0},{2,3},{3,2},{4,5},{5,4},{6,7},{7,6},{8,9},{9,8},{10,11... | collective-permute-start | bytes 786440 | tf_op jit(solution)/shard_map/ppermute | solution.py:18
  43.8 1.4 %collective-permute-start.17 = (bf16[128,512]{1,0:T(8,128)(2,1)S(1)}, bf16[128,512]{1,0:T(8,128)(2,1)S(1)}, u32[]{:S(2)}, u32[]{:S(2)}) collective-permute-start(bf16[128,512]{1,0:T(8,128)(2,1)S(1)} %get-tuple-element.51), channel_id=1, source_target_pairs={{0,8},{8,0},{16,24},{24,16},{1,9},{9,1},{17,25},{25,17},{2,10},{10... | collective-permute-start | bytes 393224 | tf_op jit(solution)/shard_map/ppermute | solution.py:18
  43.9 1.5 %collective-permute-start.18 = (bf16[128,512]{1,0:T(8,128)(2,1)S(1)}, bf16[128,512]{1,0:T(8,128)(2,1)S(1)}, u32[]{:S(2)}, u32[]{:S(2)}) collective-permute-start(bf16[128,512]{1,0:T(8,128)(2,1)S(1)} %get-tuple-element.52), channel_id=1, source_target_pairs={{0,8},{8,0},{16,24},{24,16},{1,9},{9,1},{17,25},{25,17},{2,10},{10... | collective-permute-start | bytes 393224 | tf_op jit(solution)/shard_map/ppermute | solution.py:18
  45.4 14.6 %copy-start.1 = (bf16[2048,128]{1,0:T(8,128)(2,1)S(1)}, bf16[2048,128]{1,0:T(8,128)(2,1)}, u32[]{:S(2)}) copy-start(bf16[2048,128]{1,0:T(8,128)(2,1)} %samples_ref.3) | copy-start | bytes 1572868
  45.4 14.6 %copy-start.4 = (f32[2048]{0:T(1024)S(1)}, f32[2048]{0:T(1024)}, u32[]{:S(2)}) copy-start(f32[2048]{0:T(1024)} %param.16) | copy-start | bytes 24580
  46.8 18.2 %copy-start.3 = (f32[8,8192]{1,0:T(8,128)S(1)}, f32[8,8192]{1,0:T(8,128)}, u32[]{:S(2)}) copy-start(f32[8,8192]{1,0:T(8,128)} %x_ref.1) | copy-start | bytes 786436
  46.8 18.2 %copy-start.7 = (f32[8192]{0:T(1024)S(1)}, f32[8192]{0:T(1024)}, u32[]{:S(2)}) copy-start(f32[8192]{0:T(1024)} %param.14) | copy-start | bytes 98308
  46.8 8.6 %collective-permute-start.19 = (bf16[64,2048]{1,0:T(8,128)(2,1)S(1)}, bf16[64,2048]{1,0:T(8,128)(2,1)S(1)}, u32[]{:S(2)}, u32[]{:S(2)}) collective-permute-start(bf16[64,2048]{1,0:T(8,128)(2,1)S(1)} %get-tuple-element.40), channel_id=1, source_target_pairs={{0,1},{1,0},{2,3},{3,2},{4,5},{5,4},{6,7},{7,6},{8,9},{9,8},{10,11... | collective-permute-start | bytes 786440 | tf_op jit(solution)/shard_map/ppermute | solution.py:18
  49.5 6.5 %collective-permute-start.13 = (bf16[16,2048]{1,0:T(8,128)(2,1)S(1)}, bf16[16,2048]{1,0:T(8,128)(2,1)S(1)}, u32[]{:S(2)}, u32[]{:S(2)}) collective-permute-start(bf16[16,2048]{1,0:T(8,128)(2,1)S(1)} %get-tuple-element.47), channel_id=1, source_target_pairs={{0,6},{1,7},{2,4},{3,5},{4,2},{5,3},{6,0},{7,1},{8,14},{9,15},{10,... | collective-permute-start | bytes 196616 | tf_op jit(solution)/shard_map/ppermute | solution.py:18
  49.9 10.0 %collective-permute-start.14 = (bf16[16,2048]{1,0:T(8,128)(2,1)S(1)}, bf16[16,2048]{1,0:T(8,128)(2,1)S(1)}, u32[]{:S(2)}, u32[]{:S(2)}) collective-permute-start(bf16[16,2048]{1,0:T(8,128)(2,1)S(1)} %get-tuple-element.46), channel_id=1, source_target_pairs={{0,4},{1,5},{2,6},{3,7},{4,0},{5,1},{6,2},{7,3},{8,12},{9,13},{10,... | collective-permute-start | bytes 196616 | tf_op jit(solution)/shard_map/ppermute | solution.py:18
  49.9 10.0 %collective-permute-start.15 = (bf16[16,2048]{1,0:T(8,128)(2,1)S(1)}, bf16[16,2048]{1,0:T(8,128)(2,1)S(1)}, u32[]{:S(2)}, u32[]{:S(2)}) collective-permute-start(bf16[16,2048]{1,0:T(8,128)(2,1)S(1)} %get-tuple-element.45), channel_id=1, source_target_pairs={{0,2},{1,3},{2,0},{3,1},{4,6},{5,7},{6,4},{7,5},{8,10},{9,11},{10,... | collective-permute-start | bytes 196616 | tf_op jit(solution)/shard_map/ppermute | solution.py:18
  55.5 6.8 %collective-permute-start.20 = (bf16[16,2048]{1,0:T(8,128)(2,1)S(1)}, bf16[16,2048]{1,0:T(8,128)(2,1)S(1)}, u32[]{:S(2)}, u32[]{:S(2)}) collective-permute-start(bf16[16,2048]{1,0:T(8,128)(2,1)S(1)} %get-tuple-element.50), channel_id=1, source_target_pairs={{0,6},{1,7},{2,4},{3,5},{4,2},{5,3},{6,0},{7,1},{8,14},{9,15},{10,... | collective-permute-start | bytes 196616 | tf_op jit(solution)/shard_map/ppermute | solution.py:18
  55.9 6.4 %collective-permute-start.21 = (bf16[16,2048]{1,0:T(8,128)(2,1)S(1)}, bf16[16,2048]{1,0:T(8,128)(2,1)S(1)}, u32[]{:S(2)}, u32[]{:S(2)}) collective-permute-start(bf16[16,2048]{1,0:T(8,128)(2,1)S(1)} %get-tuple-element.49), channel_id=1, source_target_pairs={{0,4},{1,5},{2,6},{3,7},{4,0},{5,1},{6,2},{7,3},{8,12},{9,13},{10,... | collective-permute-start | bytes 196616 | tf_op jit(solution)/shard_map/ppermute | solution.py:18
  56.0 7.0 %collective-permute-start.22 = (bf16[16,2048]{1,0:T(8,128)(2,1)S(1)}, bf16[16,2048]{1,0:T(8,128)(2,1)S(1)}, u32[]{:S(2)}, u32[]{:S(2)}) collective-permute-start(bf16[16,2048]{1,0:T(8,128)(2,1)S(1)} %get-tuple-element.48), channel_id=1, source_target_pairs={{0,2},{1,3},{2,0},{3,1},{4,6},{5,7},{6,4},{7,5},{8,10},{9,11},{10,... | collective-permute-start | bytes 196616 | tf_op jit(solution)/shard_map/ppermute | solution.py:18
  60.6 5.1 %collective-permute-start.16 = (f32[8,128]{1,0:T(8,128)S(1)}, f32[8,128]{1,0:T(8,128)S(1)}, u32[]{:S(2)}, u32[]{:S(2)}) collective-permute-start(f32[8,128]{1,0:T(8,128)S(1)} %slice.103), channel_id=1, source_target_pairs={{0,16},{8,24},{16,0},{24,8},{1,17},{9,25},{17,1},{25,9},{2,18},{10... | collective-permute-start | bytes 12296 | tf_op jit(solution)/shard_map/ppermute | solution.py:18
  63.6 3.1 %collective-permute-start.23 = (f32[8,128]{1,0:T(8,128)S(1)}, f32[8,128]{1,0:T(8,128)S(1)}, u32[]{:S(2)}, u32[]{:S(2)}) collective-permute-start(f32[8,128]{1,0:T(8,128)S(1)} %get-tuple-element.59), channel_id=1, source_target_pairs={{0,24},{8,16},{16,8},{24,0},{1,25},{9,17},{17,9},{25,1},{2,26},{10... | collective-permute-start | bytes 12296 | tf_op jit(solution)/shard_map/ppermute | solution.py:18
  63.6 3.0 %collective-permute-start.24 = (f32[8,128]{1,0:T(8,128)S(1)}, f32[8,128]{1,0:T(8,128)S(1)}, u32[]{:S(2)}, u32[]{:S(2)}) collective-permute-start(f32[8,128]{1,0:T(8,128)S(1)} %get-tuple-element.60), channel_id=1, source_target_pairs={{0,8},{8,0},{16,24},{24,16},{1,9},{9,1},{17,25},{25,17},{2,10},{10... | collective-permute-start | bytes 12296 | tf_op jit(solution)/shard_map/ppermute | solution.py:18
  (3 other events, 14.4 us)

commit v8 on v5

--- a/solution.py
+++ b/solution.py
@@ -158,7 +158,7 @@
         m = jnp.concatenate([m, swap(m, "fsdp", bit)], axis=0)
     (keep, send), right = force_parts(m, kernel, bias, amplitude)
     got, right = lax.optimization_barrier((swap(send, "fsdp", 1), right))
-    columns = [keep + got, right[0] + swap(right[1], "fsdp", 1)]
+    columns = [keep + got, right[0] + swap(right[1].astype(BF16), "fsdp", 1).astype(F32)]
     for bit in bits[1:]:
         half = columns[0].shape[0] // 2
         columns = [c[:half] + swap(c[half:].astype(BF16), "fsdp", bit).astype(F32) for c in columns]

time: 67.4 us -> 67.4 us (level)
  transfers between devices with their start and end apart: 25 -> 25, of which waited for: 15 -> 15; matrix products, arithmetic and copies ran while one was open for 3% -> 3% of each run, Pallas kernels for 8% -> 7%
where the time goes in v8:
time: 67.4 us; the launch traced here: 67.3 us
  starting transfers between devices  28.7 us (43%)
  waiting for transfers between devices  21.1 us (31%)
  Pallas kernels  12.3 us (18%)
  other arithmetic  1.71 us (3%)
  local copies, waits for them, and re-layouts  1.26 us (2%)
  matrix products  1.18 us (2%)
  between operations  0.95 us (1%)
    ppermute x24, starting transfers between devices, swap(): return lax.ppermute(x, axis, [(i, i ^ bit) for i in range(n)])  27.1 us
    ppermute x24, waiting for transfers between devices, swap(): return lax.ppermute(x, axis, [(i, i ^ bit) for i in range(n)])  20.4 us
    pallas_call x1, Pallas kernels, force_parts(): pl.pallas_call(force_kernel, out_shape=(out, out, pltpu.VMEM((n, hidden),...  5.98 us
    pallas_call x2, Pallas kernels, angle_parts(): pl.pallas_call(functools.partial(angle_kernel, rows=rows, starts=[starts...  2.62 us
    pallas_call x1, Pallas kernels, load(): pl.pallas_call(functools.partial(load_kernel, start=start), out_shape=tup...  2.2 us
    ppermute x1, starting transfers between devices, swap_both(): return lax.ppermute(x, ('fsdp', 'cand'), pairs)  1.67 us
    pallas_call x1, Pallas kernels, force_parts(): pl.pallas_call(functools.partial(columns_kernel, start=cols), out_shape=(...  1.53 us
  transfers between devices with their start and end apart: 25, of which 15 were waited for; matrix products, arithmetic and copies ran while one was open for 3% of the time, Pallas kernels for 7%

profile of v8, /device:TPU:0, one launch (start us, length us, event | category | flops | bytes accessed | tf_op | source)
XLA Modules:
  0.0 67.3 jit_solution(10468274081330081623)
XLA Ops:
  0.7 1.1 %copy-done.2 = f32[8,8192]{1,0:T(8,128)S(1)} copy-done((f32[8,8192]{1,0:T(8,128)S(1)}, f32[8,8192]{1,0:T(8,128)}, u32[]{:S(2)}) %copy-start.2) | copy-done | bytes 262168
  1.8 3.0 %collective-permute-start = (bf16[8,8192]{1,0:T(8,128)(2,1)S(1)}, bf16[8,8192]{1,0:T(8,128)(2,1)S(1)}, u32[]{:S(2)}, u32[]{:S(2)}) collective-permute-start(bf16[8,8192]{1,0:T(8,128)(2,1)S(1)} %rounded.1), channel_id=1, source_target_pairs={{0,16},{8,24},{16,0},{24,8},{1,17},{9,25},{17,1},{25,9},{2,18},{10... | collective-permute-start | bytes 393224 | tf_op jit(solution)/shard_map/ppermute | solution.py:18
  4.8 3.5 %collective-permute-done = bf16[8,8192]{1,0:T(8,128)(2,1)S(1)} collective-permute-done((bf16[8,8192]{1,0:T(8,128)(2,1)S(1)}, bf16[8,8192]{1,0:T(8,128)(2,1)S(1)}, u32[]{:S(2)}, u32[]{:S(2)}) %collective-permute-start) | collective-permute-done | bytes 131104 | tf_op jit(solution)/shard_map/ppermute | solution.py:18
  8.5 1.5 %collective-permute-done.1 = bf16[16,8192]{1,0:T(8,128)(2,1)S(1)} collective-permute-done((bf16[16,8192]{1,0:T(8,128)(2,1)S(1)}, bf16[16,8192]{1,0:T(8,128)(2,1)S(1)}, u32[]{:S(2)}, u32[]{:S(2)}) %collective-permute-start.1) | collective-permute-done | bytes 262176 | tf_op jit(solution)/shard_map/ppermute | solution.py:18
  10.0 6.0 %force_left.1 = (f32[16,4096]{1,0:T(8,128)S(1)}, f32[16,4096]{1,0:T(8,128)S(1)}, bf16[32,1024]{1,0:T(8,128)(2,1)S(1)}) custom-call(bf16[32,8192]{1,0:T(8,128)(2,1)S(1)} %pad_maximum_fusion.m_ref, bf16[1024,8192]{1,0:T(8,128)(2,1)S(1)} %copy-done.1, bf16[1,1024]{1,0:T(2,128)(2,1)S(1)} %broadcast_in_dim.4.b_ref, bf16[1,1024]{1,0:T(2,128)(2,1)S(1)} %broadcast_in_dim.10.a_ref), custom_call_target="tpu_custom_call" | custom-call | flops 6442450944 | bytes 16777216 | tf_op jit(solution)/shard_map/force_left/pallas_call | solution.py:98
  16.1 1.5 %force_right.1 = (f32[16,4096]{1,0:T(8,128)S(1)}, f32[16,4096]{1,0:T(8,128)S(1)}) custom-call(bf16[32,1024]{1,0:T(8,128)(2,1)S(1)} %get-tuple-element.24.act_ref, bf16[1024,8192]{1,0:T(8,128)(2,1)S(1)} %copy-done.1), custom_call_target="tpu_custom_call" | custom-call | flops 2147483648 | bytes 8388608 | tf_op jit(solution)/shard_map/force_right/pallas_call | solution.py:110
  18.2 1.8 %collective-permute-start.3 = (bf16[8,4096]{1,0:T(8,128)(2,1)S(1)}, bf16[8,4096]{1,0:T(8,128)(2,1)S(1)}, u32[]{:S(2)}, u32[]{:S(2)}) collective-permute-start(bf16[8,4096]{1,0:T(8,128)(2,1)S(1)} %slice.152), channel_id=1, source_target_pairs={{0,16},{8,24},{16,0},{24,8},{1,17},{9,25},{17,1},{25,9},{2,18},{10... | collective-permute-start | bytes 196616 | tf_op jit(solution)/shard_map/ppermute | solution.py:18
  20.0 0.9 %collective-permute-start.5 = (bf16[8,4096]{1,0:T(8,128)(2,1)S(1)}, bf16[8,4096]{1,0:T(8,128)(2,1)S(1)}, u32[]{:S(2)}, u32[]{:S(2)}) collective-permute-start(bf16[8,4096]{1,0:T(8,128)(2,1)S(1)} %slice.151), channel_id=1, source_target_pairs={{0,16},{8,24},{16,0},{24,8},{1,17},{9,25},{17,1},{25,9},{2,18},{10... | collective-permute-start | bytes 196616 | tf_op jit(solution)/shard_map/ppermute | solution.py:18
  21.0 1.5 %collective-permute-done.3 = bf16[8,4096]{1,0:T(8,128)(2,1)S(1)} collective-permute-done((bf16[8,4096]{1,0:T(8,128)(2,1)S(1)}, bf16[8,4096]{1,0:T(8,128)(2,1)S(1)}, u32[]{:S(2)}, u32[]{:S(2)}) %collective-permute-start.3) | collective-permute-done | bytes 65568 | tf_op jit(solution)/shard_map/ppermute | solution.py:18
  22.5 1.8 %collective-permute-done.5 = bf16[8,4096]{1,0:T(8,128)(2,1)S(1)} collective-permute-done((bf16[8,4096]{1,0:T(8,128)(2,1)S(1)}, bf16[8,4096]{1,0:T(8,128)(2,1)S(1)}, u32[]{:S(2)}, u32[]{:S(2)}) %collective-permute-start.5) | collective-permute-done | bytes 65568 | tf_op jit(solution)/shard_map/ppermute | solution.py:18
  24.5 1.6 %collective-permute-start.6 = (bf16[8,2048]{1,0:T(8,128)(2,1)S(1)}, bf16[8,2048]{1,0:T(8,128)(2,1)S(1)}, u32[]{:S(2)}, u32[]{:S(2)}) collective-permute-start(bf16[8,2048]{1,0:T(8,128)(2,1)S(1)} %get-tuple-element.58), channel_id=1, source_target_pairs={{0,2},{1,3},{2,0},{3,1},{4,6},{5,7},{6,4},{7,5},{8,10},{9,11},{10,... | collective-permute-start | bytes 98312 | tf_op jit(solution)/shard_map/ppermute | solution.py:18
  26.1 2.6 %collective-permute-start.7 = (bf16[8,2048]{1,0:T(8,128)(2,1)S(1)}, bf16[8,2048]{1,0:T(8,128)(2,1)S(1)}, u32[]{:S(2)}, u32[]{:S(2)}) collective-permute-start(bf16[8,2048]{1,0:T(8,128)(2,1)S(1)} %get-tuple-element.57), channel_id=1, source_target_pairs={{0,4},{1,5},{2,6},{3,7},{4,0},{5,1},{6,2},{7,3},{8,12},{9,13},{10,... | collective-permute-start | bytes 98312 | tf_op jit(solution)/shard_map/ppermute | solution.py:18
  28.9 2.2 %collective-permute-done.7 = bf16[8,2048]{1,0:T(8,128)(2,1)S(1)} collective-permute-done((bf16[8,2048]{1,0:T(8,128)(2,1)S(1)}, bf16[8,2048]{1,0:T(8,128)(2,1)S(1)}, u32[]{:S(2)}, u32[]{:S(2)}) %collective-permute-start.7) | collective-permute-done | bytes 32800 | tf_op jit(solution)/shard_map/ppermute | solution.py:18
  31.2 3.2 %collective-permute-done.8 = bf16[8,2048]{1,0:T(8,128)(2,1)S(1)} collective-permute-done((bf16[8,2048]{1,0:T(8,128)(2,1)S(1)}, bf16[8,2048]{1,0:T(8,128)(2,1)S(1)}, u32[]{:S(2)}, u32[]{:S(2)}) %collective-permute-start.8) | collective-permute-done | bytes 32800 | tf_op jit(solution)/shard_map/ppermute | solution.py:18
  34.4 1.4 %collective-permute-start.10 = (bf16[32,1024]{1,0:T(8,128)(2,1)S(1)}, bf16[32,1024]{1,0:T(8,128)(2,1)S(1)}, u32[]{:S(2)}, u32[]{:S(2)}) collective-permute-start(bf16[32,1024]{1,0:T(8,128)(2,1)S(1)} %get-tuple-element.30), channel_id=1, source_target_pairs={{0,16},{8,24},{16,0},{24,8},{1,17},{9,25},{17,1},{25,9},{2,18},{10... | collective-permute-start | bytes 196616 | tf_op jit(solution)/shard_map/ppermute | solution.py:18
  35.8 1.7 %collective-permute-start.11 = (bf16[32,1024]{1,0:T(8,128)(2,1)S(1)}, bf16[32,1024]{1,0:T(8,128)(2,1)S(1)}, u32[]{:S(2)}, u32[]{:S(2)}) collective-permute-start(bf16[32,1024]{1,0:T(8,128)(2,1)S(1)} %get-tuple-element.31), channel_id=1, source_target_pairs={{0,17},{1,16},{2,19},{3,18},{4,21},{5,20},{6,23},{7,22},{8,25},{9,... | collective-permute-start | bytes 196616 | tf_op jit(solution)/shard_map/ppermute | solution.py:24
  38.0 2.2 %load_omega.1.w_ref = bf16[2048,1024]{1,0:T(8,128)(2,1)S(1)} custom-call(bf16[2048,1024]{1,0:T(8,128)(2,1)} %src_ref), custom_call_target="tpu_custom_call" | custom-call | bytes 8388608 | tf_op jit(solution)/shard_map/load_omega/pallas_call | solution.py:55
  40.2 0.7 %collective-permute-done.11 = bf16[32,1024]{1,0:T(8,128)(2,1)S(1)} collective-permute-done((bf16[32,1024]{1,0:T(8,128)(2,1)S(1)}, bf16[32,1024]{1,0:T(8,128)(2,1)S(1)}, u32[]{:S(2)}, u32[]{:S(2)}) %collective-permute-start.11) | collective-permute-done | bytes 65568 | tf_op jit(solution)/shard_map/ppermute | solution.py:24
  41.0 0.8 %collective-permute-done.9 = bf16[32,1024]{1,0:T(8,128)(2,1)S(1)} collective-permute-done((bf16[32,1024]{1,0:T(8,128)(2,1)S(1)}, bf16[32,1024]{1,0:T(8,128)(2,1)S(1)}, u32[]{:S(2)}, u32[]{:S(2)}) %collective-permute-start.9) | collective-permute-done | bytes 65568 | tf_op jit(solution)/shard_map/ppermute | solution.py:18
  41.8 1.3 %angle_parts.2 = (f32[64,2048]{1,0:T(8,128)S(1)}, bf16[64,2048]{1,0:T(8,128)(2,1)S(1)}) custom-call(bf16[128,1024]{1,0:T(8,128)(2,1)S(1)} %pad_maximum_fusion.2.t_ref, bf16[2048,1024]{1,0:T(8,128)(2,1)S(1)} %load_omega.1.w_ref), custom_call_target="tpu_custom_call" | custom-call | flops 536870912 | bytes 4194304 | tf_op jit(solution)/shard_map/angle_parts/pallas_call | solution.py:132
  43.1 0.8 %collective-permute-start.12 = (bf16[64,2048]{1,0:T(8,128)(2,1)S(1)}, bf16[64,2048]{1,0:T(8,128)(2,1)S(1)}, u32[]{:S(2)}, u32[]{:S(2)}) collective-permute-start(bf16[64,2048]{1,0:T(8,128)(2,1)S(1)} %get-tuple-element.37), channel_id=1, source_target_pairs={{0,1},{1,0},{2,3},{3,2},{4,5},{5,4},{6,7},{7,6},{8,9},{9,8},{10,11... | collective-permute-start | bytes 786440 | tf_op jit(solution)/shard_map/ppermute | solution.py:18
  44.5 0.8 %collective-permute-done.17 = bf16[128,512]{1,0:T(8,128)(2,1)S(1)} collective-permute-done((bf16[128,512]{1,0:T(8,128)(2,1)S(1)}, bf16[128,512]{1,0:T(8,128)(2,1)S(1)}, u32[]{:S(2)}, u32[]{:S(2)}) %collective-permute-start.17) | collective-permute-done | bytes 131104 | tf_op jit(solution)/shard_map/ppermute | solution.py:18
  45.6 1.3 %angle_parts.3 = (f32[64,2048]{1,0:T(8,128)S(1)}, bf16[64,2048]{1,0:T(8,128)(2,1)S(1)}) custom-call(bf16[128,1024]{1,0:T(8,128)(2,1)S(1)} %pad_maximum_fusion.3.t_ref, bf16[2048,1024]{1,0:T(8,128)(2,1)S(1)} %load_omega.1.w_ref), custom_call_target="tpu_custom_call" | custom-call | tf_op jit(solution)/shard_map/angle_parts/pallas_call | solution.py:132
  46.9 1.4 %collective-permute-start.19 = (bf16[64,2048]{1,0:T(8,128)(2,1)S(1)}, bf16[64,2048]{1,0:T(8,128)(2,1)S(1)}, u32[]{:S(2)}, u32[]{:S(2)}) collective-permute-start(bf16[64,2048]{1,0:T(8,128)(2,1)S(1)} %get-tuple-element.40), channel_id=1, source_target_pairs={{0,1},{1,0},{2,3},{3,2},{4,5},{5,4},{6,7},{7,6},{8,9},{9,8},{10,11... | collective-permute-start | bytes 786440 | tf_op jit(solution)/shard_map/ppermute | solution.py:18
  48.2 1.3 %collective-permute-done.12 = bf16[64,2048]{1,0:T(8,128)(2,1)S(1)} collective-permute-done((bf16[64,2048]{1,0:T(8,128)(2,1)S(1)}, bf16[64,2048]{1,0:T(8,128)(2,1)S(1)}, u32[]{:S(2)}, u32[]{:S(2)}) %collective-permute-start.12) | collective-permute-done | bytes 262176 | tf_op jit(solution)/shard_map/ppermute | solution.py:18
  50.0 4.0 %collective-permute-start.15 = (bf16[16,2048]{1,0:T(8,128)(2,1)S(1)}, bf16[16,2048]{1,0:T(8,128)(2,1)S(1)}, u32[]{:S(2)}, u32[]{:S(2)}) collective-permute-start(bf16[16,2048]{1,0:T(8,128)(2,1)S(1)} %get-tuple-element.46), channel_id=1, source_target_pairs={{0,2},{1,3},{2,0},{3,1},{4,6},{5,7},{6,4},{7,5},{8,10},{9,11},{10,... | collective-permute-start | bytes 196616 | tf_op jit(solution)/shard_map/ppermute | solution.py:18
  54.1 1.4 %collective-permute-done.19 = bf16[64,2048]{1,0:T(8,128)(2,1)S(1)} collective-permute-done((bf16[64,2048]{1,0:T(8,128)(2,1)S(1)}, bf16[64,2048]{1,0:T(8,128)(2,1)S(1)}, u32[]{:S(2)}, u32[]{:S(2)}) %collective-permute-start.19) | collective-permute-done | bytes 262176 | tf_op jit(solution)/shard_map/ppermute | solution.py:18
  56.1 3.9 %collective-permute-start.22 = (bf16[16,2048]{1,0:T(8,128)(2,1)S(1)}, bf16[16,2048]{1,0:T(8,128)(2,1)S(1)}, u32[]{:S(2)}, u32[]{:S(2)}) collective-permute-start(bf16[16,2048]{1,0:T(8,128)(2,1)S(1)} %get-tuple-element.49), channel_id=1, source_target_pairs={{0,2},{1,3},{2,0},{3,1},{4,6},{5,7},{6,4},{7,5},{8,10},{9,11},{10,... | collective-permute-start | bytes 196616 | tf_op jit(solution)/shard_map/ppermute | solution.py:18
  60.6 1.3 %collective-permute-start.16 = (f32[8,128]{1,0:T(8,128)S(1)}, f32[8,128]{1,0:T(8,128)S(1)}, u32[]{:S(2)}, u32[]{:S(2)}) collective-permute-start(f32[8,128]{1,0:T(8,128)S(1)} %slice.103), channel_id=1, source_target_pairs={{0,16},{8,24},{16,0},{24,8},{1,17},{9,25},{17,1},{25,9},{2,18},{10... | collective-permute-start | bytes 12296 | tf_op jit(solution)/shard_map/ppermute | solution.py:18
  63.7 1.4 %collective-permute-start.24 = (f32[8,128]{1,0:T(8,128)S(1)}, f32[8,128]{1,0:T(8,128)S(1)}, u32[]{:S(2)}, u32[]{:S(2)}) collective-permute-start(f32[8,128]{1,0:T(8,128)S(1)} %get-tuple-element.60), channel_id=1, source_target_pairs={{0,8},{8,0},{16,24},{24,16},{1,9},{9,1},{17,25},{25,17},{2,10},{10... | collective-permute-start | bytes 12296 | tf_op jit(solution)/shard_map/ppermute | solution.py:18
  65.0 0.7 %broadcast_add_fusion = f32[8,8192]{1,0:T(8,128)} fusion(f32[8,8192]{1,0:T(8,128)S(1)} %copy-done.3, f32[8192]{0:T(1024)S(1)} %copy-done.7), kind=kLoop, calls=%fused_computation.28 | loop fusion | flops 65536 | bytes 557056 | tf_op jit(solution)/shard_map/add | solution.py:179
  65.8 0.9 %collective-permute-done.23 = f32[8,128]{1,0:T(8,128)S(1)} collective-permute-done((f32[8,128]{1,0:T(8,128)S(1)}, f32[8,128]{1,0:T(8,128)S(1)}, u32[]{:S(2)}, u32[]{:S(2)}) %collective-permute-start.23) | collective-permute-done | bytes 4128 | tf_op jit(solution)/shard_map/ppermute | solution.py:18
  (72 shorter events, 6.6 us)
Async XLA Ops:
  0.6 59.4 %copy-start = (bf16[2048,128]{1,0:T(8,128)(2,1)S(1)}, bf16[2048,128]{1,0:T(8,128)(2,1)}, u32[]{:S(2)}) copy-start(bf16[2048,128]{1,0:T(8,128)(2,1)} %param.17) | copy-start | bytes 1572868
  0.6 9.3 %copy-start.1 = (bf16[1024,8192]{1,0:T(8,128)(2,1)S(1)}, bf16[1024,8192]{1,0:T(8,128)(2,1)}, u32[]{:S(2)}) copy-start(bf16[1024,8192]{1,0:T(8,128)(2,1)} %k_ref.3) | copy-start | bytes 50331652
  1.8 6.5 %collective-permute-start = (bf16[8,8192]{1,0:T(8,128)(2,1)S(1)}, bf16[8,8192]{1,0:T(8,128)(2,1)S(1)}, u32[]{:S(2)}, u32[]{:S(2)}) collective-permute-start(bf16[8,8192]{1,0:T(8,128)(2,1)S(1)} %rounded.1), channel_id=1, source_target_pairs={{0,16},{8,24},{16,0},{24,8},{1,17},{9,25},{17,1},{25,9},{2,18},{10... | collective-permute-start | bytes 393224 | tf_op jit(solution)/shard_map/ppermute | solution.py:18
  8.3 1.6 %collective-permute-start.1 = (bf16[16,8192]{1,0:T(8,128)(2,1)S(1)}, bf16[16,8192]{1,0:T(8,128)(2,1)S(1)}, u32[]{:S(2)}, u32[]{:S(2)}) collective-permute-start(bf16[16,8192]{1,0:T(8,128)(2,1)S(1)} %pad_maximum_fusion.1), channel_id=1, source_target_pairs={{0,8},{8,0},{16,24},{24,16},{1,9},{9,1},{17,25},{25,17},{2,10},{10... | collective-permute-start | bytes 786440 | tf_op jit(solution)/shard_map/ppermute | solution.py:18
  16.0 1.7 %collective-permute-start.2 = (f32[16,4096]{1,0:T(8,128)S(1)}, f32[16,4096]{1,0:T(8,128)S(1)}, u32[]{:S(2)}, u32[]{:S(2)}) collective-permute-start(f32[16,4096]{1,0:T(8,128)S(1)} %get-tuple-element.23), channel_id=1, source_target_pairs={{0,8},{8,0},{16,24},{24,16},{1,9},{9,1},{17,25},{25,17},{2,10},{10... | collective-permute-start | bytes 786440 | tf_op jit(solution)/shard_map/ppermute | solution.py:18
  16.1 8.3 %copy-start.5 = (f32[8,8192]{1,0:T(8,128)S(1)}, f32[8,8192]{1,0:T(8,128)}, u32[]{:S(2)}) copy-start(f32[8,8192]{1,0:T(8,128)} %param.9) | copy-start | bytes 786436
  17.7 2.3 %collective-permute-start.4 = (bf16[16,4096]{1,0:T(8,128)(2,1)S(1)}, bf16[16,4096]{1,0:T(8,128)(2,1)S(1)}, u32[]{:S(2)}, u32[]{:S(2)}) collective-permute-start(bf16[16,4096]{1,0:T(8,128)(2,1)S(1)} %convert_element_type.54), channel_id=1, source_target_pairs={{0,8},{8,0},{16,24},{24,16},{1,9},{9,1},{17,25},{25,17},{2,10},{10... | collective-permute-start | bytes 393224 | tf_op jit(solution)/shard_map/ppermute | solution.py:18
  18.2 4.3 %collective-permute-start.3 = (bf16[8,4096]{1,0:T(8,128)(2,1)S(1)}, bf16[8,4096]{1,0:T(8,128)(2,1)S(1)}, u32[]{:S(2)}, u32[]{:S(2)}) collective-permute-start(bf16[8,4096]{1,0:T(8,128)(2,1)S(1)} %slice.152), channel_id=1, source_target_pairs={{0,16},{8,24},{16,0},{24,8},{1,17},{9,25},{17,1},{25,9},{2,18},{10... | collective-permute-start | bytes 196616 | tf_op jit(solution)/shard_map/ppermute | solution.py:18
  20.0 4.3 %collective-permute-start.5 = (bf16[8,4096]{1,0:T(8,128)(2,1)S(1)}, bf16[8,4096]{1,0:T(8,128)(2,1)S(1)}, u32[]{:S(2)}, u32[]{:S(2)}) collective-permute-start(bf16[8,4096]{1,0:T(8,128)(2,1)S(1)} %slice.151), channel_id=1, source_target_pairs={{0,16},{8,24},{16,0},{24,8},{1,17},{9,25},{17,1},{25,9},{2,18},{10... | collective-permute-start | bytes 196616 | tf_op jit(solution)/shard_map/ppermute | solution.py:18
  24.4 15.8 %copy-start.4 = (bf16[8,8192]{1,0:T(8,128)(2,1)}, bf16[8,8192]{1,0:T(8,128)(2,1)S(1)}, u32[]{:S(2)}) copy-start(bf16[8,8192]{1,0:T(8,128)(2,1)S(1)} %fusion) | copy-start | bytes 393220
  24.5 4.5 %collective-permute-start.6 = (bf16[8,2048]{1,0:T(8,128)(2,1)S(1)}, bf16[8,2048]{1,0:T(8,128)(2,1)S(1)}, u32[]{:S(2)}, u32[]{:S(2)}) collective-permute-start(bf16[8,2048]{1,0:T(8,128)(2,1)S(1)} %get-tuple-element.58), channel_id=1, source_target_pairs={{0,2},{1,3},{2,0},{3,1},{4,6},{5,7},{6,4},{7,5},{8,10},{9,11},{10,... | collective-permute-start | bytes 98312 | tf_op jit(solution)/shard_map/ppermute | solution.py:18
  26.1 5.1 %collective-permute-start.7 = (bf16[8,2048]{1,0:T(8,128)(2,1)S(1)}, bf16[8,2048]{1,0:T(8,128)(2,1)S(1)}, u32[]{:S(2)}, u32[]{:S(2)}) collective-permute-start(bf16[8,2048]{1,0:T(8,128)(2,1)S(1)} %get-tuple-element.57), channel_id=1, source_target_pairs={{0,4},{1,5},{2,6},{3,7},{4,0},{5,1},{6,2},{7,3},{8,12},{9,13},{10,... | collective-permute-start | bytes 98312 | tf_op jit(solution)/shard_map/ppermute | solution.py:18
  28.7 5.7 %collective-permute-start.8 = (bf16[8,2048]{1,0:T(8,128)(2,1)S(1)}, bf16[8,2048]{1,0:T(8,128)(2,1)S(1)}, u32[]{:S(2)}, u32[]{:S(2)}) collective-permute-start(bf16[8,2048]{1,0:T(8,128)(2,1)S(1)} %get-tuple-element.56), channel_id=1, source_target_pairs={{0,6},{1,7},{2,4},{3,5},{4,2},{5,3},{6,0},{7,1},{8,14},{9,15},{10,... | collective-permute-start | bytes 98312 | tf_op jit(solution)/shard_map/ppermute | solution.py:18
  34.4 5.8 %collective-permute-start.10 = (bf16[32,1024]{1,0:T(8,128)(2,1)S(1)}, bf16[32,1024]{1,0:T(8,128)(2,1)S(1)}, u32[]{:S(2)}, u32[]{:S(2)}) collective-permute-start(bf16[32,1024]{1,0:T(8,128)(2,1)S(1)} %get-tuple-element.30), channel_id=1, source_target_pairs={{0,16},{8,24},{16,0},{24,8},{1,17},{9,25},{17,1},{25,9},{2,18},{10... | collective-permute-start | bytes 196616 | tf_op jit(solution)/shard_map/ppermute | solution.py:18
  35.8 5.2 %collective-permute-start.11 = (bf16[32,1024]{1,0:T(8,128)(2,1)S(1)}, bf16[32,1024]{1,0:T(8,128)(2,1)S(1)}, u32[]{:S(2)}, u32[]{:S(2)}) collective-permute-start(bf16[32,1024]{1,0:T(8,128)(2,1)S(1)} %get-tuple-element.31), channel_id=1, source_target_pairs={{0,17},{1,16},{2,19},{3,18},{4,21},{5,20},{6,23},{7,22},{8,25},{9,... | collective-permute-start | bytes 196616 | tf_op jit(solution)/shard_map/ppermute | solution.py:24
  37.5 4.3 %collective-permute-start.9 = (bf16[32,1024]{1,0:T(8,128)(2,1)S(1)}, bf16[32,1024]{1,0:T(8,128)(2,1)S(1)}, u32[]{:S(2)}, u32[]{:S(2)}) collective-permute-start(bf16[32,1024]{1,0:T(8,128)(2,1)S(1)} %get-tuple-element.31), channel_id=1, source_target_pairs={{0,1},{1,0},{2,3},{3,2},{4,5},{5,4},{6,7},{7,6},{8,9},{9,8},{10,11... | collective-permute-start | bytes 196616 | tf_op jit(solution)/shard_map/ppermute | solution.py:18
  43.1 6.4 %collective-permute-start.12 = (bf16[64,2048]{1,0:T(8,128)(2,1)S(1)}, bf16[64,2048]{1,0:T(8,128)(2,1)S(1)}, u32[]{:S(2)}, u32[]{:S(2)}) collective-permute-start(bf16[64,2048]{1,0:T(8,128)(2,1)S(1)} %get-tuple-element.37), channel_id=1, source_target_pairs={{0,1},{1,0},{2,3},{3,2},{4,5},{5,4},{6,7},{7,6},{8,9},{9,8},{10,11... | collective-permute-start | bytes 786440 | tf_op jit(solution)/shard_map/ppermute | solution.py:18
  43.9 1.4 %collective-permute-start.17 = (bf16[128,512]{1,0:T(8,128)(2,1)S(1)}, bf16[128,512]{1,0:T(8,128)(2,1)S(1)}, u32[]{:S(2)}, u32[]{:S(2)}) collective-permute-start(bf16[128,512]{1,0:T(8,128)(2,1)S(1)} %get-tuple-element.51), channel_id=1, source_target_pairs={{0,8},{8,0},{16,24},{24,16},{1,9},{9,1},{17,25},{25,17},{2,10},{10... | collective-permute-start | bytes 393224 | tf_op jit(solution)/shard_map/ppermute | solution.py:18
  44.0 1.5 %collective-permute-start.18 = (bf16[128,512]{1,0:T(8,128)(2,1)S(1)}, bf16[128,512]{1,0:T(8,128)(2,1)S(1)}, u32[]{:S(2)}, u32[]{:S(2)}) collective-permute-start(bf16[128,512]{1,0:T(8,128)(2,1)S(1)} %get-tuple-element.52), channel_id=1, source_target_pairs={{0,8},{8,0},{16,24},{24,16},{1,9},{9,1},{17,25},{25,17},{2,10},{10... | collective-permute-start | bytes 393224 | tf_op jit(solution)/shard_map/ppermute | solution.py:18
  45.5 14.5 %copy-start.6 = (f32[2048]{0:T(1024)S(1)}, f32[2048]{0:T(1024)}, u32[]{:S(2)}) copy-start(f32[2048]{0:T(1024)} %param.16) | copy-start | bytes 24580
  45.5 19.5 %copy-start.3 = (f32[8,8192]{1,0:T(8,128)S(1)}, f32[8,8192]{1,0:T(8,128)}, u32[]{:S(2)}) copy-start(f32[8,8192]{1,0:T(8,128)} %x_ref.1) | copy-start | bytes 786436
  45.5 19.5 %copy-start.7 = (f32[8192]{0:T(1024)S(1)}, f32[8192]{0:T(1024)}, u32[]{:S(2)}) copy-start(f32[8192]{0:T(1024)} %param.14) | copy-start | bytes 98308
  46.9 8.6 %collective-permute-start.19 = (bf16[64,2048]{1,0:T(8,128)(2,1)S(1)}, bf16[64,2048]{1,0:T(8,128)(2,1)S(1)}, u32[]{:S(2)}, u32[]{:S(2)}) collective-permute-start(bf16[64,2048]{1,0:T(8,128)(2,1)S(1)} %get-tuple-element.40), channel_id=1, source_target_pairs={{0,1},{1,0},{2,3},{3,2},{4,5},{5,4},{6,7},{7,6},{8,9},{9,8},{10,11... | collective-permute-start | bytes 786440 | tf_op jit(solution)/shard_map/ppermute | solution.py:18
  49.6 6.5 %collective-permute-start.13 = (bf16[16,2048]{1,0:T(8,128)(2,1)S(1)}, bf16[16,2048]{1,0:T(8,128)(2,1)S(1)}, u32[]{:S(2)}, u32[]{:S(2)}) collective-permute-start(bf16[16,2048]{1,0:T(8,128)(2,1)S(1)} %get-tuple-element.45), channel_id=1, source_target_pairs={{0,6},{1,7},{2,4},{3,5},{4,2},{5,3},{6,0},{7,1},{8,14},{9,15},{10,... | collective-permute-start | bytes 196616 | tf_op jit(solution)/shard_map/ppermute | solution.py:18
  50.0 10.0 %collective-permute-start.14 = (bf16[16,2048]{1,0:T(8,128)(2,1)S(1)}, bf16[16,2048]{1,0:T(8,128)(2,1)S(1)}, u32[]{:S(2)}, u32[]{:S(2)}) collective-permute-start(bf16[16,2048]{1,0:T(8,128)(2,1)S(1)} %get-tuple-element.47), channel_id=1, source_target_pairs={{0,4},{1,5},{2,6},{3,7},{4,0},{5,1},{6,2},{7,3},{8,12},{9,13},{10,... | collective-permute-start | bytes 196616 | tf_op jit(solution)/shard_map/ppermute | solution.py:18
  50.0 10.0 %collective-permute-start.15 = (bf16[16,2048]{1,0:T(8,128)(2,1)S(1)}, bf16[16,2048]{1,0:T(8,128)(2,1)S(1)}, u32[]{:S(2)}, u32[]{:S(2)}) collective-permute-start(bf16[16,2048]{1,0:T(8,128)(2,1)S(1)} %get-tuple-element.46), channel_id=1, source_target_pairs={{0,2},{1,3},{2,0},{3,1},{4,6},{5,7},{6,4},{7,5},{8,10},{9,11},{10,... | collective-permute-start | bytes 196616 | tf_op jit(solution)/shard_map/ppermute | solution.py:18
  55.6 6.8 %collective-permute-start.20 = (bf16[16,2048]{1,0:T(8,128)(2,1)S(1)}, bf16[16,2048]{1,0:T(8,128)(2,1)S(1)}, u32[]{:S(2)}, u32[]{:S(2)}) collective-permute-start(bf16[16,2048]{1,0:T(8,128)(2,1)S(1)} %get-tuple-element.48), channel_id=1, source_target_pairs={{0,6},{1,7},{2,4},{3,5},{4,2},{5,3},{6,0},{7,1},{8,14},{9,15},{10,... | collective-permute-start | bytes 196616 | tf_op jit(solution)/shard_map/ppermute | solution.py:18
  56.0 6.4 %collective-permute-start.21 = (bf16[16,2048]{1,0:T(8,128)(2,1)S(1)}, bf16[16,2048]{1,0:T(8,128)(2,1)S(1)}, u32[]{:S(2)}, u32[]{:S(2)}) collective-permute-start(bf16[16,2048]{1,0:T(8,128)(2,1)S(1)} %get-tuple-element.50), channel_id=1, source_target_pairs={{0,4},{1,5},{2,6},{3,7},{4,0},{5,1},{6,2},{7,3},{8,12},{9,13},{10,... | collective-permute-start | bytes 196616 | tf_op jit(solution)/shard_map/ppermute | solution.py:18
  56.1 6.9 %collective-permute-start.22 = (bf16[16,2048]{1,0:T(8,128)(2,1)S(1)}, bf16[16,2048]{1,0:T(8,128)(2,1)S(1)}, u32[]{:S(2)}, u32[]{:S(2)}) collective-permute-start(bf16[16,2048]{1,0:T(8,128)(2,1)S(1)} %get-tuple-element.49), channel_id=1, source_target_pairs={{0,2},{1,3},{2,0},{3,1},{4,6},{5,7},{6,4},{7,5},{8,10},{9,11},{10,... | collective-permute-start | bytes 196616 | tf_op jit(solution)/shard_map/ppermute | solution.py:18
  60.6 5.1 %collective-permute-start.16 = (f32[8,128]{1,0:T(8,128)S(1)}, f32[8,128]{1,0:T(8,128)S(1)}, u32[]{:S(2)}, u32[]{:S(2)}) collective-permute-start(f32[8,128]{1,0:T(8,128)S(1)} %slice.103), channel_id=1, source_target_pairs={{0,16},{8,24},{16,0},{24,8},{1,17},{9,25},{17,1},{25,9},{2,18},{10... | collective-permute-start | bytes 12296 | tf_op jit(solution)/shard_map/ppermute | solution.py:18
  63.6 3.0 %collective-permute-start.23 = (f32[8,128]{1,0:T(8,128)S(1)}, f32[8,128]{1,0:T(8,128)S(1)}, u32[]{:S(2)}, u32[]{:S(2)}) collective-permute-start(f32[8,128]{1,0:T(8,128)S(1)} %get-tuple-element.59), channel_id=1, source_target_pairs={{0,24},{8,16},{16,8},{24,0},{1,25},{9,17},{17,9},{25,1},{2,26},{10... | collective-permute-start | bytes 12296 | tf_op jit(solution)/shard_map/ppermute | solution.py:18
  63.7 3.0 %collective-permute-start.24 = (f32[8,128]{1,0:T(8,128)S(1)}, f32[8,128]{1,0:T(8,128)S(1)}, u32[]{:S(2)}, u32[]{:S(2)}) collective-permute-start(f32[8,128]{1,0:T(8,128)S(1)} %get-tuple-element.60), channel_id=1, source_target_pairs={{0,8},{8,0},{16,24},{24,16},{1,9},{9,1},{17,25},{25,17},{2,10},{10... | collective-permute-start | bytes 12296 | tf_op jit(solution)/shard_map/ppermute | solution.py:18
  (3 other events, 14.4 us)
